TPU v7x, 768 devices: a whole 4x8x12 slice. The times are simulated.
768 devices in a mesh: dp: 32 (over x, y), expert: 4 (over z_hi), tensor: 6 (over z_lo, core).
Axes of the slice: x: 4, y: 8, z: 12 (z_hi: 4, z_lo: 3; z = z_hi * 3 + z_lo), core: 2. Of those that a mesh axis runs over, the one named last changes fastest.
Arguments:
- grad_out: bfloat16 [6144, 7168], P(('dp', 'expert')), may hold values from -24 to 24
- gate_prob: bfloat16 [6144, 2], P(('dp', 'expert')), may hold values from 0.049804688 to 0.94921875
- expert_ids: int32 [6144, 2], P(('dp', 'expert')), may hold values from 0 to 3, as said below
- slot_positions: int32 [6144, 2], P(('dp', 'expert')), may hold values from 0 to 38, as said below
- expert_down: bfloat16 [4, 2496, 7168], P('expert', 'tensor'), may hold values from -0.03125 to 0.03125
- dense_down: bfloat16 [2496, 7168], P(('expert', 'tensor')), may hold values from -0.03125 to 0.03125
- expert_gate_pre: bfloat16 [4, 4992, 2496], P('expert', 'dp', 'tensor'), may hold values from -6 to 6
- expert_up_pre: bfloat16 [4, 4992, 2496], P('expert', 'dp', 'tensor'), may hold values from -6 to 6
- dense_gate_pre: bfloat16 [6144, 2496], P('dp', ('expert', 'tensor')), may hold values from -6 to 6
- dense_up_pre: bfloat16 [6144, 2496], P('dp', ('expert', 'tensor')), may hold values from -6 to 6
Outputs:
- expert_gate_grad: bfloat16 [4, 4992, 2496], P('expert', 'dp', 'tensor')
- expert_up_grad: bfloat16 [4, 4992, 2496], P('expert', 'dp', 'tensor')
- slot_prob_grad: float32 [4, 4992], P('expert', 'dp')
- expert_down_grad: bfloat16 [4, 7168, 2496], P('expert', 'dp', 'tensor')
- dense_gate_grad: bfloat16 [6144, 2496], P('dp', ('expert', 'tensor'))
- dense_up_grad: bfloat16 [6144, 2496], P('dp', ('expert', 'tensor'))
- dense_down_grad: bfloat16 [7168, 2496], P('dp', ('expert', 'tensor'))
Inputs may be any that keep to these rules, and one draw needn't show every extreme that they name: `expert_ids`: the two experts of a token differ. In each block of 48 tokens of one index of dp and expert, no expert is named more than 39 times, and one expert is named exactly 39 times; it is the same expert in all 4 blocks of one dp index. `slot_positions`: the rank of an assignment among the assignments of its block of 48 tokens to the same expert, counting tokens in order and a token's first expert before its second.
All inputs are finite; a program needn't handle non-finite values.
Results may differ from a plain program's by a relative error of at most 0.024.
Values may be sent and summed in bfloat16 or wider, within the bound.
No kernel may reach another device: no remote copies, remote signals or barrier semaphores. Data moves between devices by JAX's collectives and lax.ppermute only.
A program may use at most 64 MiB of HBM per device.

v0:
```python
import jax
import jax.numpy as jnp
from jax import lax
from jax.sharding import PartitionSpec as P


def silu_parts(gate_val):
    gate_sig = jax.nn.sigmoid(gate_val)
    activated = gate_val * gate_sig
    slope = gate_sig * (1.0 + gate_val * (1.0 - gate_sig))
    return (activated, slope)


def local(
    grad_out,
    gate_prob,
    expert_ids,
    slot_positions,
    expert_down,
    dense_down,
    expert_gate_pre,
    expert_up_pre,
    dense_gate_pre,
    dense_up_pre,
):
    n_expert = lax.axis_size("expert")
    n_replica = lax.axis_size("dp")
    width = grad_out.shape[1]
    capacity = expert_gate_pre.shape[1] // n_expert
    flat_ids = expert_ids.reshape(-1)
    flat_slots = slot_positions.reshape(-1)
    repeated = jnp.repeat(grad_out, 2, axis=0)
    send_rows = (
        jnp.zeros((n_expert, capacity, width), jnp.bfloat16).at[flat_ids, flat_slots].set(repeated)
    )
    send_prob = (
        jnp.zeros((n_expert, capacity), jnp.bfloat16)
        .at[flat_ids, flat_slots]
        .set(gate_prob.reshape(-1))
    )
    recv_rows, recv_prob = (
        lax.all_to_all(send_rows, "expert", split_axis=0, concat_axis=0, tiled=True),
        lax.all_to_all(send_prob, "expert", split_axis=0, concat_axis=0, tiled=True),
    )
    slot_rows = recv_rows.reshape(n_expert * capacity, width)
    slot_prob = recv_prob.reshape(-1).astype(jnp.float32)
    weight_local = expert_down[0]
    back_hidden = lax.dot_general(
        slot_rows, weight_local, (((1,), (1,)), ((), ())), preferred_element_type=jnp.float32
    )
    gate_val = expert_gate_pre[0].astype(jnp.float32)
    up_val = expert_up_pre[0].astype(jnp.float32)
    activated, slope = silu_parts(gate_val)
    hidden = activated * up_val
    partial_dots = jnp.sum(back_hidden * hidden, axis=1)
    slot_dots = lax.psum(partial_dots, "tensor")
    scaled = slot_prob[:, None] * back_hidden
    expert_gate_grad = (scaled * up_val * slope).astype(jnp.bfloat16)[None]
    expert_up_grad = (scaled * activated).astype(jnp.bfloat16)[None]
    weighted = (slot_prob[:, None] * hidden).astype(jnp.bfloat16)
    expert_summed = lax.psum_scatter(
        lax.dot_general(
            slot_rows, weighted, (((0,), (0,)), ((), ())), preferred_element_type=jnp.float32
        ).astype(jnp.bfloat16),
        "dp",
        scatter_dimension=0,
        tiled=True,
    ).astype(jnp.float32)
    expert_down_grad = (expert_summed / n_replica).astype(jnp.bfloat16)[None]
    shard_rows = lax.all_gather(grad_out, "expert", axis=0, tiled=True)
    back_dense = lax.dot_general(
        shard_rows, dense_down, (((1,), (1,)), ((), ())), preferred_element_type=jnp.float32
    )
    dense_gate = dense_gate_pre.astype(jnp.float32)
    dense_up = dense_up_pre.astype(jnp.float32)
    dense_act, dense_slope = silu_parts(dense_gate)
    gate_buffer = (back_dense * dense_up * dense_slope).astype(jnp.bfloat16)
    up_buffer = (back_dense * dense_act).astype(jnp.bfloat16)
    dense_hidden = (dense_act * dense_up).astype(jnp.bfloat16)
    weight_sum = lax.dot_general(
        shard_rows, dense_hidden, (((0,), (0,)), ((), ())), preferred_element_type=jnp.float32
    )
    dense_summed = lax.psum_scatter(
        weight_sum.astype(jnp.bfloat16), "dp", scatter_dimension=0, tiled=True
    ).astype(jnp.float32)
    dense_down_grad = (dense_summed / n_replica).astype(jnp.bfloat16)
    return (
        expert_gate_grad,
        expert_up_grad,
        slot_dots[None],
        expert_down_grad,
        gate_buffer,
        up_buffer,
        dense_down_grad,
    )


def solution(mesh):
    return jax.shard_map(
        local,
        mesh=mesh,
        in_specs=(
            P(("dp", "expert"), None),
            P(("dp", "expert"), None),
            P(("dp", "expert"), None),
            P(("dp", "expert"), None),
            P("expert", "tensor", None),
            P(("expert", "tensor"), None),
            P("expert", "dp", "tensor"),
            P("expert", "dp", "tensor"),
            P("dp", ("expert", "tensor")),
            P("dp", ("expert", "tensor")),
        ),
        out_specs=(
            P("expert", "dp", "tensor"),
            P("expert", "dp", "tensor"),
            P("expert", "dp"),
            P("expert", "dp", "tensor"),
            P("dp", ("expert", "tensor")),
            P("dp", ("expert", "tensor")),
            P("dp", ("expert", "tensor")),
        ),
        check_vma=False,
    )
```

profile of v0, /device:TPU:1, one launch (start us, length us, event | category | flops | bytes accessed | tf_op | source)
XLA Modules:
  0.0 659.8 jit_solution(8424807960178690715)
XLA Ops:
  7.2 0.0 copy-start
  7.2 0.0 all-gather.2.cloned.1.call-start
  7.2 0.7 all-gather.2.cloned.1.call-update
  7.9 0.8 copy.24
  8.7 0.1 reshape.108
  8.8 0.8 copy.25
  9.6 0.1 reshape.109
  9.7 0.8 copy.26
  10.5 0.1 reshape.118
  10.6 5.1 scatter_fusion
  15.7 0.6 copy.27
  16.3 15.0 %all-to-all-start = ((bf16[4,1,39]{2,1,0:T(2,128)(2,1)}), bf16[4,1,39]{2,1,0:T(2,128)(2,1)S(1)}, u32[]{:S(2)}, u32[]{:S(2)}) async-start(bf16[4,1,39]{2,1,0:T(2,128)(2,1)} %copy.27), calls=%async_computation | async-start | bytes 4096 | tf_op jit(solution)/shard_map/all_to_all | solution.py:43
  31.3 1.8 broadcast_in_dim.29
  33.1 1.4 reshape.124
  34.5 0.0 copy-start.2
  34.5 1.9 broadcast_in_dim.28
  36.5 0.0 copy-done.2
  36.5 33.1 %scatter_fusion.1 = bf16[4,39,7168]{2,0,1:T(4,128)(2,1)} fusion(bf16[4,39,7168]{2,0,1:T(4,128)(2,1)} %broadcast_in_dim.28, s32[96]{0:T(128)S(1)} %fusion.38, bf16[96,7168]{1,0:T(8,128)(2,1)S(1)} %copy-done.2), kind=kCustom, calls=%fused_computation.1 | custom fusion | bytes 4129536 | tf_op jit(solution)/shard_map/scatter | solution.py:34
  69.5 3.7 copy.28
  73.2 0.0 copy-start.5
  73.2 0.0 copy-start.6
  73.2 0.0 all-to-all-done
  73.2 9.0 %all-to-all-start.1 = ((bf16[4,39,7168]{2,1,0:T(8,128)(2,1)}), bf16[4,39,7168]{2,1,0:T(8,128)(2,1)}, u32[]{:S(2)}, u32[]{:S(2)}) async-start(bf16[4,39,7168]{2,1,0:T(8,128)(2,1)} %copy.28), calls=%async_computation.1 | async-start | bytes 4587520 | tf_op jit(solution)/shard_map/all_to_all | solution.py:42
  82.2 0.0 reduce-scatter.9.cloned.1.call-start
  82.2 11.9 %all-gather.2.cloned.1.call-done = bf16[192,7168]{1,0:T(8,128)(2,1)} async-done(((bf16[48,7168]{1,0:T(8,128)(2,1)}), bf16[192,7168]{1,0:T(8,128)(2,1)}) %all-gather.2.cloned.1.call-update) | async-done | bytes 2752528 | tf_op jit(solution)/shard_map/all_gather | solution.py:70
  94.1 0.0 copy-done.5
  94.1 0.0 copy-done.6
  94.1 2.4 fusion
  96.5 2.3 copy.31
  98.8 0.0 reduce-scatter.9.cloned.1.call-update
  98.8 0.2 reduce-scatter.7.cloned.1.call-start
  99.1 0.1 reshape.113
  99.2 0.0 copy-start.3
  99.2 0.0 copy-start.4
  99.2 76.1 %all-to-all-done.1 = bf16[4,39,7168]{2,1,0:T(8,128)(2,1)} async-done(((bf16[4,39,7168]{2,1,0:T(8,128)(2,1)}), bf16[4,39,7168]{2,1,0:T(8,128)(2,1)}, u32[]{:S(2)}, u32[]{:S(2)}) %all-to-all-start.1) | async-done | bytes 2236448 | tf_op jit(solution)/shard_map/all_to_all | solution.py:42
  175.3 3.8 reshape.112
  179.0 0.0 copy-done.3
  179.0 0.0 copy-done.4
  179.0 6.1 convolution_convert_fusion
  185.2 9.5 %copy.29 = bf16[7168,416]{1,0:T(8,128)(2,1)} copy(bf16[7168,416]{0,1:T(8,128)(2,1)} %convolution_convert_fusion) | data formatting | bytes 11927552
  194.7 0.0 reduce-scatter.7.cloned.1.call-update
  194.7 0.0 copy-done
  194.7 0.0 copy-start.1
  194.7 3.4 multiply_convert_fusion.3
  198.2 0.0 copy-done.1
  198.2 5.5 fusion.11
  203.6 20.1 %psum.7 = f32[1,156]{1,0:T(1,128)} all-reduce(f32[1,156]{1,0:T(1,128)S(1)} %bitcast.74), channel_id=1, replica_groups=mesh['dp'=32,'expert'=4,'tensor'=6] {'tensor'}, use_global_device_ids=true, to_apply=%region_3.0 | all-reduce | flops 156 | bytes 1248 | tf_op jit(solution)/shard_map/psum | solution.py:56
  223.7 183.6 %reduce-scatter.9.cloned.1.call-done = bf16[224,104]{1,0:T(8,128)(2,1)} async-done(((bf16[7168,104]{1,0:T(8,128)(2,1)}), bf16[224,104]{1,0:T(8,128)(2,1)}) %reduce-scatter.9.cloned.1.call-update) | async-done | bytes 46608
  407.3 0.9 copy.32
  408.2 0.6 multiply_convert_fusion.2
  408.9 242.6 %reduce-scatter.7.cloned.1.call-done = bf16[224,416]{1,0:T(8,128)(2,1)} async-done(((bf16[7168,416]{1,0:T(8,128)(2,1)}), bf16[224,416]{1,0:T(8,128)(2,1)}) %reduce-scatter.7.cloned.1.call-update) | async-done | bytes 186384
  651.4 1.1 copy.30
  652.5 0.7 fusion.22
  (3 shorter events, 0.0 us)
Async XLA Ops:
  7.2 187.5 %copy-start = (bf16[104,7168]{1,0:T(8,128)(2,1)S(1)}, bf16[104,7168]{1,0:T(8,128)(2,1)}, u32[]{:S(2)}) copy-start(bf16[104,7168]{1,0:T(8,128)(2,1)} %param.15) | copy-start | bytes 4472836
  7.2 86.9 %all-gather.2.cloned.1.call-start = ((), (), s32[]{:S(2)}) async-start(), calls=%async_computation.4 | async-start | bytes 3440640 | tf_op jit(solution)/shard_map/all_gather | solution.py:70
  16.3 56.9 %all-to-all-start = ((bf16[4,1,39]{2,1,0:T(2,128)(2,1)}), bf16[4,1,39]{2,1,0:T(2,128)(2,1)S(1)}, u32[]{:S(2)}, u32[]{:S(2)}) async-start(bf16[4,1,39]{2,1,0:T(2,128)(2,1)} %copy.27), calls=%async_computation | async-start | bytes 4096 | tf_op jit(solution)/shard_map/all_to_all | solution.py:43
  34.5 1.9 copy-start.2
  73.2 20.9 %copy-start.5 = (bf16[192,104]{1,0:T(8,128)(2,1)S(1)}, bf16[192,104]{1,0:T(8,128)(2,1)}, u32[]{:S(2)}) copy-start(bf16[192,104]{1,0:T(8,128)(2,1)} %param.19) | copy-start | bytes 119812
  73.2 20.9 %copy-start.6 = (bf16[192,104]{1,0:T(8,128)(2,1)S(1)}, bf16[192,104]{1,0:T(8,128)(2,1)}, u32[]{:S(2)}) copy-start(bf16[192,104]{1,0:T(8,128)(2,1)} %param.18) | copy-start | bytes 119812
  73.2 102.1 %all-to-all-start.1 = ((bf16[4,39,7168]{2,1,0:T(8,128)(2,1)}), bf16[4,39,7168]{2,1,0:T(8,128)(2,1)}, u32[]{:S(2)}, u32[]{:S(2)}) async-start(bf16[4,39,7168]{2,1,0:T(8,128)(2,1)} %copy.28), calls=%async_computation.1 | async-start | bytes 4587520 | tf_op jit(solution)/shard_map/all_to_all | solution.py:42
  82.2 325.1 %reduce-scatter.9.cloned.1.call-start = ((), (), s32[]{:S(2)}) async-start(), calls=%async_computation.6 | async-start | bytes 1892352
  98.8 552.6 %reduce-scatter.7.cloned.1.call-start = ((), (), s32[]{:S(2)}) async-start(), calls=%async_computation.5 | async-start | bytes 7569408
  99.2 79.9 %copy-start.3 = (bf16[1,156,416]{2,1,0:T(8,128)(2,1)S(1)}, bf16[1,156,416]{2,1,0:T(8,128)(2,1)}, u32[]{:S(2)}) copy-start(bf16[1,156,416]{2,1,0:T(8,128)(2,1)} %param.17) | copy-start | bytes 389380
  99.2 79.9 %copy-start.4 = (bf16[1,156,416]{2,1,0:T(8,128)(2,1)S(1)}, bf16[1,156,416]{2,1,0:T(8,128)(2,1)}, u32[]{:S(2)}) copy-start(bf16[1,156,416]{2,1,0:T(8,128)(2,1)} %param.16) | copy-start | bytes 389380
  194.7 3.4 copy-start.1
Sparse Core Ops, SparseCore 0:
  10.4 83.6 all-gather.1
  99.1 308.1 reduce-scatter.8
  413.3 238.0 reduce-scatter.6
where the time goes:
time: 664 us; the launch traced here: 660 us
  waiting for transfers between devices  515 us (78%)
  local copies, waits for them, and re-layouts  67.8 us (10%)
  starting transfers between devices  24.4 us (4%)
  blocking collectives  20.1 us (3%)
  matrix products  17.4 us (3%)
  between operations  13.8 us (2%)
    unnamed x5, waiting for transfers between devices  427 us
    all_to_all x1, waiting for transfers between devices, local(): lax.all_to_all(send_rows, 'expert', split_axis=0, concat_axis=0, tiled=True)  76.1 us
    scatter x2, local copies, waits for them, and re-layouts, local(): jnp.zeros((n_expert, capacity, width), jnp.bfloat16)  36.7 us
    psum x1, blocking collectives, local(): slot_dots = lax.psum(partial_dots, 'tensor')  20.1 us
    unnamed x21, local copies, waits for them, and re-layouts  16.1 us
    all_to_all x1, starting transfers between devices, local(): lax.all_to_all(send_prob, 'expert', split_axis=0, concat_axis=0, tiled=True)  15 us
  transfers between devices with their start and end apart: 5, of which 4 were waited for; matrix products, arithmetic and copies ran while one was open for 13% of the time, Pallas kernels for 0%

commit v1 on v0

v1 whole, which is shorter than its diff:
```python
import functools

import jax
import jax.numpy as jnp
from jax import lax
from jax.experimental import pallas as pl
from jax.experimental.pallas import tpu as pltpu
from jax.sharding import Mesh
from jax.sharding import PartitionSpec as P

X_CHIPS = 4
RUN = 3
CORES = 2
LANES = 128
SLOT_ROWS = 160
VMEM_BYTES = 56 * 1024 * 1024


def silu_parts(gate_val):
    gate_sig = jax.nn.sigmoid(gate_val)
    activated = gate_val * gate_sig
    slope = gate_sig * (1.0 + gate_val * (1.0 - gate_sig))
    return (activated, slope)


def whole(*shape):
    return pl.BlockSpec(shape, lambda *idx: (0,) * len(shape))


def params():
    return pltpu.CompilerParams(vmem_limit_bytes=VMEM_BYTES)


def hidden_kernel(gate_ref, up_ref, dgate_ref, dup_ref, out_ref):
    slots, width = gate_ref.shape[1:]
    tokens, dwidth = dgate_ref.shape
    quarter = tokens // 4
    out_ref[...] = jnp.zeros_like(out_ref)
    activated, _ = silu_parts(gate_ref[0].astype(jnp.float32))
    hidden = activated * up_ref[0].astype(jnp.float32)
    pad = jnp.zeros((SLOT_ROWS - slots, width), jnp.float32)
    out_ref[:SLOT_ROWS, :width] = jnp.concatenate([hidden, pad], axis=0).astype(jnp.bfloat16)
    dactivated, _ = silu_parts(dgate_ref[...].astype(jnp.float32))
    dhidden = (dactivated * dup_ref[...].astype(jnp.float32)).astype(jnp.bfloat16)
    for j in range(4):
        out_ref[SLOT_ROWS : SLOT_ROWS + quarter, j * LANES : j * LANES + dwidth] = dhidden[
            j * quarter : (j + 1) * quarter
        ]


def split_kernel(nx, ny, rows_ref, out_ref):
    width = rows_ref.shape[1] - LANES
    block = width // (nx * ny)
    for y in range(ny):
        for x in range(nx):
            at = (x * ny + y) * block
            out_ref[y, :, x * block : (x + 1) * block] = rows_ref[:, at : at + block]
        out_ref[y, :, nx * block :] = rows_ref[:, width:]


def routing(meta, expert):
    hit0 = meta[:, 0:1] == expert
    hit1 = meta[:, 1:2] == expert
    slot = jnp.where(hit0, meta[:, 2:3], jnp.where(hit1, meta[:, 3:4], -1.0)).astype(jnp.int32)
    prob = jnp.where(hit0, meta[:, 4:5], jnp.where(hit1, meta[:, 5:6], 0.0))
    token = meta[:, 6:7].astype(jnp.int32)
    return slot, prob, token


def one_hot(index, count, value=1.0):
    lane = lax.broadcasted_iota(jnp.int32, (index.shape[0], count), 1)
    return jnp.where(lane == index, value, 0.0).astype(jnp.bfloat16)


def dot(a, b, dims):
    return lax.dot_general(a, b, (dims, ((), ())), preferred_element_type=jnp.float32)


def weight_kernel(width, dwidth, expert_ref, *refs):
    pieces, hid_ref, out_ref, a_ref, b_ref = refs[:6], refs[6], refs[7], refs[8], refs[9]
    ny, rows, total = pieces[0].shape
    cols = total - LANES
    group = 6 * rows
    expert = expert_ref[0].astype(jnp.float32)
    quarter = hid_ref.shape[1] - SLOT_ROWS
    base = out_ref.shape[2] - LANES
    b_ref[...] = jnp.zeros_like(b_ref)
    for y in range(ny):
        top = y * group
        for i, piece in enumerate(pieces):
            a_ref[top + i * rows : top + (i + 1) * rows, :] = piece[y, :, :cols]
        meta = jnp.concatenate([piece[y, :, cols:] for piece in pieces], axis=0).astype(jnp.float32)
        slot, prob, token = routing(meta, expert)
        weighted = dot(one_hot(slot, SLOT_ROWS, prob), hid_ref[y, :SLOT_ROWS, :width], ((1,), (0,)))
        b_ref[top : top + group, :width] = weighted.astype(jnp.bfloat16)
        dense = jnp.concatenate(
            [hid_ref[y, SLOT_ROWS:, j * LANES : (j + 1) * LANES] for j in range(4)], axis=0
        )
        moved = dot(one_hot(token, 4 * quarter), dense, ((1,), (0,)))
        b_ref[top : top + group, base : base + LANES] = moved.astype(jnp.bfloat16)
    summed = dot(a_ref[...], b_ref[...], ((0,), (0,))).astype(jnp.bfloat16)
    block = out_ref.shape[1]
    for x in range(out_ref.shape[0]):
        out_ref[x] = summed[x * block : (x + 1) * block]


def sum_kernel(scale, in_ref, expert_ref, dense_ref):
    summed = in_ref[0].astype(jnp.float32)
    for x in range(1, in_ref.shape[0]):
        summed = summed + in_ref[x].astype(jnp.float32)
    summed = (summed * scale).astype(jnp.bfloat16)
    base = in_ref.shape[2] - LANES
    expert_ref[0] = summed[:, : expert_ref.shape[2]]
    dense_ref[...] = summed[:, base : base + dense_ref.shape[1]]


def place(onehot, values):
    high = values.astype(jnp.bfloat16)
    rest = values - high.astype(jnp.float32)
    middle = rest.astype(jnp.bfloat16)
    low = (rest - middle.astype(jnp.float32)).astype(jnp.bfloat16)
    dims = ((0,), (0,))
    return dot(onehot, high, dims) + dot(onehot, middle, dims) + dot(onehot, low, dims)


def back_kernel(expert_ref, *refs):
    datas, metas = refs[:6], refs[6:12]
    we_ref, wd_ref, gate_ref, up_ref, dgate_ref, dup_ref = refs[12:18]
    gate_out, up_out, dots_out, dgate_out, dup_out = refs[18:23]
    acc_e, acc_d = refs[23:25]
    step = pl.program_id(0)

    @pl.when(step == 0)
    def _():
        acc_e[...] = jnp.zeros_like(acc_e)
        acc_d[...] = jnp.zeros_like(acc_d)

    rows = jnp.concatenate([data[...] for data in datas], axis=0)
    acc_e[...] += dot(rows, we_ref[0], ((1,), (1,)))
    acc_d[...] += dot(rows, wd_ref[...], ((1,), (1,)))

    @pl.when(step == pl.num_programs(0) - 1)
    def _():
        meta = jnp.concatenate([m[...] for m in metas], axis=0).astype(jnp.float32)
        slot, prob, token = routing(meta, expert_ref[0].astype(jnp.float32))
        slots = gate_ref.shape[1]
        hot = one_hot(slot, slots)
        back = place(hot, acc_e[...])
        wide = jnp.broadcast_to(prob, (prob.shape[0], LANES)).astype(jnp.bfloat16)
        slot_prob = dot(hot, wide, ((0,), (0,)))[:, :1]
        up_val = up_ref[0].astype(jnp.float32)
        activated, slope = silu_parts(gate_ref[0].astype(jnp.float32))
        product = back * (activated * up_val)
        ones = jnp.ones((8, product.shape[1]), jnp.float32)
        dots_out[...] = lax.dot_general(
            ones,
            product,
            (((1,), (1,)), ((), ())),
            precision=lax.Precision.HIGHEST,
            preferred_element_type=jnp.float32,
        )
        scaled = slot_prob * back
        gate_out[0] = (scaled * up_val * slope).astype(jnp.bfloat16)
        up_out[0] = (scaled * activated).astype(jnp.bfloat16)
        dback = place(one_hot(token, dgate_ref.shape[0]), acc_d[...])
        dactivated, dslope = silu_parts(dgate_ref[...].astype(jnp.float32))
        dgate_out[...] = (dback * dup_ref[...].astype(jnp.float32) * dslope).astype(jnp.bfloat16)
        dup_out[...] = (dback * dactivated).astype(jnp.bfloat16)


def ring(count, step):
    return [(i, (i + step) % count) for i in range(count)]


def local(
    grad_out,
    gate_prob,
    expert_ids,
    slot_positions,
    expert_down,
    dense_down,
    expert_gate_pre,
    expert_up_pre,
    dense_gate_pre,
    dense_up_pre,
):
    nx, ny, ne = lax.axis_size("x"), lax.axis_size("y"), lax.axis_size("e")
    expert, part = lax.axis_index("e"), lax.axis_index(("l", "c"))
    tokens, width = grad_out.shape
    slots, hwidth = expert_gate_pre.shape[1:]
    dwidth = dense_gate_pre.shape[1]
    capacity = slots // ne
    eighth = tokens // (RUN * CORES)
    block = width // (nx * ny)
    bf16 = jnp.bfloat16
    expert_arr = expert.reshape(1).astype(jnp.int32)
    smem = pl.BlockSpec(memory_space=pltpu.SMEM)

    hidden = pl.pallas_call(
        hidden_kernel,
        out_shape=jax.ShapeDtypeStruct((SLOT_ROWS + ne * tokens // 4, 4 * LANES), bf16),
        compiler_params=params(),
    )(expert_gate_pre, expert_up_pre, dense_gate_pre, dense_up_pre)
    hiddens = lax.all_gather(hidden, "y", axis=0)

    token = expert * tokens + lax.broadcasted_iota(jnp.int32, (tokens, 1), 0)
    meta = jnp.concatenate(
        [
            expert_ids.astype(bf16),
            (slot_positions + expert * capacity).astype(bf16),
            gate_prob,
            token.astype(bf16),
        ],
        axis=1,
    )
    meta = jnp.pad(meta, ((0, 0), (0, LANES - meta.shape[1])))
    mine = jnp.concatenate(
        [
            lax.dynamic_slice(grad_out, (part * eighth, 0), (eighth, width)),
            lax.dynamic_slice(meta, (part * eighth, 0), (eighth, LANES)),
        ],
        axis=1,
    )
    rows = lax.all_gather(mine, "e", axis=0, tiled=True)

    chunks = pl.pallas_call(
        functools.partial(split_kernel, nx, ny),
        out_shape=jax.ShapeDtypeStruct((ny, ne * eighth, nx * block + LANES), bf16),
        compiler_params=params(),
    )(rows)
    chunks = lax.all_to_all(chunks, "y", split_axis=0, concat_axis=0, tiled=True)

    def spread(piece):
        along = [piece] + [lax.ppermute(piece, ("e", "l"), ring(ne * RUN, d)) for d in (1, -1)]
        other = [lax.ppermute(p, "c", ring(CORES, 1)) for p in along]
        return along + other

    row_pieces = spread(rows)
    chunk_pieces = spread(chunks)

    cols = hwidth + (-hwidth) % LANES + LANES
    ktotal = ny * 6 * ne * eighth
    partial_sums = pl.pallas_call(
        functools.partial(weight_kernel, hwidth, dwidth),
        out_shape=jax.ShapeDtypeStruct((nx, block, cols), bf16),
        in_specs=[smem] + [pl.BlockSpec(memory_space=pltpu.VMEM)] * 7,
        scratch_shapes=[
            pltpu.VMEM((ktotal, nx * block), bf16),
            pltpu.VMEM((ktotal, cols), bf16),
        ],
        compiler_params=params(),
    )(expert_arr, *chunk_pieces, hiddens)
    landed = lax.all_to_all(partial_sums, "x", split_axis=0, concat_axis=0, tiled=True)
    expert_down_grad, dense_down_grad = pl.pallas_call(
        functools.partial(sum_kernel, 1.0 / (nx * ny)),
        out_shape=(
            jax.ShapeDtypeStruct((1, block, hwidth), bf16),
            jax.ShapeDtypeStruct((block, dwidth), bf16),
        ),
        compiler_params=params(),
    )(landed)

    depth = 1024
    data_spec = pl.BlockSpec((ne * eighth, depth), lambda k: (0, k))
    meta_spec = pl.BlockSpec((ne * eighth, LANES), lambda k: (0, width // LANES))
    gate_grad, up_grad, dots, dense_gate_grad, dense_up_grad = pl.pallas_call(
        back_kernel,
        grid=(width // depth,),
        out_shape=(
            jax.ShapeDtypeStruct((1, slots, hwidth), bf16),
            jax.ShapeDtypeStruct((1, slots, hwidth), bf16),
            jax.ShapeDtypeStruct((8, slots), jnp.float32),
            jax.ShapeDtypeStruct((ne * tokens, dwidth), bf16),
            jax.ShapeDtypeStruct((ne * tokens, dwidth), bf16),
        ),
        in_specs=[smem]
        + [data_spec] * 6
        + [meta_spec] * 6
        + [
            pl.BlockSpec((1, hwidth, depth), lambda k: (0, 0, k)),
            pl.BlockSpec((dwidth, depth), lambda k: (0, k)),
            whole(1, slots, hwidth),
            whole(1, slots, hwidth),
            whole(ne * tokens, dwidth),
            whole(ne * tokens, dwidth),
        ],
        out_specs=(
            whole(1, slots, hwidth),
            whole(1, slots, hwidth),
            whole(8, slots),
            whole(ne * tokens, dwidth),
            whole(ne * tokens, dwidth),
        ),
        scratch_shapes=[
            pltpu.VMEM((ne * tokens, hwidth), jnp.float32),
            pltpu.VMEM((ne * tokens, dwidth), jnp.float32),
        ],
        compiler_params=params(),
    )(
        expert_arr,
        *row_pieces,
        *row_pieces,
        expert_down,
        dense_down,
        expert_gate_pre,
        expert_up_pre,
        dense_gate_pre,
        dense_up_pre,
    )
    slot_prob_grad = lax.psum(dots[:1], ("l", "c"))
    return (
        gate_grad,
        up_grad,
        slot_prob_grad,
        expert_down_grad,
        dense_gate_grad,
        dense_up_grad,
        dense_down_grad,
    )


def solution(mesh):
    n_dp, n_expert, n_tensor = (mesh.shape[a] for a in ("dp", "expert", "tensor"))
    fine = Mesh(
        mesh.devices.reshape(X_CHIPS, n_dp // X_CHIPS, n_expert, n_tensor // CORES, CORES),
        ("x", "y", "e", "l", "c"),
    )
    dp, tensor = ("x", "y"), ("l", "c")
    return jax.shard_map(
        local,
        mesh=fine,
        in_specs=(
            P((*dp, "e"), None),
            P((*dp, "e"), None),
            P((*dp, "e"), None),
            P((*dp, "e"), None),
            P("e", tensor, None),
            P(("e", *tensor), None),
            P("e", dp, tensor),
            P("e", dp, tensor),
            P(dp, ("e", *tensor)),
            P(dp, ("e", *tensor)),
        ),
        out_specs=(
            P("e", dp, tensor),
            P("e", dp, tensor),
            P("e", dp),
            P("e", dp, tensor),
            P(dp, ("e", *tensor)),
            P(dp, ("e", *tensor)),
            P(dp, ("e", *tensor)),
        ),
        check_vma=False,
    )
```

time: 664 us -> 156 us (0.23)
  waiting for transfers between devices: 515 us -> 4.61 us
  local copies, waits for them, and re-layouts: 67.8 us -> 7.52 us
  blocking collectives: 20.1 us -> 67.5 us
  Pallas kernels: 0 us -> 23.4 us
  matrix products: 17.4 us -> 0 us
  starting transfers between devices: 24.4 us -> 35.2 us
    unnamed x5 -> x1, waiting for transfers between devices: 427 us -> 0.02 us
    all_to_all x2 -> x1, waiting for transfers between devices: 76.1 us -> 0.01 us  [local(): lax.all_to_all(partial_sums, 'x', split_axis=0, concat_axis=0, tiled=True)]
    scatter x3 -> x0, local copies, waits for them, and re-layouts: 41.8 us -> none  [the longest x2 36.7 us: local(): jnp.zeros((n_expert, capacity, width), jnp.bfloat16)]
    ppermute x0 -> x10, starting transfers between devices: none -> 31.1 us  [the longest x6 19.7 us: spread(): other = [lax.ppermute(p, 'c', ring(CORES, 1)) for p in along]]
    all_to_all x0 -> x1, blocking collectives: none -> 28.7 us  [local(): lax.all_to_all(chunks, 'y', split_axis=0, concat_axis=0, tiled=True)]
    all_gather x0 -> x1, blocking collectives: none -> 27.9 us  [local(): rows = lax.all_gather(mine, 'e', axis=0, tiled=True)]
    pallas_call x0 -> x5, Pallas kernels: none -> 23.4 us  [the longest x1 9.97 us: local(): pl.pallas_call(back_kernel, grid=(width // depth,), out_shape=(jax.ShapeD...]
    all_to_all x2 -> x1, starting transfers between devices: 24.1 us -> 4.06 us  [local(): lax.all_to_all(partial_sums, 'x', split_axis=0, concat_axis=0, tiled=True)]
  transfers between devices with their start and end apart: 5 -> 12, of which waited for: 4 -> 2; matrix products, arithmetic and copies ran while one was open for 13% -> 2% of each run, Pallas kernels for 0% -> 13%
where the time goes in v1:
time: 156 us; the launch traced here: 155 us
  blocking collectives  67.5 us (43%)
  starting transfers between devices  35.2 us (23%)
  Pallas kernels  23.4 us (15%)
  between operations  14.3 us (9%)
  local copies, waits for them, and re-layouts  7.52 us (5%)
  waiting for transfers between devices  4.61 us (3%)
  other arithmetic  2.05 us (1%)
    all_to_all x1, blocking collectives, local(): lax.all_to_all(chunks, 'y', split_axis=0, concat_axis=0, tiled=True)  28.7 us
    all_gather x1, blocking collectives, local(): rows = lax.all_gather(mine, 'e', axis=0, tiled=True)  27.9 us
    ppermute x6, starting transfers between devices, spread(): other = [lax.ppermute(p, 'c', ring(CORES, 1)) for p in along]  19.7 us
    ppermute x4, starting transfers between devices, spread(): lax.ppermute(piece, ('e', 'l'), ring(ne * RUN, d))  11.4 us
    psum x1, blocking collectives, local(): slot_prob_grad = lax.psum(dots[:1], ('l', 'c'))  10.9 us
    pallas_call x1, Pallas kernels, local(): pl.pallas_call(back_kernel, grid=(width // depth,), out_shape=(jax.ShapeD...  9.97 us
    pallas_call x1, Pallas kernels, local(): pl.pallas_call(functools.partial(weight_kernel, hwidth, dwidth), out_shap...  7.37 us
    unnamed x28, local copies, waits for them, and re-layouts  6.68 us
  transfers between devices with their start and end apart: 12, of which 2 were waited for; matrix products, arithmetic and copies ran while one was open for 2% of the time, Pallas kernels for 13%

profile of v1, /device:TPU:1, one launch (start us, length us, event | category | flops | bytes accessed | tf_op | source)
XLA Modules:
  0.0 154.6 jit_solution(1091837148408296455)
XLA Ops:
  7.2 0.0 copy-start
  7.2 0.0 all-gather.3.cloned.1.call-start
  7.2 1.8 %shard_map.155 = bf16[208,512]{1,0:T(8,128)(2,1)} custom-call(bf16[1,156,416]{2,1,0:T(8,128)(2,1)} %gate_ref.1, bf16[1,156,416]{2,1,0:T(8,128)(2,1)} %up_ref.1, bf16[192,104]{1,0:T(8,128)(2,1)} %dgate_ref.1, bf16[192,104]{1,0:T(8,128)(2,1)} %dup_ref.1), custom_call_target="tpu_custom_call" | custom-call | tf_op jit(solution)/shard_map/pallas_call | solution.py:199
  9.1 0.0 all-gather.3.cloned.1.call-update
  9.1 0.7 convert_element_type.19
  9.8 0.7 add_convert_fusion
  10.5 0.7 pad_maximum_fusion.1
  11.2 0.1 copy.23
  11.3 0.0 copy-done
  11.3 27.9 %all_gather.9.refs_0_.refs_6_.rows_ref = bf16[32,7296]{1,0:T(8,128)(2,1)} all-gather(bf16[8,7296]{1,0:T(8,128)(2,1)S(1)} %pad_maximum_fusion), channel_id=1, replica_groups=mesh['x'=4,'y'=8,'e'=4,'l'=3,'c'=2] {'e'}, dimensions={0}, use_global_device_ids=true | all-gather | bytes 583680 | tf_op jit(solution)/shard_map/all_gather | solution.py:224
  39.2 0.0 copy-start.1
  39.2 2.1 %shard_map.154 = bf16[8,32,1024]{2,1,0:T(8,128)(2,1)} custom-call(bf16[32,7296]{1,0:T(8,128)(2,1)} %all_gather.9.refs_0_.refs_6_.rows_ref), custom_call_target="tpu_custom_call" | custom-call | tf_op jit(solution)/shard_map/pallas_call | solution.py:226
  41.4 28.7 %all_to_all.10.refs_0_ = bf16[8,32,1024]{2,1,0:T(8,128)(2,1)S(1)} all-to-all(bf16[8,32,1024]{2,1,0:T(8,128)(2,1)} %shard_map.154), channel_id=1, replica_groups=mesh['x'=4,'y'=8,'e'=4,'l'=3,'c'=2] {'y'}, dimensions={0} | all-to-all | bytes 1048576 | tf_op jit(solution)/shard_map/all_to_all | solution.py:231
  70.0 0.0 copy-start.3
  70.0 1.9 %collective-permute-start.6 = (bf16[8,32,1024]{2,1,0:T(8,128)(2,1)S(1)}, bf16[8,32,1024]{2,1,0:T(8,128)(2,1)S(1)}, u32[]{:S(2)}, u32[]{:S(2)}) collective-permute-start(bf16[8,32,1024]{2,1,0:T(8,128)(2,1)S(1)} %all_to_all.10.refs_0_), channel_id=1, source_target_pairs={{0,22},{2,0},{4,2},{6,4},{8,6},{10,8},{12,10},{14,12},{16,14},{18,... | collective-permute-start | bytes 1572872 | tf_op jit(solution)/shard_map/ppermute | solution.py:234
  71.9 4.2 %collective-permute-start.5 = (bf16[8,32,1024]{2,1,0:T(8,128)(2,1)S(1)}, bf16[8,32,1024]{2,1,0:T(8,128)(2,1)S(1)}, u32[]{:S(2)}, u32[]{:S(2)}) collective-permute-start(bf16[8,32,1024]{2,1,0:T(8,128)(2,1)S(1)} %all_to_all.10.refs_0_), channel_id=1, source_target_pairs={{0,2},{2,4},{4,6},{6,8},{8,10},{10,12},{12,14},{14,16},{16,18},{18... | collective-permute-start | bytes 1572872 | tf_op jit(solution)/shard_map/ppermute | solution.py:234
  76.2 5.5 %collective-permute-start.7 = (bf16[8,32,1024]{2,1,0:T(8,128)(2,1)S(1)}, bf16[8,32,1024]{2,1,0:T(8,128)(2,1)S(1)}, u32[]{:S(2)}, u32[]{:S(2)}) collective-permute-start(bf16[8,32,1024]{2,1,0:T(8,128)(2,1)S(1)} %all_to_all.10.refs_0_), channel_id=1, source_target_pairs={{0,1},{1,0},{2,3},{3,2},{4,5},{5,4},{6,7},{7,6},{8,9},{9,8},{10,11... | collective-permute-start | bytes 1572872 | tf_op jit(solution)/shard_map/ppermute | solution.py:235
  81.7 3.2 %collective-permute-done.6.refs_2_ = bf16[8,32,1024]{2,1,0:T(8,128)(2,1)S(1)} collective-permute-done((bf16[8,32,1024]{2,1,0:T(8,128)(2,1)S(1)}, bf16[8,32,1024]{2,1,0:T(8,128)(2,1)S(1)}, u32[]{:S(2)}, u32[]{:S(2)}) %collective-permute-start.6) | collective-permute-done | bytes 524320 | tf_op jit(solution)/shard_map/ppermute | solution.py:234
  84.9 0.0 copy-start.9
  84.9 4.1 %collective-permute-start.9 = (bf16[8,32,1024]{2,1,0:T(8,128)(2,1)S(1)}, bf16[8,32,1024]{2,1,0:T(8,128)(2,1)S(1)}, u32[]{:S(2)}, u32[]{:S(2)}) collective-permute-start(bf16[8,32,1024]{2,1,0:T(8,128)(2,1)S(1)} %collective-permute-done.6.refs_2_), channel_id=1, source_target_pairs={{0,1},{1,0},{2,3},{3,2},{4,5},{5,4},{6,7},{7,6},{8,9},{9,8},{10,11... | collective-permute-start | bytes 1572872 | tf_op jit(solution)/shard_map/ppermute | solution.py:235
  89.0 0.0 collective-permute-done.5.refs_1_
  89.0 0.0 copy-start.10
  89.0 3.0 %collective-permute-start.8 = (bf16[8,32,1024]{2,1,0:T(8,128)(2,1)S(1)}, bf16[8,32,1024]{2,1,0:T(8,128)(2,1)}, u32[]{:S(2)}, u32[]{:S(2)}) collective-permute-start(bf16[8,32,1024]{2,1,0:T(8,128)(2,1)S(1)} %collective-permute-done.5.refs_1_), channel_id=1, source_target_pairs={{0,1},{1,0},{2,3},{3,2},{4,5},{5,4},{6,7},{7,6},{8,9},{9,8},{10,11... | collective-permute-start | bytes 1572872 | tf_op jit(solution)/shard_map/ppermute | solution.py:235
  92.1 0.0 copy-done.1
  92.1 1.9 %collective-permute-start.1 = (bf16[32,7296]{1,0:T(8,128)(2,1)S(1)}, bf16[32,7296]{1,0:T(8,128)(2,1)S(1)}, u32[]{:S(2)}, u32[]{:S(2)}) collective-permute-start(bf16[32,7296]{1,0:T(8,128)(2,1)S(1)} %copy-done.1), channel_id=1, source_target_pairs={{0,22},{2,0},{4,2},{6,4},{8,6},{10,8},{12,10},{14,12},{16,14},{18,... | collective-permute-start | bytes 1400840 | tf_op jit(solution)/shard_map/ppermute | solution.py:234
  94.0 3.4 %collective-permute-start = (bf16[32,7296]{1,0:T(8,128)(2,1)S(1)}, bf16[32,7296]{1,0:T(8,128)(2,1)S(1)}, u32[]{:S(2)}, u32[]{:S(2)}) collective-permute-start(bf16[32,7296]{1,0:T(8,128)(2,1)S(1)} %copy-done.1), channel_id=1, source_target_pairs={{0,2},{2,4},{4,6},{6,8},{8,10},{10,12},{12,14},{14,16},{16,18},{18... | collective-permute-start | bytes 1400840 | tf_op jit(solution)/shard_map/ppermute | solution.py:234
  97.4 0.0 collective-permute-done.7.refs_3_
  97.4 0.0 copy-start.11
  97.4 0.0 collective-permute-done.9.refs_5_
  97.4 0.0 copy-done.10
  97.4 0.8 copy-done.11
  98.2 0.0 copy-start.12
  98.2 0.8 copy-done.12
  98.9 0.0 collective-permute-done.8.refs_4_
  99.0 0.0 copy-done.3
  99.0 0.0 copy-done.9
  99.0 7.4 %shard_map.156 = bf16[4,224,640]{2,1,0:T(8,128)(2,1)} custom-call(s32[1]{0:T(128)} %bitcast.expert_ref, bf16[8,32,1024]{2,1,0:T(8,128)(2,1)} %copy-done.3, bf16[8,32,1024]{2,1,0:T(8,128)(2,1)} %copy-done.10, bf16[8,32,1024]{2,1,0:T(8,128)(2,1)} %copy-done.9, bf16[8,32,1024]{2,1,0:T(8,128)(2,1)} %copy-done.11, ...), custom_call_target="tpu_custom_call" | custom-call | tf_op jit(solution)/shard_map/pallas_call | solution.py:243
  106.3 4.1 %all-to-all-start.1 = ((bf16[4,224,640]{2,1,0:T(8,128)(2,1)}), bf16[4,224,640]{2,1,0:T(8,128)(2,1)S(1)}, u32[]{:S(2)}, u32[]{:S(2)}) async-start(bf16[4,224,640]{2,1,0:T(8,128)(2,1)} %shard_map.156), calls=%async_computation.1 | async-start | bytes 2293760 | tf_op jit(solution)/shard_map/all_to_all | solution.py:253
  110.4 2.7 %collective-permute-start.2 = (bf16[32,7296]{1,0:T(8,128)(2,1)S(1)}, bf16[32,7296]{1,0:T(8,128)(2,1)S(1)}, u32[]{:S(2)}, u32[]{:S(2)}) collective-permute-start(bf16[32,7296]{1,0:T(8,128)(2,1)S(1)} %copy-done.1), channel_id=1, source_target_pairs={{0,1},{1,0},{2,3},{3,2},{4,5},{5,4},{6,7},{7,6},{8,9},{9,8},{10,11... | collective-permute-start | bytes 1400840 | tf_op jit(solution)/shard_map/ppermute | solution.py:235
  113.1 0.0 collective-permute-done.1.refs_2_.refs_8_
  113.1 0.0 copy-start.4
  113.2 1.9 %collective-permute-start.4 = (bf16[32,7296]{1,0:T(8,128)(2,1)S(1)}, bf16[32,7296]{1,0:T(8,128)(2,1)S(1)}, u32[]{:S(2)}, u32[]{:S(2)}) collective-permute-start(bf16[32,7296]{1,0:T(8,128)(2,1)S(1)} %collective-permute-done.1.refs_2_.refs_8_), channel_id=1, source_target_pairs={{0,1},{1,0},{2,3},{3,2},{4,5},{5,4},{6,7},{7,6},{8,9},{9,8},{10,11... | collective-permute-start | bytes 1400840 | tf_op jit(solution)/shard_map/ppermute | solution.py:235
  115.1 0.0 collective-permute-done.refs_1_.refs_7_
  115.1 0.0 copy-start.5
  115.1 2.4 %collective-permute-start.3 = (bf16[32,7296]{1,0:T(8,128)(2,1)S(1)}, bf16[32,7296]{1,0:T(8,128)(2,1)S(1)}, u32[]{:S(2)}, u32[]{:S(2)}) collective-permute-start(bf16[32,7296]{1,0:T(8,128)(2,1)S(1)} %collective-permute-done.refs_1_.refs_7_), channel_id=1, source_target_pairs={{0,1},{1,0},{2,3},{3,2},{4,5},{5,4},{6,7},{7,6},{8,9},{9,8},{10,11... | collective-permute-start | bytes 1400840 | tf_op jit(solution)/shard_map/ppermute | solution.py:235
  117.5 0.0 collective-permute-done.2.refs_3_.refs_9_
  117.5 0.0 copy-start.6
  117.5 0.0 collective-permute-done.4.refs_5_.refs_11_
  117.5 0.0 copy-start.7
  117.6 1.4 collective-permute-done.3.refs_4_.refs_10_
  119.0 0.0 copy-done.4
  119.0 0.0 copy-done.5
  119.0 0.0 copy-done.6
  119.0 0.0 copy-done.7
  119.0 0.0 copy-start.8
  119.0 0.8 copy-done.8
  119.7 10.0 %shard_map.153 = (bf16[1,156,416]{2,1,0:T(8,128)(2,1)}, bf16[1,156,416]{2,1,0:T(8,128)(2,1)}, f32[8,156]{1,0:T(8,128)}, bf16[192,104]{1,0:T(8,128)(2,1)}, bf16[192,104]{1,0:T(8,128)(2,1)}) custom-call(s32[1]{0:T(128)} %bitcast.expert_ref, bf16[32,7296]{1,0:T(8,128)(2,1)} %all_gather.9.refs_0_.refs_6_.rows_ref, bf16[32,7296]{1,0:T(8,128)(2,1)} %copy-done.5, ...), custom_call_target="tpu_custom_call" | custom-call | tf_op jit(solution)/shard_map/pallas_call | solution.py:266
  129.7 0.7 slice.3
  130.4 10.9 %psum.7 = f32[1,156]{1,0:T(1,128)} all-reduce(f32[1,156]{1,0:T(1,128)S(1)} %slice.3), channel_id=1, replica_groups=mesh['x'=4,'y'=8,'e'=4,'l'=3,'c'=2] {'l','c'}, use_global_device_ids=true, to_apply=%region_0.1 | all-reduce | flops 156 | bytes 1248 | tf_op jit(solution)/shard_map/psum | solution.py:310
  141.3 0.0 all-to-all-done.1.in_ref
  141.3 1.0 copy-done.2
  142.4 2.1 %shard_map.157 = (bf16[1,224,416]{2,1,0:T(8,128)(2,1)}, bf16[224,104]{1,0:T(8,128)(2,1)}) custom-call(bf16[4,224,640]{2,1,0:T(8,128)(2,1)} %copy-done.2), custom_call_target="tpu_custom_call" | custom-call | tf_op jit(solution)/shard_map/pallas_call | solution.py:254
  144.5 1.8 %copy.24 = bf16[1,224,416]{1,2,0:T(8,128)(2,1)} copy(bf16[1,224,416]{2,1,0:T(8,128)(2,1)} %get-tuple-element.31) | data formatting | bytes 372736
  146.2 1.5 copy.25
  (6 shorter events, 0.0 us)
Async XLA Ops:
  7.2 4.1 %copy-start = (bf16[48,7168]{1,0:T(8,128)(2,1)S(1)}, bf16[48,7168]{1,0:T(8,128)(2,1)}, u32[]{:S(2)}) copy-start(bf16[48,7168]{1,0:T(8,128)(2,1)} %param.10) | copy-start | bytes 2064388
  7.2 91.8 %all-gather.3.cloned.1.call-start = ((), (), s32[]{:S(2)}) async-start(), calls=%async_computation.2 | async-start | bytes 1916928 | tf_op jit(solution)/shard_map/all_gather | solution.py:204
  39.2 52.8 %copy-start.1 = (bf16[32,7296]{1,0:T(8,128)(2,1)S(1)}, bf16[32,7296]{1,0:T(8,128)(2,1)}, u32[]{:S(2)}) copy-start(bf16[32,7296]{1,0:T(8,128)(2,1)} %all_gather.9.refs_0_.refs_6_.rows_ref) | copy-start | bytes 1400836
  70.0 28.9 %copy-start.3 = (bf16[8,32,1024]{2,1,0:T(8,128)(2,1)}, bf16[8,32,1024]{2,1,0:T(8,128)(2,1)S(1)}, u32[]{:S(2)}) copy-start(bf16[8,32,1024]{2,1,0:T(8,128)(2,1)S(1)} %all_to_all.10.refs_0_) | copy-start | bytes 1572868
  70.0 14.9 %collective-permute-start.6 = (bf16[8,32,1024]{2,1,0:T(8,128)(2,1)S(1)}, bf16[8,32,1024]{2,1,0:T(8,128)(2,1)S(1)}, u32[]{:S(2)}, u32[]{:S(2)}) collective-permute-start(bf16[8,32,1024]{2,1,0:T(8,128)(2,1)S(1)} %all_to_all.10.refs_0_), channel_id=1, source_target_pairs={{0,22},{2,0},{4,2},{6,4},{8,6},{10,8},{12,10},{14,12},{16,14},{18,... | collective-permute-start | bytes 1572872 | tf_op jit(solution)/shard_map/ppermute | solution.py:234
  71.9 17.1 %collective-permute-start.5 = (bf16[8,32,1024]{2,1,0:T(8,128)(2,1)S(1)}, bf16[8,32,1024]{2,1,0:T(8,128)(2,1)S(1)}, u32[]{:S(2)}, u32[]{:S(2)}) collective-permute-start(bf16[8,32,1024]{2,1,0:T(8,128)(2,1)S(1)} %all_to_all.10.refs_0_), channel_id=1, source_target_pairs={{0,2},{2,4},{4,6},{6,8},{8,10},{10,12},{12,14},{14,16},{16,18},{18... | collective-permute-start | bytes 1572872 | tf_op jit(solution)/shard_map/ppermute | solution.py:234
  76.2 21.2 %collective-permute-start.7 = (bf16[8,32,1024]{2,1,0:T(8,128)(2,1)S(1)}, bf16[8,32,1024]{2,1,0:T(8,128)(2,1)S(1)}, u32[]{:S(2)}, u32[]{:S(2)}) collective-permute-start(bf16[8,32,1024]{2,1,0:T(8,128)(2,1)S(1)} %all_to_all.10.refs_0_), channel_id=1, source_target_pairs={{0,1},{1,0},{2,3},{3,2},{4,5},{5,4},{6,7},{7,6},{8,9},{9,8},{10,11... | collective-permute-start | bytes 1572872 | tf_op jit(solution)/shard_map/ppermute | solution.py:235
  84.9 14.1 %copy-start.9 = (bf16[8,32,1024]{2,1,0:T(8,128)(2,1)}, bf16[8,32,1024]{2,1,0:T(8,128)(2,1)S(1)}, u32[]{:S(2)}) copy-start(bf16[8,32,1024]{2,1,0:T(8,128)(2,1)S(1)} %collective-permute-done.6.refs_2_) | copy-start | bytes 1572868
  84.9 12.5 %collective-permute-start.9 = (bf16[8,32,1024]{2,1,0:T(8,128)(2,1)S(1)}, bf16[8,32,1024]{2,1,0:T(8,128)(2,1)S(1)}, u32[]{:S(2)}, u32[]{:S(2)}) collective-permute-start(bf16[8,32,1024]{2,1,0:T(8,128)(2,1)S(1)} %collective-permute-done.6.refs_2_), channel_id=1, source_target_pairs={{0,1},{1,0},{2,3},{3,2},{4,5},{5,4},{6,7},{7,6},{8,9},{9,8},{10,11... | collective-permute-start | bytes 1572872 | tf_op jit(solution)/shard_map/ppermute | solution.py:235
  89.0 8.4 %copy-start.10 = (bf16[8,32,1024]{2,1,0:T(8,128)(2,1)}, bf16[8,32,1024]{2,1,0:T(8,128)(2,1)S(1)}, u32[]{:S(2)}) copy-start(bf16[8,32,1024]{2,1,0:T(8,128)(2,1)S(1)} %collective-permute-done.5.refs_1_) | copy-start | bytes 1572868
  89.0 9.9 %collective-permute-start.8 = (bf16[8,32,1024]{2,1,0:T(8,128)(2,1)S(1)}, bf16[8,32,1024]{2,1,0:T(8,128)(2,1)}, u32[]{:S(2)}, u32[]{:S(2)}) collective-permute-start(bf16[8,32,1024]{2,1,0:T(8,128)(2,1)S(1)} %collective-permute-done.5.refs_1_), channel_id=1, source_target_pairs={{0,1},{1,0},{2,3},{3,2},{4,5},{5,4},{6,7},{7,6},{8,9},{9,8},{10,11... | collective-permute-start | bytes 1572872 | tf_op jit(solution)/shard_map/ppermute | solution.py:235
  92.1 21.1 %collective-permute-start.1 = (bf16[32,7296]{1,0:T(8,128)(2,1)S(1)}, bf16[32,7296]{1,0:T(8,128)(2,1)S(1)}, u32[]{:S(2)}, u32[]{:S(2)}) collective-permute-start(bf16[32,7296]{1,0:T(8,128)(2,1)S(1)} %copy-done.1), channel_id=1, source_target_pairs={{0,22},{2,0},{4,2},{6,4},{8,6},{10,8},{12,10},{14,12},{16,14},{18,... | collective-permute-start | bytes 1400840 | tf_op jit(solution)/shard_map/ppermute | solution.py:234
  94.0 21.1 %collective-permute-start = (bf16[32,7296]{1,0:T(8,128)(2,1)S(1)}, bf16[32,7296]{1,0:T(8,128)(2,1)S(1)}, u32[]{:S(2)}, u32[]{:S(2)}) collective-permute-start(bf16[32,7296]{1,0:T(8,128)(2,1)S(1)} %copy-done.1), channel_id=1, source_target_pairs={{0,2},{2,4},{4,6},{6,8},{8,10},{10,12},{12,14},{14,16},{16,18},{18... | collective-permute-start | bytes 1400840 | tf_op jit(solution)/shard_map/ppermute | solution.py:234
  97.4 0.8 copy-start.11
  98.2 0.8 copy-start.12
  106.3 35.0 %all-to-all-start.1 = ((bf16[4,224,640]{2,1,0:T(8,128)(2,1)}), bf16[4,224,640]{2,1,0:T(8,128)(2,1)S(1)}, u32[]{:S(2)}, u32[]{:S(2)}) async-start(bf16[4,224,640]{2,1,0:T(8,128)(2,1)} %shard_map.156), calls=%async_computation.1 | async-start | bytes 2293760 | tf_op jit(solution)/shard_map/all_to_all | solution.py:253
  110.4 7.1 %collective-permute-start.2 = (bf16[32,7296]{1,0:T(8,128)(2,1)S(1)}, bf16[32,7296]{1,0:T(8,128)(2,1)S(1)}, u32[]{:S(2)}, u32[]{:S(2)}) collective-permute-start(bf16[32,7296]{1,0:T(8,128)(2,1)S(1)} %copy-done.1), channel_id=1, source_target_pairs={{0,1},{1,0},{2,3},{3,2},{4,5},{5,4},{6,7},{7,6},{8,9},{9,8},{10,11... | collective-permute-start | bytes 1400840 | tf_op jit(solution)/shard_map/ppermute | solution.py:235
  113.1 5.8 %copy-start.4 = (bf16[32,7296]{1,0:T(8,128)(2,1)}, bf16[32,7296]{1,0:T(8,128)(2,1)S(1)}, u32[]{:S(2)}) copy-start(bf16[32,7296]{1,0:T(8,128)(2,1)S(1)} %collective-permute-done.1.refs_2_.refs_8_) | copy-start | bytes 1400836
  113.2 4.4 %collective-permute-start.4 = (bf16[32,7296]{1,0:T(8,128)(2,1)S(1)}, bf16[32,7296]{1,0:T(8,128)(2,1)S(1)}, u32[]{:S(2)}, u32[]{:S(2)}) collective-permute-start(bf16[32,7296]{1,0:T(8,128)(2,1)S(1)} %collective-permute-done.1.refs_2_.refs_8_), channel_id=1, source_target_pairs={{0,1},{1,0},{2,3},{3,2},{4,5},{5,4},{6,7},{7,6},{8,9},{9,8},{10,11... | collective-permute-start | bytes 1400840 | tf_op jit(solution)/shard_map/ppermute | solution.py:235
  115.1 3.9 %copy-start.5 = (bf16[32,7296]{1,0:T(8,128)(2,1)}, bf16[32,7296]{1,0:T(8,128)(2,1)S(1)}, u32[]{:S(2)}) copy-start(bf16[32,7296]{1,0:T(8,128)(2,1)S(1)} %collective-permute-done.refs_1_.refs_7_) | copy-start | bytes 1400836
  115.1 3.8 %collective-permute-start.3 = (bf16[32,7296]{1,0:T(8,128)(2,1)S(1)}, bf16[32,7296]{1,0:T(8,128)(2,1)S(1)}, u32[]{:S(2)}, u32[]{:S(2)}) collective-permute-start(bf16[32,7296]{1,0:T(8,128)(2,1)S(1)} %collective-permute-done.refs_1_.refs_7_), channel_id=1, source_target_pairs={{0,1},{1,0},{2,3},{3,2},{4,5},{5,4},{6,7},{7,6},{8,9},{9,8},{10,11... | collective-permute-start | bytes 1400840 | tf_op jit(solution)/shard_map/ppermute | solution.py:235
  117.5 1.4 copy-start.6
  117.5 1.4 copy-start.7
  119.0 0.8 copy-start.8
  141.3 1.0 copy-start.2
Sparse Core Ops, SparseCore 0:
  11.0 57.2 all-gather.2

commit v2 on v1

--- a/solution.py
+++ b/solution.py
@@ -48,14 +48,39 @@
         ]
 
 
+def pick_kernel(capacity, at_ref, rows_ref, prob_ref, ids_ref, slots_ref, out_ref):
+    expert, part = at_ref[0], at_ref[1]
+    eighth = out_ref.shape[0]
+    tokens, width = rows_ref.shape
+    lane = lax.broadcasted_iota(jnp.int32, (eighth, tokens), 1)
+    row = lax.broadcasted_iota(jnp.int32, (eighth, tokens), 0)
+    chosen = jnp.where(lane == row + part * eighth, 1.0, 0.0).astype(jnp.bfloat16)
+    out_ref[:, :width] = dot(chosen, rows_ref[...], ((1,), (0,))).astype(jnp.bfloat16)
+    token = expert * tokens + lax.broadcasted_iota(jnp.int32, (2, tokens), 1)
+    meta = jnp.concatenate(
+        [
+            ids_ref[...].astype(jnp.float32),
+            (slots_ref[...] + expert * capacity).astype(jnp.float32),
+            prob_ref[...].astype(jnp.float32),
+            token.astype(jnp.float32),
+        ],
+        axis=0,
+    ).astype(jnp.bfloat16)
+    meta = jnp.concatenate([meta, jnp.zeros((LANES - 8, tokens), jnp.bfloat16)], axis=0)
+    out_ref[:, width:] = dot(chosen, meta, ((1,), (1,))).astype(jnp.bfloat16)
+
+
 def split_kernel(nx, ny, rows_ref, out_ref):
     width = rows_ref.shape[1] - LANES
     block = width // (nx * ny)
+    stride = out_ref.shape[2] // nx
     for y in range(ny):
         for x in range(nx):
             at = (x * ny + y) * block
-            out_ref[y, :, x * block : (x + 1) * block] = rows_ref[:, at : at + block]
-        out_ref[y, :, nx * block :] = rows_ref[:, width:]
+            out_ref[y, :, x * stride : x * stride + block] = rows_ref[:, at : at + block]
+            out_ref[y, :, x * stride + block : (x + 1) * stride] = rows_ref[
+                :, width : width + stride - block
+            ]
 
 
 def routing(meta, expert):
@@ -76,32 +101,33 @@
     return lax.dot_general(a, b, (dims, ((), ())), preferred_element_type=jnp.float32)
 
 
-def weight_kernel(width, dwidth, expert_ref, *refs):
-    pieces, hid_ref, out_ref, a_ref, b_ref = refs[:6], refs[6], refs[7], refs[8], refs[9]
-    ny, rows, total = pieces[0].shape
-    cols = total - LANES
+def weight_kernel(block, expert_ref, *refs):
+    pieces, hid_ref, out_ref, a_ref, be_ref, bd_ref = refs[:6], *refs[6:11]
+    ny, rows, _ = pieces[0].shape
     group = 6 * rows
     expert = expert_ref[0].astype(jnp.float32)
+    width = be_ref.shape[1]
     quarter = hid_ref.shape[1] - SLOT_ROWS
-    base = out_ref.shape[2] - LANES
-    b_ref[...] = jnp.zeros_like(b_ref)
     for y in range(ny):
         top = y * group
         for i, piece in enumerate(pieces):
-            a_ref[top + i * rows : top + (i + 1) * rows, :] = piece[y, :, :cols]
-        meta = jnp.concatenate([piece[y, :, cols:] for piece in pieces], axis=0).astype(jnp.float32)
-        slot, prob, token = routing(meta, expert)
+            a_ref[top + i * rows : top + (i + 1) * rows, :] = piece[y]
+        meta = jnp.concatenate([piece[y, :, block : block + 8] for piece in pieces], axis=0)
+        slot, prob, token = routing(meta.astype(jnp.float32), expert)
         weighted = dot(one_hot(slot, SLOT_ROWS, prob), hid_ref[y, :SLOT_ROWS, :width], ((1,), (0,)))
-        b_ref[top : top + group, :width] = weighted.astype(jnp.bfloat16)
+        be_ref[top : top + group, :] = weighted.astype(jnp.bfloat16)
         dense = jnp.concatenate(
             [hid_ref[y, SLOT_ROWS:, j * LANES : (j + 1) * LANES] for j in range(4)], axis=0
         )
         moved = dot(one_hot(token, 4 * quarter), dense, ((1,), (0,)))
-        b_ref[top : top + group, base : base + LANES] = moved.astype(jnp.bfloat16)
-    summed = dot(a_ref[...], b_ref[...], ((0,), (0,))).astype(jnp.bfloat16)
-    block = out_ref.shape[1]
-    for x in range(out_ref.shape[0]):
-        out_ref[x] = summed[x * block : (x + 1) * block]
+        bd_ref[top : top + group, :] = moved.astype(jnp.bfloat16)
+    rows_in = a_ref[...]
+    nx, height, stride = out_ref.shape
+    summed = dot(be_ref[...], rows_in, ((0,), (0,))).astype(jnp.bfloat16)
+    dsummed = dot(bd_ref[...], rows_in, ((0,), (0,))).astype(jnp.bfloat16)
+    for x in range(nx):
+        out_ref[x, :width, :] = summed[:, x * stride : (x + 1) * stride]
+        out_ref[x, width:, :] = dsummed[: height - width, x * stride : (x + 1) * stride]
 
 
 def sum_kernel(scale, in_ref, expert_ref, dense_ref):
@@ -109,9 +135,9 @@
     for x in range(1, in_ref.shape[0]):
         summed = summed + in_ref[x].astype(jnp.float32)
     summed = (summed * scale).astype(jnp.bfloat16)
-    base = in_ref.shape[2] - LANES
-    expert_ref[0] = summed[:, : expert_ref.shape[2]]
-    dense_ref[...] = summed[:, base : base + dense_ref.shape[1]]
+    width, block = expert_ref.shape
+    expert_ref[...] = summed[:width, :block]
+    dense_ref[...] = summed[width : width + dense_ref.shape[0], :block]
 
 
 def place(onehot, values):
@@ -193,8 +219,10 @@
     eighth = tokens // (RUN * CORES)
     block = width // (nx * ny)
     bf16 = jnp.bfloat16
+    stride = -(-(block + 8) // LANES) * LANES
     expert_arr = expert.reshape(1).astype(jnp.int32)
     smem = pl.BlockSpec(memory_space=pltpu.SMEM)
+    vmem = pl.BlockSpec(memory_space=pltpu.VMEM)
 
     hidden = pl.pallas_call(
         hidden_kernel,
@@ -203,29 +231,23 @@
     )(expert_gate_pre, expert_up_pre, dense_gate_pre, dense_up_pre)
     hiddens = lax.all_gather(hidden, "y", axis=0)
 
-    token = expert * tokens + lax.broadcasted_iota(jnp.int32, (tokens, 1), 0)
-    meta = jnp.concatenate(
-        [
-            expert_ids.astype(bf16),
-            (slot_positions + expert * capacity).astype(bf16),
-            gate_prob,
-            token.astype(bf16),
-        ],
-        axis=1,
-    )
-    meta = jnp.pad(meta, ((0, 0), (0, LANES - meta.shape[1])))
-    mine = jnp.concatenate(
-        [
-            lax.dynamic_slice(grad_out, (part * eighth, 0), (eighth, width)),
-            lax.dynamic_slice(meta, (part * eighth, 0), (eighth, LANES)),
-        ],
-        axis=1,
+    mine = pl.pallas_call(
+        functools.partial(pick_kernel, capacity),
+        out_shape=jax.ShapeDtypeStruct((eighth, width + LANES), bf16),
+        in_specs=[smem] + [vmem] * 4,
+        compiler_params=params(),
+    )(
+        jnp.stack([expert, part]).astype(jnp.int32),
+        grad_out,
+        gate_prob.T,
+        expert_ids.T,
+        slot_positions.T,
     )
     rows = lax.all_gather(mine, "e", axis=0, tiled=True)
 
     chunks = pl.pallas_call(
         functools.partial(split_kernel, nx, ny),
-        out_shape=jax.ShapeDtypeStruct((ny, ne * eighth, nx * block + LANES), bf16),
+        out_shape=jax.ShapeDtypeStruct((ny, ne * eighth, nx * stride), bf16),
         compiler_params=params(),
     )(rows)
     chunks = lax.all_to_all(chunks, "y", split_axis=0, concat_axis=0, tiled=True)
@@ -236,29 +258,8 @@
         return along + other
 
     row_pieces = spread(rows)
+    chunks, *row_pieces = lax.optimization_barrier((chunks, *row_pieces))
     chunk_pieces = spread(chunks)
-
-    cols = hwidth + (-hwidth) % LANES + LANES
-    ktotal = ny * 6 * ne * eighth
-    partial_sums = pl.pallas_call(
-        functools.partial(weight_kernel, hwidth, dwidth),
-        out_shape=jax.ShapeDtypeStruct((nx, block, cols), bf16),
-        in_specs=[smem] + [pl.BlockSpec(memory_space=pltpu.VMEM)] * 7,
-        scratch_shapes=[
-            pltpu.VMEM((ktotal, nx * block), bf16),
-            pltpu.VMEM((ktotal, cols), bf16),
-        ],
-        compiler_params=params(),
-    )(expert_arr, *chunk_pieces, hiddens)
-    landed = lax.all_to_all(partial_sums, "x", split_axis=0, concat_axis=0, tiled=True)
-    expert_down_grad, dense_down_grad = pl.pallas_call(
-        functools.partial(sum_kernel, 1.0 / (nx * ny)),
-        out_shape=(
-            jax.ShapeDtypeStruct((1, block, hwidth), bf16),
-            jax.ShapeDtypeStruct((block, dwidth), bf16),
-        ),
-        compiler_params=params(),
-    )(landed)
 
     depth = 1024
     data_spec = pl.BlockSpec((ne * eighth, depth), lambda k: (0, k))
@@ -307,15 +308,40 @@
         dense_gate_pre,
         dense_up_pre,
     )
+
+    expert_arr, dots = lax.optimization_barrier((expert_arr, dots))
+    height = hwidth + -(-dwidth // 16) * 16
+    ktotal = ny * ne * tokens
+    partial_sums = pl.pallas_call(
+        functools.partial(weight_kernel, block),
+        out_shape=jax.ShapeDtypeStruct((nx, height, stride), bf16),
+        in_specs=[smem] + [vmem] * 7,
+        scratch_shapes=[
+            pltpu.VMEM((ktotal, nx * stride), bf16),
+            pltpu.VMEM((ktotal, hwidth), bf16),
+            pltpu.VMEM((ktotal, LANES), bf16),
+        ],
+        compiler_params=params(),
+    )(expert_arr, *chunk_pieces, hiddens)
+    partial_sums, dots = lax.optimization_barrier((partial_sums, dots))
+    landed = lax.all_to_all(partial_sums, "x", split_axis=0, concat_axis=0, tiled=True)
     slot_prob_grad = lax.psum(dots[:1], ("l", "c"))
+    expert_down_grad, dense_down_grad = pl.pallas_call(
+        functools.partial(sum_kernel, 1.0 / (nx * ny)),
+        out_shape=(
+            jax.ShapeDtypeStruct((hwidth, block), bf16),
+            jax.ShapeDtypeStruct((dwidth, block), bf16),
+        ),
+        compiler_params=params(),
+    )(landed)
     return (
         gate_grad,
         up_grad,
         slot_prob_grad,
-        expert_down_grad,
+        expert_down_grad.T[None],
         dense_gate_grad,
         dense_up_grad,
-        dense_down_grad,
+        dense_down_grad.T,
     )
 
 

time: 156 us -> 143 us (0.917)
  blocking collectives: 67.5 us -> 39.3 us
  starting transfers between devices: 35.2 us -> 49.4 us
  waiting for transfers between devices: 4.61 us -> 10.7 us
  local copies, waits for them, and re-layouts: 7.52 us -> 3.32 us
    all_to_all x1 -> x0, blocking collectives: 28.7 us -> none  [local(): lax.all_to_all(chunks, 'y', split_axis=0, concat_axis=0, tiled=True)]
    all_to_all x0 -> x1, starting transfers between devices: none -> 7.13 us  [local(): lax.all_to_all(chunks, 'y', split_axis=0, concat_axis=0, tiled=True)]
    ppermute x4, starting transfers between devices: 11.4 us -> 16 us  [spread(): lax.ppermute(piece, ('e', 'l'), ring(ne * RUN, d))]
    all_to_all x1, waiting for transfers between devices: 0.01 us -> 4.11 us  [local(): lax.all_to_all(partial_sums, 'x', split_axis=0, concat_axis=0, tiled=True)]
    unnamed x28 -> x24, local copies, waits for them, and re-layouts: 6.68 us -> 2.63 us
    ppermute x6, starting transfers between devices: 19.7 us -> 22.2 us  [spread(): other = [lax.ppermute(p, 'c', ring(CORES, 1)) for p in along]]
    all_to_all x0 -> x1, waiting for transfers between devices: none -> 1.88 us  [local(): lax.all_to_all(chunks, 'y', split_axis=0, concat_axis=0, tiled=True)]
    pallas_call x1 -> x2, Pallas kernels: 7.37 us -> 8.75 us  [the longest x1 6.75 us: local(): pl.pallas_call(functools.partial(weight_kernel, block), out_shape=jax.Sha...]
  transfers between devices with their start and end apart: 12 -> 13, of which waited for: 2 -> 3; matrix products, arithmetic and copies ran while one was open for 2% -> 1% of each run, Pallas kernels for 13% -> 10%
where the time goes in v2:
time: 143 us; the launch traced here: 142 us
  starting transfers between devices  49.4 us (35%)
  blocking collectives  39.3 us (27%)
  Pallas kernels  24.8 us (17%)
  between operations  14.3 us (10%)
  waiting for transfers between devices  10.7 us (7%)
  local copies, waits for them, and re-layouts  3.32 us (2%)
    all_gather x1, blocking collectives, local(): rows = lax.all_gather(mine, 'e', axis=0, tiled=True)  28.9 us
    ppermute x6, starting transfers between devices, spread(): other = [lax.ppermute(p, 'c', ring(CORES, 1)) for p in along]  22.2 us
    ppermute x4, starting transfers between devices, spread(): lax.ppermute(piece, ('e', 'l'), ring(ne * RUN, d))  16 us
    psum x1, blocking collectives, local(): slot_prob_grad = lax.psum(dots[:1], ('l', 'c'))  10.5 us
    pallas_call x1, Pallas kernels, local(): pl.pallas_call(back_kernel, grid=(width // depth,), out_shape=(jax.ShapeD...  10 us
    all_to_all x1, starting transfers between devices, local(): lax.all_to_all(chunks, 'y', split_axis=0, concat_axis=0, tiled=True)  7.13 us
    pallas_call x1, Pallas kernels, local(): pl.pallas_call(functools.partial(weight_kernel, block), out_shape=jax.Sha...  6.75 us
    ppermute x4, waiting for transfers between devices, spread(): lax.ppermute(piece, ('e', 'l'), ring(ne * RUN, d))  4.65 us
  transfers between devices with their start and end apart: 13, of which 3 were waited for; matrix products, arithmetic and copies ran while one was open for 1% of the time, Pallas kernels for 10%

profile of v2, /device:TPU:1, one launch (start us, length us, event | category | flops | bytes accessed | tf_op | source)
XLA Modules:
  0.0 142.4 jit_solution(11886560292980984489)
XLA Ops:
  7.2 0.0 all-gather.3.cloned.1.call-start
  7.2 1.8 %shard_map.156 = bf16[208,512]{1,0:T(8,128)(2,1)} custom-call(bf16[1,156,416]{2,1,0:T(8,128)(2,1)} %gate_ref.1, bf16[1,156,416]{2,1,0:T(8,128)(2,1)} %up_ref.1, bf16[192,104]{1,0:T(8,128)(2,1)} %dgate_ref.1, bf16[192,104]{1,0:T(8,128)(2,1)} %dup_ref.1), custom_call_target="tpu_custom_call" | custom-call | tf_op jit(solution)/shard_map/pallas_call | solution.py:227
  9.0 0.0 all-gather.3.cloned.1.call-update
  9.0 0.6 pad_add_fusion.at_ref
  9.6 2.0 %shard_map.153 = bf16[8,7296]{1,0:T(8,128)(2,1)} custom-call(s32[2]{0:T(128)} %pad_add_fusion.at_ref, bf16[48,7168]{1,0:T(8,128)(2,1)} %rows_ref.1, bf16[2,48]{1,0:T(2,128)(2,1)} %bitcast.13, s32[2,48]{1,0:T(2,128)} %bitcast.11, s32[2,48]{1,0:T(2,128)} %bitcast.12), custom_call_target="tpu_custom_call" | custom-call | tf_op jit(solution)/shard_map/pallas_call | solution.py:234
  11.6 28.9 %all_gather.9.rows_ref.refs_0_.refs_6_ = bf16[32,7296]{1,0:T(8,128)(2,1)S(1)} all-gather(bf16[8,7296]{1,0:T(8,128)(2,1)} %shard_map.153), channel_id=1, replica_groups=mesh['x'=4,'y'=8,'e'=4,'l'=3,'c'=2] {'e'}, dimensions={0}, use_global_device_ids=true | all-gather | bytes 583680 | tf_op jit(solution)/shard_map/all_gather | solution.py:246
  40.5 0.0 copy-start
  40.5 3.4 %collective-permute-start.1 = (bf16[32,7296]{1,0:T(8,128)(2,1)S(1)}, bf16[32,7296]{1,0:T(8,128)(2,1)S(1)}, u32[]{:S(2)}, u32[]{:S(2)}) collective-permute-start(bf16[32,7296]{1,0:T(8,128)(2,1)S(1)} %all_gather.9.rows_ref.refs_0_.refs_6_), channel_id=1, source_target_pairs={{0,22},{2,0},{4,2},{6,4},{8,6},{10,8},{12,10},{14,12},{16,14},{18,... | collective-permute-start | bytes 1400840 | tf_op jit(solution)/shard_map/ppermute | solution.py:256
  43.9 2.4 %collective-permute-start = (bf16[32,7296]{1,0:T(8,128)(2,1)S(1)}, bf16[32,7296]{1,0:T(8,128)(2,1)S(1)}, u32[]{:S(2)}, u32[]{:S(2)}) collective-permute-start(bf16[32,7296]{1,0:T(8,128)(2,1)S(1)} %all_gather.9.rows_ref.refs_0_.refs_6_), channel_id=1, source_target_pairs={{0,2},{2,4},{4,6},{6,8},{8,10},{10,12},{12,14},{14,16},{16,18},{18... | collective-permute-start | bytes 1400840 | tf_op jit(solution)/shard_map/ppermute | solution.py:256
  46.4 0.0 copy-done
  46.4 2.2 %shard_map.154 = bf16[8,32,1024]{2,1,0:T(8,128)(2,1)} custom-call(bf16[32,7296]{1,0:T(8,128)(2,1)} %copy-done), custom_call_target="tpu_custom_call" | custom-call | tf_op jit(solution)/shard_map/pallas_call | solution.py:248
  48.5 7.1 %all-to-all-start = ((bf16[8,32,1024]{2,1,0:T(8,128)(2,1)}), bf16[8,32,1024]{2,1,0:T(8,128)(2,1)S(1)}, u32[]{:S(2)}, u32[]{:S(2)}) async-start(bf16[8,32,1024]{2,1,0:T(8,128)(2,1)} %shard_map.154), calls=%async_computation | async-start | bytes 1048576 | tf_op jit(solution)/shard_map/all_to_all | solution.py:253
  55.7 7.1 %collective-permute-start.2 = (bf16[32,7296]{1,0:T(8,128)(2,1)}, bf16[32,7296]{1,0:T(8,128)(2,1)S(1)}, u32[]{:S(2)}, u32[]{:S(2)}) collective-permute-start(bf16[32,7296]{1,0:T(8,128)(2,1)} %copy-done), channel_id=1, source_target_pairs={{0,1},{1,0},{2,3},{3,2},{4,5},{5,4},{6,7},{7,6},{8,9},{9,8},{10,11... | collective-permute-start | bytes 1400840 | tf_op jit(solution)/shard_map/ppermute | solution.py:257
  62.8 0.0 collective-permute-done.1.refs_2_.refs_8_
  62.8 0.0 copy-start.3
  62.8 1.9 %collective-permute-start.4 = (bf16[32,7296]{1,0:T(8,128)(2,1)S(1)}, bf16[32,7296]{1,0:T(8,128)(2,1)S(1)}, u32[]{:S(2)}, u32[]{:S(2)}) collective-permute-start(bf16[32,7296]{1,0:T(8,128)(2,1)S(1)} %collective-permute-done.1.refs_2_.refs_8_), channel_id=1, source_target_pairs={{0,1},{1,0},{2,3},{3,2},{4,5},{5,4},{6,7},{7,6},{8,9},{9,8},{10,11... | collective-permute-start | bytes 1400840 | tf_op jit(solution)/shard_map/ppermute | solution.py:257
  64.8 0.0 collective-permute-done.refs_1_.refs_7_
  64.8 0.0 copy-start.4
  64.8 2.4 %collective-permute-start.3 = (bf16[32,7296]{1,0:T(8,128)(2,1)S(1)}, bf16[32,7296]{1,0:T(8,128)(2,1)S(1)}, u32[]{:S(2)}, u32[]{:S(2)}) collective-permute-start(bf16[32,7296]{1,0:T(8,128)(2,1)S(1)} %collective-permute-done.refs_1_.refs_7_), channel_id=1, source_target_pairs={{0,1},{1,0},{2,3},{3,2},{4,5},{5,4},{6,7},{7,6},{8,9},{9,8},{10,11... | collective-permute-start | bytes 1400840 | tf_op jit(solution)/shard_map/ppermute | solution.py:257
  67.2 0.0 collective-permute-done.2.refs_3_.refs_9_
  67.2 0.0 copy-start.5
  67.2 1.9 %all-to-all-done.refs_0_ = bf16[8,32,1024]{2,1,0:T(8,128)(2,1)S(1)} async-done(((bf16[8,32,1024]{2,1,0:T(8,128)(2,1)}), bf16[8,32,1024]{2,1,0:T(8,128)(2,1)S(1)}, u32[]{:S(2)}, u32[]{:S(2)}) %all-to-all-start) | async-done | bytes 524320 | tf_op jit(solution)/shard_map/all_to_all | solution.py:253
  69.1 0.0 copy-start.2
  69.1 0.0 collective-permute-done.4.refs_5_.refs_11_
  69.1 0.0 copy-start.6
  69.1 0.0 collective-permute-done.3.refs_4_.refs_10_
  69.1 0.0 copy-start.7
  69.1 5.6 %collective-permute-start.6 = (bf16[8,32,1024]{2,1,0:T(8,128)(2,1)S(1)}, bf16[8,32,1024]{2,1,0:T(8,128)(2,1)S(1)}, u32[]{:S(2)}, u32[]{:S(2)}) collective-permute-start(bf16[8,32,1024]{2,1,0:T(8,128)(2,1)S(1)} %all-to-all-done.refs_0_), channel_id=1, source_target_pairs={{0,22},{2,0},{4,2},{6,4},{8,6},{10,8},{12,10},{14,12},{16,14},{18,... | collective-permute-start | bytes 1572872 | tf_op jit(solution)/shard_map/ppermute | solution.py:256
  74.7 4.6 %collective-permute-start.5 = (bf16[8,32,1024]{2,1,0:T(8,128)(2,1)S(1)}, bf16[8,32,1024]{2,1,0:T(8,128)(2,1)S(1)}, u32[]{:S(2)}, u32[]{:S(2)}) collective-permute-start(bf16[8,32,1024]{2,1,0:T(8,128)(2,1)S(1)} %all-to-all-done.refs_0_), channel_id=1, source_target_pairs={{0,2},{2,4},{4,6},{6,8},{8,10},{10,12},{12,14},{14,16},{16,18},{18... | collective-permute-start | bytes 1572872 | tf_op jit(solution)/shard_map/ppermute | solution.py:256
  79.3 4.6 %collective-permute-start.7 = (bf16[8,32,1024]{2,1,0:T(8,128)(2,1)S(1)}, bf16[8,32,1024]{2,1,0:T(8,128)(2,1)S(1)}, u32[]{:S(2)}, u32[]{:S(2)}) collective-permute-start(bf16[8,32,1024]{2,1,0:T(8,128)(2,1)S(1)} %all-to-all-done.refs_0_), channel_id=1, source_target_pairs={{0,1},{1,0},{2,3},{3,2},{4,5},{5,4},{6,7},{7,6},{8,9},{9,8},{10,11... | collective-permute-start | bytes 1572872 | tf_op jit(solution)/shard_map/ppermute | solution.py:257
  83.9 4.6 %collective-permute-done.6.refs_2_ = bf16[8,32,1024]{2,1,0:T(8,128)(2,1)S(1)} collective-permute-done((bf16[8,32,1024]{2,1,0:T(8,128)(2,1)S(1)}, bf16[8,32,1024]{2,1,0:T(8,128)(2,1)S(1)}, u32[]{:S(2)}, u32[]{:S(2)}) %collective-permute-start.6) | collective-permute-done | bytes 524320 | tf_op jit(solution)/shard_map/ppermute | solution.py:256
  88.5 0.0 copy-start.8
  88.5 3.6 %collective-permute-start.9 = (bf16[8,32,1024]{2,1,0:T(8,128)(2,1)S(1)}, bf16[8,32,1024]{2,1,0:T(8,128)(2,1)S(1)}, u32[]{:S(2)}, u32[]{:S(2)}) collective-permute-start(bf16[8,32,1024]{2,1,0:T(8,128)(2,1)S(1)} %collective-permute-done.6.refs_2_), channel_id=1, source_target_pairs={{0,1},{1,0},{2,3},{3,2},{4,5},{5,4},{6,7},{7,6},{8,9},{9,8},{10,11... | collective-permute-start | bytes 1572872 | tf_op jit(solution)/shard_map/ppermute | solution.py:257
  92.1 0.0 collective-permute-done.5.refs_1_
  92.2 0.0 copy-start.9
  92.2 2.6 %collective-permute-start.8 = (bf16[8,32,1024]{2,1,0:T(8,128)(2,1)S(1)}, bf16[8,32,1024]{2,1,0:T(8,128)(2,1)}, u32[]{:S(2)}, u32[]{:S(2)}) collective-permute-start(bf16[8,32,1024]{2,1,0:T(8,128)(2,1)S(1)} %collective-permute-done.5.refs_1_), channel_id=1, source_target_pairs={{0,1},{1,0},{2,3},{3,2},{4,5},{5,4},{6,7},{7,6},{8,9},{9,8},{10,11... | collective-permute-start | bytes 1572872 | tf_op jit(solution)/shard_map/ppermute | solution.py:257
  94.7 0.0 copy-done.3
  94.8 0.0 copy-done.4
  94.8 0.0 copy-done.5
  94.8 0.0 copy-done.6
  94.8 0.0 copy-done.7
  94.8 10.0 %shard_map.155 = (bf16[1,156,416]{2,1,0:T(8,128)(2,1)}, bf16[1,156,416]{2,1,0:T(8,128)(2,1)}, f32[8,156]{1,0:T(8,128)}, bf16[192,104]{1,0:T(8,128)(2,1)}, bf16[192,104]{1,0:T(8,128)(2,1)}) custom-call(s32[1]{0:T(128)} %bitcast.expert_ref, bf16[32,7296]{1,0:T(8,128)(2,1)} %copy-done, bf16[32,7296]{1,0:T(8,128)(2,1)} %copy-done.4, bf16[32,7296]{1,0:T(8,128)(2,1)} %copy-done.3, ...), custom_call_target="tpu_custom_call" | custom-call | tf_op jit(solution)/shard_map/pallas_call | solution.py:267
  104.8 0.0 copy-done.2
  104.8 0.0 copy-done.8
  104.8 0.0 copy-done.9
  104.8 0.0 collective-permute-done.7.refs_3_
  104.8 0.0 copy-start.10
  104.8 0.0 collective-permute-done.9.refs_5_
  104.9 0.8 copy-done.10
  105.6 0.0 copy-start.11
  105.6 0.8 copy-done.11
  106.4 0.0 collective-permute-done.8.refs_4_
  106.4 0.0 all-gather.3.cloned.1.call-done
  106.4 6.8 %shard_map.157 = bf16[4,528,256]{2,1,0:T(8,128)(2,1)} custom-call(s32[1]{0:T(128)} %bitcast.expert_ref, bf16[8,32,1024]{2,1,0:T(8,128)(2,1)} %copy-done.2, bf16[8,32,1024]{2,1,0:T(8,128)(2,1)} %copy-done.9, bf16[8,32,1024]{2,1,0:T(8,128)(2,1)} %copy-done.8, bf16[8,32,1024]{2,1,0:T(8,128)(2,1)} %copy-done.10, ...), custom_call_target="tpu_custom_call" | custom-call | tf_op jit(solution)/shard_map/pallas_call | solution.py:315
  113.2 4.0 %all-to-all-start.1 = ((bf16[4,528,256]{2,1,0:T(8,128)(2,1)}), bf16[4,528,256]{2,1,0:T(8,128)(2,1)S(1)}, u32[]{:S(2)}, u32[]{:S(2)}) async-start(bf16[4,528,256]{2,1,0:T(8,128)(2,1)} %shard_map.157), calls=%async_computation.1 | async-start | bytes 2162688 | tf_op jit(solution)/shard_map/all_to_all | solution.py:327
  117.2 0.7 slice.3
  117.9 10.5 %psum.7 = f32[1,156]{1,0:T(1,128)} all-reduce(f32[1,156]{1,0:T(1,128)S(1)} %slice.3), channel_id=1, replica_groups=mesh['x'=4,'y'=8,'e'=4,'l'=3,'c'=2] {'l','c'}, use_global_device_ids=true, to_apply=%region_0.0 | all-reduce | flops 156 | bytes 1248 | tf_op jit(solution)/shard_map/psum | solution.py:328
  128.4 4.1 %all-to-all-done.1.in_ref = bf16[4,528,256]{2,1,0:T(8,128)(2,1)S(1)} async-done(((bf16[4,528,256]{2,1,0:T(8,128)(2,1)}), bf16[4,528,256]{2,1,0:T(8,128)(2,1)S(1)}, u32[]{:S(2)}, u32[]{:S(2)}) %all-to-all-start.1) | async-done | bytes 1081376 | tf_op jit(solution)/shard_map/all_to_all | solution.py:327
  132.5 0.0 copy-start.1
  132.5 1.0 copy-done.1
  133.5 2.0 %shard_map.158 = (bf16[416,224]{1,0:T(8,128)(2,1)}, bf16[104,224]{1,0:T(8,128)(2,1)}) custom-call(bf16[4,528,256]{2,1,0:T(8,128)(2,1)} %copy-done.1), custom_call_target="tpu_custom_call" | custom-call | tf_op jit(solution)/shard_map/pallas_call | solution.py:329
Async XLA Ops:
  7.2 99.3 %all-gather.3.cloned.1.call-start = ((), (), s32[]{:S(2)}) async-start(), calls=%async_computation.2 | async-start | bytes 1916928 | tf_op jit(solution)/shard_map/all_gather | solution.py:232
  40.5 5.9 %copy-start = (bf16[32,7296]{1,0:T(8,128)(2,1)}, bf16[32,7296]{1,0:T(8,128)(2,1)S(1)}, u32[]{:S(2)}) copy-start(bf16[32,7296]{1,0:T(8,128)(2,1)S(1)} %all_gather.9.rows_ref.refs_0_.refs_6_) | copy-start | bytes 1400836
  40.5 22.3 %collective-permute-start.1 = (bf16[32,7296]{1,0:T(8,128)(2,1)S(1)}, bf16[32,7296]{1,0:T(8,128)(2,1)S(1)}, u32[]{:S(2)}, u32[]{:S(2)}) collective-permute-start(bf16[32,7296]{1,0:T(8,128)(2,1)S(1)} %all_gather.9.rows_ref.refs_0_.refs_6_), channel_id=1, source_target_pairs={{0,22},{2,0},{4,2},{6,4},{8,6},{10,8},{12,10},{14,12},{16,14},{18,... | collective-permute-start | bytes 1400840 | tf_op jit(solution)/shard_map/ppermute | solution.py:256
  43.9 20.9 %collective-permute-start = (bf16[32,7296]{1,0:T(8,128)(2,1)S(1)}, bf16[32,7296]{1,0:T(8,128)(2,1)S(1)}, u32[]{:S(2)}, u32[]{:S(2)}) collective-permute-start(bf16[32,7296]{1,0:T(8,128)(2,1)S(1)} %all_gather.9.rows_ref.refs_0_.refs_6_), channel_id=1, source_target_pairs={{0,2},{2,4},{4,6},{6,8},{8,10},{10,12},{12,14},{14,16},{16,18},{18... | collective-permute-start | bytes 1400840 | tf_op jit(solution)/shard_map/ppermute | solution.py:256
  48.5 20.5 %all-to-all-start = ((bf16[8,32,1024]{2,1,0:T(8,128)(2,1)}), bf16[8,32,1024]{2,1,0:T(8,128)(2,1)S(1)}, u32[]{:S(2)}, u32[]{:S(2)}) async-start(bf16[8,32,1024]{2,1,0:T(8,128)(2,1)} %shard_map.154), calls=%async_computation | async-start | bytes 1048576 | tf_op jit(solution)/shard_map/all_to_all | solution.py:253
  55.7 11.5 %collective-permute-start.2 = (bf16[32,7296]{1,0:T(8,128)(2,1)}, bf16[32,7296]{1,0:T(8,128)(2,1)S(1)}, u32[]{:S(2)}, u32[]{:S(2)}) collective-permute-start(bf16[32,7296]{1,0:T(8,128)(2,1)} %copy-done), channel_id=1, source_target_pairs={{0,1},{1,0},{2,3},{3,2},{4,5},{5,4},{6,7},{7,6},{8,9},{9,8},{10,11... | collective-permute-start | bytes 1400840 | tf_op jit(solution)/shard_map/ppermute | solution.py:257
  62.8 31.9 %copy-start.3 = (bf16[32,7296]{1,0:T(8,128)(2,1)}, bf16[32,7296]{1,0:T(8,128)(2,1)S(1)}, u32[]{:S(2)}) copy-start(bf16[32,7296]{1,0:T(8,128)(2,1)S(1)} %collective-permute-done.1.refs_2_.refs_8_) | copy-start | bytes 1400836
  62.8 6.3 %collective-permute-start.4 = (bf16[32,7296]{1,0:T(8,128)(2,1)S(1)}, bf16[32,7296]{1,0:T(8,128)(2,1)S(1)}, u32[]{:S(2)}, u32[]{:S(2)}) collective-permute-start(bf16[32,7296]{1,0:T(8,128)(2,1)S(1)} %collective-permute-done.1.refs_2_.refs_8_), channel_id=1, source_target_pairs={{0,1},{1,0},{2,3},{3,2},{4,5},{5,4},{6,7},{7,6},{8,9},{9,8},{10,11... | collective-permute-start | bytes 1400840 | tf_op jit(solution)/shard_map/ppermute | solution.py:257
  64.8 30.0 %copy-start.4 = (bf16[32,7296]{1,0:T(8,128)(2,1)}, bf16[32,7296]{1,0:T(8,128)(2,1)S(1)}, u32[]{:S(2)}) copy-start(bf16[32,7296]{1,0:T(8,128)(2,1)S(1)} %collective-permute-done.refs_1_.refs_7_) | copy-start | bytes 1400836
  64.8 4.3 %collective-permute-start.3 = (bf16[32,7296]{1,0:T(8,128)(2,1)S(1)}, bf16[32,7296]{1,0:T(8,128)(2,1)S(1)}, u32[]{:S(2)}, u32[]{:S(2)}) collective-permute-start(bf16[32,7296]{1,0:T(8,128)(2,1)S(1)} %collective-permute-done.refs_1_.refs_7_), channel_id=1, source_target_pairs={{0,1},{1,0},{2,3},{3,2},{4,5},{5,4},{6,7},{7,6},{8,9},{9,8},{10,11... | collective-permute-start | bytes 1400840 | tf_op jit(solution)/shard_map/ppermute | solution.py:257
  67.2 27.6 %copy-start.5 = (bf16[32,7296]{1,0:T(8,128)(2,1)}, bf16[32,7296]{1,0:T(8,128)(2,1)S(1)}, u32[]{:S(2)}) copy-start(bf16[32,7296]{1,0:T(8,128)(2,1)S(1)} %collective-permute-done.2.refs_3_.refs_9_) | copy-start | bytes 1400836
  69.1 35.7 %copy-start.2 = (bf16[8,32,1024]{2,1,0:T(8,128)(2,1)}, bf16[8,32,1024]{2,1,0:T(8,128)(2,1)S(1)}, u32[]{:S(2)}) copy-start(bf16[8,32,1024]{2,1,0:T(8,128)(2,1)S(1)} %all-to-all-done.refs_0_) | copy-start | bytes 1572868
  69.1 25.7 %copy-start.6 = (bf16[32,7296]{1,0:T(8,128)(2,1)}, bf16[32,7296]{1,0:T(8,128)(2,1)S(1)}, u32[]{:S(2)}) copy-start(bf16[32,7296]{1,0:T(8,128)(2,1)S(1)} %collective-permute-done.4.refs_5_.refs_11_) | copy-start | bytes 1400836
  69.1 25.7 %copy-start.7 = (bf16[32,7296]{1,0:T(8,128)(2,1)}, bf16[32,7296]{1,0:T(8,128)(2,1)S(1)}, u32[]{:S(2)}) copy-start(bf16[32,7296]{1,0:T(8,128)(2,1)S(1)} %collective-permute-done.3.refs_4_.refs_10_) | copy-start | bytes 1400836
  69.1 19.4 %collective-permute-start.6 = (bf16[8,32,1024]{2,1,0:T(8,128)(2,1)S(1)}, bf16[8,32,1024]{2,1,0:T(8,128)(2,1)S(1)}, u32[]{:S(2)}, u32[]{:S(2)}) collective-permute-start(bf16[8,32,1024]{2,1,0:T(8,128)(2,1)S(1)} %all-to-all-done.refs_0_), channel_id=1, source_target_pairs={{0,22},{2,0},{4,2},{6,4},{8,6},{10,8},{12,10},{14,12},{16,14},{18,... | collective-permute-start | bytes 1572872 | tf_op jit(solution)/shard_map/ppermute | solution.py:256
  74.7 17.5 %collective-permute-start.5 = (bf16[8,32,1024]{2,1,0:T(8,128)(2,1)S(1)}, bf16[8,32,1024]{2,1,0:T(8,128)(2,1)S(1)}, u32[]{:S(2)}, u32[]{:S(2)}) collective-permute-start(bf16[8,32,1024]{2,1,0:T(8,128)(2,1)S(1)} %all-to-all-done.refs_0_), channel_id=1, source_target_pairs={{0,2},{2,4},{4,6},{6,8},{8,10},{10,12},{12,14},{14,16},{16,18},{18... | collective-permute-start | bytes 1572872 | tf_op jit(solution)/shard_map/ppermute | solution.py:256
  79.3 25.5 %collective-permute-start.7 = (bf16[8,32,1024]{2,1,0:T(8,128)(2,1)S(1)}, bf16[8,32,1024]{2,1,0:T(8,128)(2,1)S(1)}, u32[]{:S(2)}, u32[]{:S(2)}) collective-permute-start(bf16[8,32,1024]{2,1,0:T(8,128)(2,1)S(1)} %all-to-all-done.refs_0_), channel_id=1, source_target_pairs={{0,1},{1,0},{2,3},{3,2},{4,5},{5,4},{6,7},{7,6},{8,9},{9,8},{10,11... | collective-permute-start | bytes 1572872 | tf_op jit(solution)/shard_map/ppermute | solution.py:257
  88.5 16.3 %copy-start.8 = (bf16[8,32,1024]{2,1,0:T(8,128)(2,1)}, bf16[8,32,1024]{2,1,0:T(8,128)(2,1)S(1)}, u32[]{:S(2)}) copy-start(bf16[8,32,1024]{2,1,0:T(8,128)(2,1)S(1)} %collective-permute-done.6.refs_2_) | copy-start | bytes 1572868
  88.5 16.3 %collective-permute-start.9 = (bf16[8,32,1024]{2,1,0:T(8,128)(2,1)S(1)}, bf16[8,32,1024]{2,1,0:T(8,128)(2,1)S(1)}, u32[]{:S(2)}, u32[]{:S(2)}) collective-permute-start(bf16[8,32,1024]{2,1,0:T(8,128)(2,1)S(1)} %collective-permute-done.6.refs_2_), channel_id=1, source_target_pairs={{0,1},{1,0},{2,3},{3,2},{4,5},{5,4},{6,7},{7,6},{8,9},{9,8},{10,11... | collective-permute-start | bytes 1572872 | tf_op jit(solution)/shard_map/ppermute | solution.py:257
  92.2 12.7 %copy-start.9 = (bf16[8,32,1024]{2,1,0:T(8,128)(2,1)}, bf16[8,32,1024]{2,1,0:T(8,128)(2,1)S(1)}, u32[]{:S(2)}) copy-start(bf16[8,32,1024]{2,1,0:T(8,128)(2,1)S(1)} %collective-permute-done.5.refs_1_) | copy-start | bytes 1572868
  92.2 14.3 %collective-permute-start.8 = (bf16[8,32,1024]{2,1,0:T(8,128)(2,1)S(1)}, bf16[8,32,1024]{2,1,0:T(8,128)(2,1)}, u32[]{:S(2)}, u32[]{:S(2)}) collective-permute-start(bf16[8,32,1024]{2,1,0:T(8,128)(2,1)S(1)} %collective-permute-done.5.refs_1_), channel_id=1, source_target_pairs={{0,1},{1,0},{2,3},{3,2},{4,5},{5,4},{6,7},{7,6},{8,9},{9,8},{10,11... | collective-permute-start | bytes 1572872 | tf_op jit(solution)/shard_map/ppermute | solution.py:257
  104.8 0.8 copy-start.10
  105.6 0.8 copy-start.11
  113.2 19.3 %all-to-all-start.1 = ((bf16[4,528,256]{2,1,0:T(8,128)(2,1)}), bf16[4,528,256]{2,1,0:T(8,128)(2,1)S(1)}, u32[]{:S(2)}, u32[]{:S(2)}) async-start(bf16[4,528,256]{2,1,0:T(8,128)(2,1)} %shard_map.157), calls=%async_computation.1 | async-start | bytes 2162688 | tf_op jit(solution)/shard_map/all_to_all | solution.py:327
  132.5 1.0 copy-start.1
Sparse Core Ops, SparseCore 0:
  10.9 49.8 all-gather.2

commit v3 on v2

--- a/solution.py
+++ b/solution.py
@@ -1,4 +1,5 @@
 import functools
+import math
 
 import jax
 import jax.numpy as jnp
@@ -48,14 +49,13 @@
         ]
 
 
-def pick_kernel(capacity, at_ref, rows_ref, prob_ref, ids_ref, slots_ref, out_ref):
-    expert, part = at_ref[0], at_ref[1]
+def pick_kernel(capacity, nx, ny, expert_ref, part_ref, rows_ref, prob_ref, ids_ref, slots_ref, out_ref, cols_ref):
+    expert, part = expert_ref[0], part_ref[0]
     eighth = out_ref.shape[0]
     tokens, width = rows_ref.shape
     lane = lax.broadcasted_iota(jnp.int32, (eighth, tokens), 1)
     row = lax.broadcasted_iota(jnp.int32, (eighth, tokens), 0)
     chosen = jnp.where(lane == row + part * eighth, 1.0, 0.0).astype(jnp.bfloat16)
-    out_ref[:, :width] = dot(chosen, rows_ref[...], ((1,), (0,))).astype(jnp.bfloat16)
     token = expert * tokens + lax.broadcasted_iota(jnp.int32, (2, tokens), 1)
     meta = jnp.concatenate(
         [
@@ -67,20 +67,24 @@
         axis=0,
     ).astype(jnp.bfloat16)
     meta = jnp.concatenate([meta, jnp.zeros((LANES - 8, tokens), jnp.bfloat16)], axis=0)
-    out_ref[:, width:] = dot(chosen, meta, ((1,), (1,))).astype(jnp.bfloat16)
-
-
-def split_kernel(nx, ny, rows_ref, out_ref):
-    width = rows_ref.shape[1] - LANES
+    meta = dot(chosen, meta, ((1,), (1,))).astype(jnp.bfloat16)
+    picked = dot(chosen, rows_ref[...], ((1,), (0,))).astype(jnp.bfloat16)
+    out_ref[:, :width] = picked
+    out_ref[:, width:] = meta
     block = width // (nx * ny)
-    stride = out_ref.shape[2] // nx
+    stride = cols_ref.shape[2] // nx
     for y in range(ny):
         for x in range(nx):
             at = (x * ny + y) * block
-            out_ref[y, :, x * stride : x * stride + block] = rows_ref[:, at : at + block]
-            out_ref[y, :, x * stride + block : (x + 1) * stride] = rows_ref[
-                :, width : width + stride - block
-            ]
+            cols_ref[y, :, x * stride : x * stride + block] = picked[:, at : at + block]
+            cols_ref[y, :, x * stride + block : (x + 1) * stride] = meta[:, : stride - block]
+
+
+def pack_kernel(cols_ref, rows_ref, out_ref):
+    ny, _, span = cols_ref.shape
+    for y in range(ny):
+        out_ref[:, y * span : (y + 1) * span] = cols_ref[y]
+    out_ref[:, ny * span :] = rows_ref[...]
 
 
 def routing(meta, expert):
@@ -101,9 +105,10 @@
     return lax.dot_general(a, b, (dims, ((), ())), preferred_element_type=jnp.float32)
 
 
-def weight_kernel(block, expert_ref, *refs):
+def weight_kernel(block, ny, expert_ref, *refs):
     pieces, hid_ref, out_ref, a_ref, be_ref, bd_ref = refs[:6], *refs[6:11]
-    ny, rows, _ = pieces[0].shape
+    rows, total = pieces[0].shape
+    span = total // ny
     group = 6 * rows
     expert = expert_ref[0].astype(jnp.float32)
     width = be_ref.shape[1]
@@ -111,8 +116,9 @@
     for y in range(ny):
         top = y * group
         for i, piece in enumerate(pieces):
-            a_ref[top + i * rows : top + (i + 1) * rows, :] = piece[y]
-        meta = jnp.concatenate([piece[y, :, block : block + 8] for piece in pieces], axis=0)
+            a_ref[top + i * rows : top + (i + 1) * rows, :] = piece[:, y * span : (y + 1) * span]
+        at = y * span + block
+        meta = jnp.concatenate([piece[:, at : at + 8] for piece in pieces], axis=0)
         slot, prob, token = routing(meta.astype(jnp.float32), expert)
         weighted = dot(one_hot(slot, SLOT_ROWS, prob), hid_ref[y, :SLOT_ROWS, :width], ((1,), (0,)))
         be_ref[top : top + group, :] = weighted.astype(jnp.bfloat16)
@@ -130,7 +136,8 @@
         out_ref[x, width:, :] = dsummed[: height - width, x * stride : (x + 1) * stride]
 
 
-def sum_kernel(scale, in_ref, expert_ref, dense_ref):
+def sum_kernel(scale, in_ref, dots_ref, expert_ref, dense_ref, dots_out):
+    dots_out[...] = jnp.sum(dots_ref[...], axis=0)
     summed = in_ref[0].astype(jnp.float32)
     for x in range(1, in_ref.shape[0]):
         summed = summed + in_ref[x].astype(jnp.float32)
@@ -184,7 +191,7 @@
             (((1,), (1,)), ((), ())),
             precision=lax.Precision.HIGHEST,
             preferred_element_type=jnp.float32,
-        )
+        )[:1]
         scaled = slot_prob * back
         gate_out[0] = (scaled * up_val * slope).astype(jnp.bfloat16)
         up_out[0] = (scaled * activated).astype(jnp.bfloat16)
@@ -231,46 +238,58 @@
     )(expert_gate_pre, expert_up_pre, dense_gate_pre, dense_up_pre)
     hiddens = lax.all_gather(hidden, "y", axis=0)
 
-    mine = pl.pallas_call(
-        functools.partial(pick_kernel, capacity),
-        out_shape=jax.ShapeDtypeStruct((eighth, width + LANES), bf16),
-        in_specs=[smem] + [vmem] * 4,
-        compiler_params=params(),
-    )(
-        jnp.stack([expert, part]).astype(jnp.int32),
-        grad_out,
-        gate_prob.T,
-        expert_ids.T,
-        slot_positions.T,
-    )
-    rows = lax.all_gather(mine, "e", axis=0, tiled=True)
-
-    chunks = pl.pallas_call(
-        functools.partial(split_kernel, nx, ny),
-        out_shape=jax.ShapeDtypeStruct((ny, ne * eighth, nx * stride), bf16),
-        compiler_params=params(),
-    )(rows)
-    chunks = lax.all_to_all(chunks, "y", split_axis=0, concat_axis=0, tiled=True)
-
-    def spread(piece):
-        along = [piece] + [lax.ppermute(piece, ("e", "l"), ring(ne * RUN, d)) for d in (1, -1)]
-        other = [lax.ppermute(p, "c", ring(CORES, 1)) for p in along]
-        return along + other
-
-    row_pieces = spread(rows)
-    chunks, *row_pieces = lax.optimization_barrier((chunks, *row_pieces))
-    chunk_pieces = spread(chunks)
-
-    depth = 1024
-    data_spec = pl.BlockSpec((ne * eighth, depth), lambda k: (0, k))
-    meta_spec = pl.BlockSpec((ne * eighth, LANES), lambda k: (0, width // LANES))
+    part_arr = part.reshape(1).astype(jnp.int32)
+    span = nx * stride
+    mine, cols = pl.pallas_call(
+        functools.partial(pick_kernel, capacity, nx, ny),
+        out_shape=(
+            jax.ShapeDtypeStruct((eighth, width + LANES), bf16),
+            jax.ShapeDtypeStruct((ny, eighth, span), bf16),
+        ),
+        in_specs=[smem] * 2 + [vmem] * 4,
+        compiler_params=params(),
+    )(expert_arr, part_arr, grad_out, gate_prob.T, expert_ids.T, slot_positions.T)
+    cols = lax.all_to_all(cols, "y", split_axis=0, concat_axis=0, tiled=True)
+    packed = pl.pallas_call(
+        pack_kernel,
+        out_shape=jax.ShapeDtypeStruct((eighth, ny * span + width + LANES), bf16),
+        compiler_params=params(),
+    )(cols, mine)
+    packed = lax.all_gather(packed, "e", axis=0, tiled=True)
+    pieces = [packed] + [lax.ppermute(packed, ("e", "l"), ring(ne * RUN, d)) for d in (1, -1)]
+    pieces += [lax.ppermute(p, "c", ring(CORES, 1)) for p in pieces]
+
+    height = hwidth + -(-dwidth // 16) * 16
+    ktotal = ny * ne * tokens
+    partial_sums = pl.pallas_call(
+        functools.partial(weight_kernel, block, ny),
+        grid=(1,),
+        out_shape=jax.ShapeDtypeStruct((nx, height, stride), bf16),
+        in_specs=[smem]
+        + [pl.BlockSpec((ne * eighth, ny * span), lambda k: (0, 0))] * 6
+        + [whole(*hiddens.shape)],
+        out_specs=whole(nx, height, stride),
+        scratch_shapes=[
+            pltpu.VMEM((ktotal, span), bf16),
+            pltpu.VMEM((ktotal, hwidth), bf16),
+            pltpu.VMEM((ktotal, LANES), bf16),
+        ],
+        compiler_params=params(),
+    )(expert_arr, *pieces, hiddens)
+    partial_sums, expert_arr = lax.optimization_barrier((partial_sums, expert_arr))
+    landed = lax.all_to_all(partial_sums, "x", split_axis=0, concat_axis=0, tiled=True)
+
+    depth = math.gcd(ny * span, width)
+    base = ny * span // depth
+    data_spec = pl.BlockSpec((ne * eighth, depth), lambda k: (0, base + k))
+    meta_spec = pl.BlockSpec((ne * eighth, LANES), lambda k: (0, (ny * span + width) // LANES))
     gate_grad, up_grad, dots, dense_gate_grad, dense_up_grad = pl.pallas_call(
         back_kernel,
         grid=(width // depth,),
         out_shape=(
             jax.ShapeDtypeStruct((1, slots, hwidth), bf16),
             jax.ShapeDtypeStruct((1, slots, hwidth), bf16),
-            jax.ShapeDtypeStruct((8, slots), jnp.float32),
+            jax.ShapeDtypeStruct((1, slots), jnp.float32),
             jax.ShapeDtypeStruct((ne * tokens, dwidth), bf16),
             jax.ShapeDtypeStruct((ne * tokens, dwidth), bf16),
         ),
@@ -288,7 +307,7 @@
         out_specs=(
             whole(1, slots, hwidth),
             whole(1, slots, hwidth),
-            whole(8, slots),
+            whole(1, slots),
             whole(ne * tokens, dwidth),
             whole(ne * tokens, dwidth),
         ),
@@ -299,8 +318,8 @@
         compiler_params=params(),
     )(
         expert_arr,
-        *row_pieces,
-        *row_pieces,
+        *pieces,
+        *pieces,
         expert_down,
         dense_down,
         expert_gate_pre,
@@ -309,31 +328,16 @@
         dense_up_pre,
     )
 
-    expert_arr, dots = lax.optimization_barrier((expert_arr, dots))
-    height = hwidth + -(-dwidth // 16) * 16
-    ktotal = ny * ne * tokens
-    partial_sums = pl.pallas_call(
-        functools.partial(weight_kernel, block),
-        out_shape=jax.ShapeDtypeStruct((nx, height, stride), bf16),
-        in_specs=[smem] + [vmem] * 7,
-        scratch_shapes=[
-            pltpu.VMEM((ktotal, nx * stride), bf16),
-            pltpu.VMEM((ktotal, hwidth), bf16),
-            pltpu.VMEM((ktotal, LANES), bf16),
-        ],
-        compiler_params=params(),
-    )(expert_arr, *chunk_pieces, hiddens)
-    partial_sums, dots = lax.optimization_barrier((partial_sums, dots))
-    landed = lax.all_to_all(partial_sums, "x", split_axis=0, concat_axis=0, tiled=True)
-    slot_prob_grad = lax.psum(dots[:1], ("l", "c"))
-    expert_down_grad, dense_down_grad = pl.pallas_call(
+    all_dots = lax.all_gather(dots, ("l", "c"), axis=0)
+    expert_down_grad, dense_down_grad, slot_prob_grad = pl.pallas_call(
         functools.partial(sum_kernel, 1.0 / (nx * ny)),
         out_shape=(
             jax.ShapeDtypeStruct((hwidth, block), bf16),
             jax.ShapeDtypeStruct((dwidth, block), bf16),
-        ),
-        compiler_params=params(),
-    )(landed)
+            jax.ShapeDtypeStruct((1, slots), jnp.float32),
+        ),
+        compiler_params=params(),
+    )(landed, all_dots)
     return (
         gate_grad,
         up_grad,

time: 143 us -> 141 us (0.986)
  starting transfers between devices: 49.4 us -> 33.8 us
  blocking collectives: 39.3 us -> 54.7 us
    all_to_all x0 -> x1, blocking collectives: none -> 15.7 us  [local(): cols = lax.all_to_all(cols, 'y', split_axis=0, concat_axis=0, tiled=True)]
    psum x1 -> x0, blocking collectives: 10.5 us -> none  [local(): slot_prob_grad = lax.psum(dots[:1], ('l', 'c'))]
    all_gather x1 -> x2, blocking collectives: 28.9 us -> 39 us  [the longest x1 32 us: local(): packed = lax.all_gather(packed, 'e', axis=0, tiled=True)]
    ppermute x10 -> x5, starting transfers between devices: 38.2 us -> 28.6 us  [the longest x3 18.9 us: local(): pieces += [lax.ppermute(p, 'c', ring(CORES, 1)) for p in pieces]]
    all_to_all x1 -> x0, starting transfers between devices: 7.13 us -> none  [local(): lax.all_to_all(chunks, 'y', split_axis=0, concat_axis=0, tiled=True)]
    ppermute x10 -> x5, waiting for transfers between devices: 4.67 us -> 10.4 us  [the longest x2 10.1 us: local(): lax.ppermute(packed, ('e', 'l'), ring(ne * RUN, d))]
    all_to_all x1, waiting for transfers between devices: 4.11 us -> 0.01 us  [local(): lax.all_to_all(partial_sums, 'x', split_axis=0, concat_axis=0, tiled=True)]
    all_to_all x1 -> x0, waiting for transfers between devices: 1.88 us -> none  [local(): lax.all_to_all(chunks, 'y', split_axis=0, concat_axis=0, tiled=True)]
  transfers between devices with their start and end apart: 13 -> 7, of which waited for: 3 -> 3; matrix products, arithmetic and copies ran while one was open for 1% -> 0% of each run, Pallas kernels for 10% -> 10%
where the time goes in v3:
time: 141 us; the launch traced here: 140 us
  blocking collectives  54.7 us (39%)
  starting transfers between devices  33.8 us (24%)
  Pallas kernels  24.4 us (17%)
  between operations  14.1 us (10%)
  waiting for transfers between devices  10.5 us (7%)
  local copies, waits for them, and re-layouts  3 us (2%)
    all_gather x1, blocking collectives, local(): packed = lax.all_gather(packed, 'e', axis=0, tiled=True)  32 us
    ppermute x3, starting transfers between devices, local(): pieces += [lax.ppermute(p, 'c', ring(CORES, 1)) for p in pieces]  18.9 us
    all_to_all x1, blocking collectives, local(): cols = lax.all_to_all(cols, 'y', split_axis=0, concat_axis=0, tiled=True)  15.7 us
    ppermute x2, waiting for transfers between devices, local(): lax.ppermute(packed, ('e', 'l'), ring(ne * RUN, d))  10.1 us
    pallas_call x1, Pallas kernels, local(): pl.pallas_call(back_kernel, grid=(width // depth,), out_shape=(jax.ShapeD...  10 us
    ppermute x2, starting transfers between devices, local(): lax.ppermute(packed, ('e', 'l'), ring(ne * RUN, d))  9.72 us
    all_gather x1, blocking collectives, local(): all_dots = lax.all_gather(dots, ('l', 'c'), axis=0)  7.06 us
    pallas_call x1, Pallas kernels, local(): pl.pallas_call(functools.partial(weight_kernel, block, ny), grid=(1,), ou...  6.76 us
  transfers between devices with their start and end apart: 7, of which 3 were waited for; matrix products, arithmetic and copies ran while one was open for 0% of the time, Pallas kernels for 10%

profile of v3, /device:TPU:1, one launch (start us, length us, event | category | flops | bytes accessed | tf_op | source)
XLA Modules:
  0.0 140.5 jit_solution(2752455438197831469)
XLA Ops:
  7.2 0.0 all-gather.5.cloned.1.call-start
  7.2 1.8 %shard_map.155 = bf16[208,512]{1,0:T(8,128)(2,1)} custom-call(bf16[1,156,416]{2,1,0:T(8,128)(2,1)} %refs_14_.1, bf16[1,156,416]{2,1,0:T(8,128)(2,1)} %refs_15_.1, bf16[192,104]{1,0:T(8,128)(2,1)} %refs_16_.1, bf16[192,104]{1,0:T(8,128)(2,1)} %refs_17_.1), custom_call_target="tpu_custom_call" | custom-call | tf_op jit(solution)/shard_map/pallas_call | solution.py:234
  9.0 0.0 all-gather.5.cloned.1.call-update
  9.0 2.1 %shard_map.153 = (bf16[8,7296]{1,0:T(8,128)(2,1)}, bf16[8,8,1024]{2,1,0:T(8,128)(2,1)}) custom-call(s32[1]{0:T(128)} %bitcast.expert_ref, s32[1]{0:T(128)} %bitcast.1.part_ref, bf16[48,7168]{1,0:T(8,128)(2,1)} %rows_ref.1, bf16[2,48]{1,0:T(2,128)(2,1)} %bitcast.15, s32[2,48]{1,0:T(2,128)} %bitcast.12, s32[2,48]{1,0:T(2,128)} %bitcast.13), custom_call_target="tpu_custom_call" | custom-call | tf_op jit(solution)/shard_map/pallas_call | solution.py:243
  11.1 15.7 %all_to_all.10.cols_ref = bf16[8,8,1024]{2,1,0:T(8,128)(2,1)} all-to-all(bf16[8,8,1024]{2,1,0:T(8,128)(2,1)} %get-tuple-element.19), channel_id=1, replica_groups=mesh['x'=4,'y'=8,'e'=4,'l'=3,'c'=2] {'y'}, dimensions={0} | all-to-all | bytes 262144 | tf_op jit(solution)/shard_map/all_to_all | solution.py:252
  26.8 1.7 %shard_map.154 = bf16[8,15488]{1,0:T(8,128)(2,1)} custom-call(bf16[8,8,1024]{2,1,0:T(8,128)(2,1)} %all_to_all.10.cols_ref, bf16[8,7296]{1,0:T(8,128)(2,1)} %get-tuple-element.20.rows_ref), custom_call_target="tpu_custom_call" | custom-call | tf_op jit(solution)/shard_map/pallas_call | solution.py:253
  28.5 32.0 %all_gather.15.refs_0_.refs_6_ = bf16[32,15488]{1,0:T(8,128)(2,1)S(1)} all-gather(bf16[8,15488]{1,0:T(8,128)(2,1)} %shard_map.154), channel_id=1, replica_groups=mesh['x'=4,'y'=8,'e'=4,'l'=3,'c'=2] {'e'}, dimensions={0}, use_global_device_ids=true | all-gather | bytes 1239040 | tf_op jit(solution)/shard_map/all_gather | solution.py:258
  60.4 0.0 copy-start
  60.4 7.8 %collective-permute-start.1 = (bf16[32,15488]{1,0:T(8,128)(2,1)S(1)}, bf16[32,15488]{1,0:T(8,128)(2,1)S(1)}, u32[]{:S(2)}, u32[]{:S(2)}) collective-permute-start(bf16[32,15488]{1,0:T(8,128)(2,1)S(1)} %all_gather.15.refs_0_.refs_6_), channel_id=1, source_target_pairs={{0,22},{2,0},{4,2},{6,4},{8,6},{10,8},{12,10},{14,12},{16,14},{18,... | collective-permute-start | bytes 2973704 | tf_op jit(solution)/shard_map/ppermute | solution.py:259
  68.2 1.9 %collective-permute-start = (bf16[32,15488]{1,0:T(8,128)(2,1)S(1)}, bf16[32,15488]{1,0:T(8,128)(2,1)S(1)}, u32[]{:S(2)}, u32[]{:S(2)}) collective-permute-start(bf16[32,15488]{1,0:T(8,128)(2,1)S(1)} %all_gather.15.refs_0_.refs_6_), channel_id=1, source_target_pairs={{0,2},{2,4},{4,6},{6,8},{8,10},{10,12},{12,14},{14,16},{16,18},{18... | collective-permute-start | bytes 2973704 | tf_op jit(solution)/shard_map/ppermute | solution.py:259
  70.2 7.6 %collective-permute-start.2 = (bf16[32,15488]{1,0:T(8,128)(2,1)S(1)}, bf16[32,15488]{1,0:T(8,128)(2,1)S(1)}, u32[]{:S(2)}, u32[]{:S(2)}) collective-permute-start(bf16[32,15488]{1,0:T(8,128)(2,1)S(1)} %all_gather.15.refs_0_.refs_6_), channel_id=1, source_target_pairs={{0,1},{1,0},{2,3},{3,2},{4,5},{5,4},{6,7},{7,6},{8,9},{9,8},{10,11... | collective-permute-start | bytes 2973704 | tf_op jit(solution)/shard_map/ppermute | solution.py:260
  77.8 8.4 %collective-permute-done.1.refs_2_.refs_8_ = bf16[32,15488]{1,0:T(8,128)(2,1)S(1)} collective-permute-done((bf16[32,15488]{1,0:T(8,128)(2,1)S(1)}, bf16[32,15488]{1,0:T(8,128)(2,1)S(1)}, u32[]{:S(2)}, u32[]{:S(2)}) %collective-permute-start.1) | collective-permute-done | bytes 991264 | tf_op jit(solution)/shard_map/ppermute | solution.py:259
  86.1 0.0 copy-start.1
  86.2 6.6 %collective-permute-start.4 = (bf16[32,15488]{1,0:T(8,128)(2,1)S(1)}, bf16[32,15488]{1,0:T(8,128)(2,1)S(1)}, u32[]{:S(2)}, u32[]{:S(2)}) collective-permute-start(bf16[32,15488]{1,0:T(8,128)(2,1)S(1)} %collective-permute-done.1.refs_2_.refs_8_), channel_id=1, source_target_pairs={{0,1},{1,0},{2,3},{3,2},{4,5},{5,4},{6,7},{7,6},{8,9},{9,8},{10,11... | collective-permute-start | bytes 2973704 | tf_op jit(solution)/shard_map/ppermute | solution.py:260
  92.7 1.8 %collective-permute-done.refs_1_.refs_7_ = bf16[32,15488]{1,0:T(8,128)(2,1)S(1)} collective-permute-done((bf16[32,15488]{1,0:T(8,128)(2,1)S(1)}, bf16[32,15488]{1,0:T(8,128)(2,1)S(1)}, u32[]{:S(2)}, u32[]{:S(2)}) %collective-permute-start) | collective-permute-done | bytes 991264 | tf_op jit(solution)/shard_map/ppermute | solution.py:259
  94.5 0.0 copy-start.2
  94.5 4.8 %collective-permute-start.3 = (bf16[32,15488]{1,0:T(8,128)(2,1)S(1)}, bf16[32,15488]{1,0:T(8,128)(2,1)}, u32[]{:S(2)}, u32[]{:S(2)}) collective-permute-start(bf16[32,15488]{1,0:T(8,128)(2,1)S(1)} %collective-permute-done.refs_1_.refs_7_), channel_id=1, source_target_pairs={{0,1},{1,0},{2,3},{3,2},{4,5},{5,4},{6,7},{7,6},{8,9},{9,8},{10,11... | collective-permute-start | bytes 2973704 | tf_op jit(solution)/shard_map/ppermute | solution.py:260
  99.2 0.0 collective-permute-done.2.refs_3_.refs_9_
  99.3 0.0 copy-start.3
  99.3 0.0 collective-permute-done.4.refs_5_.refs_11_
  99.3 0.9 copy-done.3
  100.2 0.0 copy-start.4
  100.2 1.1 copy-done.4
  101.3 0.3 collective-permute-done.3.refs_4_.refs_10_
  101.6 0.0 all-gather.5.cloned.1.call-done
  101.6 0.0 copy-done
  101.6 0.0 copy-done.1
  101.6 0.0 copy-done.2
  101.6 6.8 %shard_map.156 = bf16[4,528,256]{2,1,0:T(8,128)(2,1)} custom-call(s32[1]{0:T(128)} %bitcast.expert_ref, bf16[32,15488]{1,0:T(8,128)(2,1)} %copy-done, bf16[32,15488]{1,0:T(8,128)(2,1)} %copy-done.2, bf16[32,15488]{1,0:T(8,128)(2,1)} %copy-done.1, bf16[32,15488]{1,0:T(8,128)(2,1)} %copy-done.3, bf16[32,15488]{1,0:T(8,128)(2,1)} %collective-permute-done.3.refs_4_.refs_10_, ...), custom_call_target="tpu_custom_call" | custom-call | tf_op jit(solution)/shard_map/pallas_call | solution.py:264
  108.3 5.2 %all-to-all-start.1 = ((bf16[4,528,256]{2,1,0:T(8,128)(2,1)}), bf16[4,528,256]{2,1,0:T(8,128)(2,1)S(1)}, u32[]{:S(2)}, u32[]{:S(2)}) async-start(bf16[4,528,256]{2,1,0:T(8,128)(2,1)} %shard_map.156), calls=%async_computation.1 | async-start | bytes 2162688 | tf_op jit(solution)/shard_map/all_to_all | solution.py:280
  113.5 10.0 %shard_map.157 = (bf16[1,156,416]{2,1,0:T(8,128)(2,1)}, bf16[1,156,416]{2,1,0:T(8,128)(2,1)}, f32[1,156]{1,0:T(1,128)}, bf16[192,104]{1,0:T(8,128)(2,1)}, bf16[192,104]{1,0:T(8,128)(2,1)}) custom-call(s32[1]{0:T(128)} %bitcast.expert_ref, bf16[32,15488]{1,0:T(8,128)(2,1)} %copy-done, bf16[32,15488]{1,0:T(8,128)(2,1)} %copy-done.2, ...), custom_call_target="tpu_custom_call" | custom-call | tf_op jit(solution)/shard_map/pallas_call | solution.py:286
  123.5 7.1 %all-gather.2.dots_ref = f32[6,1,156]{2,1,0:T(1,128)} all-gather(f32[1,1,156]{2,1,0:T(1,128)} %bitcast.14), channel_id=3, replica_groups=mesh['x'=4,'y'=8,'e'=4,'l'=3,'c'=2] {'l','c'}, dimensions={0}, use_global_device_ids=true | all-gather | bytes 4368 | tf_op jit(solution)/shard_map/all_gather | solution.py:331
  130.6 0.0 all-to-all-done.1.in_ref
  130.6 0.0 copy-start.5
  130.6 1.0 copy-done.5
  131.6 2.1 %shard_map.158 = (bf16[416,224]{1,0:T(8,128)(2,1)}, bf16[104,224]{1,0:T(8,128)(2,1)}, f32[1,156]{1,0:T(1,128)}) custom-call(bf16[4,528,256]{2,1,0:T(8,128)(2,1)} %copy-done.5, f32[6,1,156]{2,1,0:T(1,128)} %all-gather.2.dots_ref), custom_call_target="tpu_custom_call" | custom-call | tf_op jit(solution)/shard_map/pallas_call | solution.py:332
Async XLA Ops:
  7.2 94.4 %all-gather.5.cloned.1.call-start = ((), (), s32[]{:S(2)}) async-start(), calls=%async_computation.2 | async-start | bytes 1916928 | tf_op jit(solution)/shard_map/all_gather | solution.py:239
  60.4 41.1 %copy-start = (bf16[32,15488]{1,0:T(8,128)(2,1)}, bf16[32,15488]{1,0:T(8,128)(2,1)S(1)}, u32[]{:S(2)}) copy-start(bf16[32,15488]{1,0:T(8,128)(2,1)S(1)} %all_gather.15.refs_0_.refs_6_) | copy-start | bytes 2973700
  60.4 25.7 %collective-permute-start.1 = (bf16[32,15488]{1,0:T(8,128)(2,1)S(1)}, bf16[32,15488]{1,0:T(8,128)(2,1)S(1)}, u32[]{:S(2)}, u32[]{:S(2)}) collective-permute-start(bf16[32,15488]{1,0:T(8,128)(2,1)S(1)} %all_gather.15.refs_0_.refs_6_), channel_id=1, source_target_pairs={{0,22},{2,0},{4,2},{6,4},{8,6},{10,8},{12,10},{14,12},{16,14},{18,... | collective-permute-start | bytes 2973704 | tf_op jit(solution)/shard_map/ppermute | solution.py:259
  68.2 26.2 %collective-permute-start = (bf16[32,15488]{1,0:T(8,128)(2,1)S(1)}, bf16[32,15488]{1,0:T(8,128)(2,1)S(1)}, u32[]{:S(2)}, u32[]{:S(2)}) collective-permute-start(bf16[32,15488]{1,0:T(8,128)(2,1)S(1)} %all_gather.15.refs_0_.refs_6_), channel_id=1, source_target_pairs={{0,2},{2,4},{4,6},{6,8},{8,10},{10,12},{12,14},{14,16},{16,18},{18... | collective-permute-start | bytes 2973704 | tf_op jit(solution)/shard_map/ppermute | solution.py:259
  70.2 29.1 %collective-permute-start.2 = (bf16[32,15488]{1,0:T(8,128)(2,1)S(1)}, bf16[32,15488]{1,0:T(8,128)(2,1)S(1)}, u32[]{:S(2)}, u32[]{:S(2)}) collective-permute-start(bf16[32,15488]{1,0:T(8,128)(2,1)S(1)} %all_gather.15.refs_0_.refs_6_), channel_id=1, source_target_pairs={{0,1},{1,0},{2,3},{3,2},{4,5},{5,4},{6,7},{7,6},{8,9},{9,8},{10,11... | collective-permute-start | bytes 2973704 | tf_op jit(solution)/shard_map/ppermute | solution.py:260
  86.1 15.4 %copy-start.1 = (bf16[32,15488]{1,0:T(8,128)(2,1)}, bf16[32,15488]{1,0:T(8,128)(2,1)S(1)}, u32[]{:S(2)}) copy-start(bf16[32,15488]{1,0:T(8,128)(2,1)S(1)} %collective-permute-done.1.refs_2_.refs_8_) | copy-start | bytes 2973700
  86.2 13.1 %collective-permute-start.4 = (bf16[32,15488]{1,0:T(8,128)(2,1)S(1)}, bf16[32,15488]{1,0:T(8,128)(2,1)S(1)}, u32[]{:S(2)}, u32[]{:S(2)}) collective-permute-start(bf16[32,15488]{1,0:T(8,128)(2,1)S(1)} %collective-permute-done.1.refs_2_.refs_8_), channel_id=1, source_target_pairs={{0,1},{1,0},{2,3},{3,2},{4,5},{5,4},{6,7},{7,6},{8,9},{9,8},{10,11... | collective-permute-start | bytes 2973704 | tf_op jit(solution)/shard_map/ppermute | solution.py:260
  94.5 7.1 %copy-start.2 = (bf16[32,15488]{1,0:T(8,128)(2,1)}, bf16[32,15488]{1,0:T(8,128)(2,1)S(1)}, u32[]{:S(2)}) copy-start(bf16[32,15488]{1,0:T(8,128)(2,1)S(1)} %collective-permute-done.refs_1_.refs_7_) | copy-start | bytes 2973700
  94.5 7.1 %collective-permute-start.3 = (bf16[32,15488]{1,0:T(8,128)(2,1)S(1)}, bf16[32,15488]{1,0:T(8,128)(2,1)}, u32[]{:S(2)}, u32[]{:S(2)}) collective-permute-start(bf16[32,15488]{1,0:T(8,128)(2,1)S(1)} %collective-permute-done.refs_1_.refs_7_), channel_id=1, source_target_pairs={{0,1},{1,0},{2,3},{3,2},{4,5},{5,4},{6,7},{7,6},{8,9},{9,8},{10,11... | collective-permute-start | bytes 2973704 | tf_op jit(solution)/shard_map/ppermute | solution.py:260
  99.3 1.0 copy-start.3
  100.2 1.1 copy-start.4
  108.3 22.2 %all-to-all-start.1 = ((bf16[4,528,256]{2,1,0:T(8,128)(2,1)}), bf16[4,528,256]{2,1,0:T(8,128)(2,1)S(1)}, u32[]{:S(2)}, u32[]{:S(2)}) async-start(bf16[4,528,256]{2,1,0:T(8,128)(2,1)} %shard_map.156), calls=%async_computation.1 | async-start | bytes 2162688 | tf_op jit(solution)/shard_map/all_to_all | solution.py:280
  130.6 1.0 copy-start.5
Sparse Core Ops, SparseCore 0:
  10.9 49.2 all-gather.4

commit v4 on v2

--- a/solution.py
+++ b/solution.py
@@ -1,4 +1,5 @@
 import functools
+import math
 
 import jax
 import jax.numpy as jnp
@@ -48,8 +49,8 @@
         ]
 
 
-def pick_kernel(capacity, at_ref, rows_ref, prob_ref, ids_ref, slots_ref, out_ref):
-    expert, part = at_ref[0], at_ref[1]
+def pick_kernel(capacity, expert_ref, part_ref, rows_ref, prob_ref, ids_ref, slots_ref, out_ref):
+    expert, part = expert_ref[0], part_ref[0]
     eighth = out_ref.shape[0]
     tokens, width = rows_ref.shape
     lane = lax.broadcasted_iota(jnp.int32, (eighth, tokens), 1)
@@ -130,7 +131,8 @@
         out_ref[x, width:, :] = dsummed[: height - width, x * stride : (x + 1) * stride]
 
 
-def sum_kernel(scale, in_ref, expert_ref, dense_ref):
+def sum_kernel(scale, in_ref, dots_ref, expert_ref, dense_ref, dots_out):
+    dots_out[...] = jnp.sum(dots_ref[...], axis=0)
     summed = in_ref[0].astype(jnp.float32)
     for x in range(1, in_ref.shape[0]):
         summed = summed + in_ref[x].astype(jnp.float32)
@@ -184,7 +186,7 @@
             (((1,), (1,)), ((), ())),
             precision=lax.Precision.HIGHEST,
             preferred_element_type=jnp.float32,
-        )
+        )[:1]
         scaled = slot_prob * back
         gate_out[0] = (scaled * up_val * slope).astype(jnp.bfloat16)
         up_out[0] = (scaled * activated).astype(jnp.bfloat16)
@@ -231,18 +233,13 @@
     )(expert_gate_pre, expert_up_pre, dense_gate_pre, dense_up_pre)
     hiddens = lax.all_gather(hidden, "y", axis=0)
 
+    part_arr = part.reshape(1).astype(jnp.int32)
     mine = pl.pallas_call(
         functools.partial(pick_kernel, capacity),
         out_shape=jax.ShapeDtypeStruct((eighth, width + LANES), bf16),
-        in_specs=[smem] + [vmem] * 4,
-        compiler_params=params(),
-    )(
-        jnp.stack([expert, part]).astype(jnp.int32),
-        grad_out,
-        gate_prob.T,
-        expert_ids.T,
-        slot_positions.T,
-    )
+        in_specs=[smem] * 2 + [vmem] * 4,
+        compiler_params=params(),
+    )(expert_arr, part_arr, grad_out, gate_prob.T, expert_ids.T, slot_positions.T)
     rows = lax.all_gather(mine, "e", axis=0, tiled=True)
 
     chunks = pl.pallas_call(
@@ -250,6 +247,7 @@
         out_shape=jax.ShapeDtypeStruct((ny, ne * eighth, nx * stride), bf16),
         compiler_params=params(),
     )(rows)
+    rows, chunks = lax.optimization_barrier((rows, chunks))
     chunks = lax.all_to_all(chunks, "y", split_axis=0, concat_axis=0, tiled=True)
 
     def spread(piece):
@@ -261,7 +259,23 @@
     chunks, *row_pieces = lax.optimization_barrier((chunks, *row_pieces))
     chunk_pieces = spread(chunks)
 
-    depth = 1024
+    height = hwidth + -(-dwidth // 16) * 16
+    ktotal = ny * ne * tokens
+    partial_sums = pl.pallas_call(
+        functools.partial(weight_kernel, block),
+        out_shape=jax.ShapeDtypeStruct((nx, height, stride), bf16),
+        in_specs=[smem] + [vmem] * 7,
+        scratch_shapes=[
+            pltpu.VMEM((ktotal, nx * stride), bf16),
+            pltpu.VMEM((ktotal, hwidth), bf16),
+            pltpu.VMEM((ktotal, LANES), bf16),
+        ],
+        compiler_params=params(),
+    )(expert_arr, *chunk_pieces, hiddens)
+    partial_sums, expert_arr = lax.optimization_barrier((partial_sums, expert_arr))
+    landed = lax.all_to_all(partial_sums, "x", split_axis=0, concat_axis=0, tiled=True)
+
+    depth = math.gcd(1024, width)
     data_spec = pl.BlockSpec((ne * eighth, depth), lambda k: (0, k))
     meta_spec = pl.BlockSpec((ne * eighth, LANES), lambda k: (0, width // LANES))
     gate_grad, up_grad, dots, dense_gate_grad, dense_up_grad = pl.pallas_call(
@@ -270,7 +284,7 @@
         out_shape=(
             jax.ShapeDtypeStruct((1, slots, hwidth), bf16),
             jax.ShapeDtypeStruct((1, slots, hwidth), bf16),
-            jax.ShapeDtypeStruct((8, slots), jnp.float32),
+            jax.ShapeDtypeStruct((1, slots), jnp.float32),
             jax.ShapeDtypeStruct((ne * tokens, dwidth), bf16),
             jax.ShapeDtypeStruct((ne * tokens, dwidth), bf16),
         ),
@@ -288,7 +302,7 @@
         out_specs=(
             whole(1, slots, hwidth),
             whole(1, slots, hwidth),
-            whole(8, slots),
+            whole(1, slots),
             whole(ne * tokens, dwidth),
             whole(ne * tokens, dwidth),
         ),
@@ -309,31 +323,16 @@
         dense_up_pre,
     )
 
-    expert_arr, dots = lax.optimization_barrier((expert_arr, dots))
-    height = hwidth + -(-dwidth // 16) * 16
-    ktotal = ny * ne * tokens
-    partial_sums = pl.pallas_call(
-        functools.partial(weight_kernel, block),
-        out_shape=jax.ShapeDtypeStruct((nx, height, stride), bf16),
-        in_specs=[smem] + [vmem] * 7,
-        scratch_shapes=[
-            pltpu.VMEM((ktotal, nx * stride), bf16),
-            pltpu.VMEM((ktotal, hwidth), bf16),
-            pltpu.VMEM((ktotal, LANES), bf16),
-        ],
-        compiler_params=params(),
-    )(expert_arr, *chunk_pieces, hiddens)
-    partial_sums, dots = lax.optimization_barrier((partial_sums, dots))
-    landed = lax.all_to_all(partial_sums, "x", split_axis=0, concat_axis=0, tiled=True)
-    slot_prob_grad = lax.psum(dots[:1], ("l", "c"))
-    expert_down_grad, dense_down_grad = pl.pallas_call(
+    all_dots = lax.all_gather(dots, ("l", "c"), axis=0)
+    expert_down_grad, dense_down_grad, slot_prob_grad = pl.pallas_call(
         functools.partial(sum_kernel, 1.0 / (nx * ny)),
         out_shape=(
             jax.ShapeDtypeStruct((hwidth, block), bf16),
             jax.ShapeDtypeStruct((dwidth, block), bf16),
-        ),
-        compiler_params=params(),
-    )(landed)
+            jax.ShapeDtypeStruct((1, slots), jnp.float32),
+        ),
+        compiler_params=params(),
+    )(landed, all_dots)
     return (
         gate_grad,
         up_grad,

time: 143 us -> 140 us (0.979)
  blocking collectives: 39.3 us -> 35.6 us
  waiting for transfers between devices: 10.7 us -> 13.3 us
    psum x1 -> x0, blocking collectives: 10.5 us -> none  [local(): slot_prob_grad = lax.psum(dots[:1], ('l', 'c'))]
    all_gather x0 -> x1, blocking collectives: none -> 7.06 us  [local(): all_dots = lax.all_gather(dots, ('l', 'c'), axis=0)]
    all_to_all x1, waiting for transfers between devices: 1.88 us -> 7.23 us  [local(): lax.all_to_all(chunks, 'y', split_axis=0, concat_axis=0, tiled=True)]
    all_to_all x1, waiting for transfers between devices: 4.11 us -> 0.01 us  [local(): lax.all_to_all(partial_sums, 'x', split_axis=0, concat_axis=0, tiled=True)]
  transfers between devices with their start and end apart: 13 -> 13, of which waited for: 3 -> 5; matrix products, arithmetic and copies ran while one was open for 1% -> 0% of each run, Pallas kernels for 10% -> 10%
where the time goes in v4:
time: 140 us; the launch traced here: 139 us
  starting transfers between devices  48.7 us (35%)
  blocking collectives  35.6 us (25%)
  Pallas kernels  24.9 us (18%)
  between operations  14.2 us (10%)
  waiting for transfers between devices  13.3 us (10%)
  local copies, waits for them, and re-layouts  2.57 us (2%)
    all_gather x1, blocking collectives, local(): rows = lax.all_gather(mine, 'e', axis=0, tiled=True)  28.5 us
    ppermute x6, starting transfers between devices, spread(): other = [lax.ppermute(p, 'c', ring(CORES, 1)) for p in along]  20.9 us
    ppermute x4, starting transfers between devices, spread(): lax.ppermute(piece, ('e', 'l'), ring(ne * RUN, d))  17 us
    pallas_call x1, Pallas kernels, local(): pl.pallas_call(back_kernel, grid=(width // depth,), out_shape=(jax.ShapeD...  10 us
    all_to_all x1, waiting for transfers between devices, local(): lax.all_to_all(chunks, 'y', split_axis=0, concat_axis=0, tiled=True)  7.23 us
    all_gather x1, blocking collectives, local(): all_dots = lax.all_gather(dots, ('l', 'c'), axis=0)  7.06 us
    all_to_all x1, starting transfers between devices, local(): lax.all_to_all(chunks, 'y', split_axis=0, concat_axis=0, tiled=True)  6.83 us
    pallas_call x1, Pallas kernels, local(): pl.pallas_call(functools.partial(weight_kernel, block), out_shape=jax.Sha...  6.77 us
  transfers between devices with their start and end apart: 13, of which 5 were waited for; matrix products, arithmetic and copies ran while one was open for 0% of the time, Pallas kernels for 10%

profile of v4, /device:TPU:1, one launch (start us, length us, event | category | flops | bytes accessed | tf_op | source)
XLA Modules:
  0.0 139.3 jit_solution(9201611601698345507)
XLA Ops:
  7.2 0.0 all-gather.5.cloned.1.call-start
  7.2 1.8 %shard_map.155 = bf16[208,512]{1,0:T(8,128)(2,1)} custom-call(bf16[1,156,416]{2,1,0:T(8,128)(2,1)} %refs_14_.1, bf16[1,156,416]{2,1,0:T(8,128)(2,1)} %refs_15_.1, bf16[192,104]{1,0:T(8,128)(2,1)} %refs_16_.1, bf16[192,104]{1,0:T(8,128)(2,1)} %refs_17_.1), custom_call_target="tpu_custom_call" | custom-call | tf_op jit(solution)/shard_map/pallas_call | solution.py:229
  9.0 0.0 all-gather.5.cloned.1.call-update
  9.0 2.0 %shard_map.153 = bf16[8,7296]{1,0:T(8,128)(2,1)} custom-call(s32[1]{0:T(128)} %bitcast.expert_ref, s32[1]{0:T(128)} %bitcast.1.part_ref, bf16[48,7168]{1,0:T(8,128)(2,1)} %rows_ref.1, bf16[2,48]{1,0:T(2,128)(2,1)} %bitcast.15, s32[2,48]{1,0:T(2,128)} %bitcast.12, s32[2,48]{1,0:T(2,128)} %bitcast.13), custom_call_target="tpu_custom_call" | custom-call | tf_op jit(solution)/shard_map/pallas_call | solution.py:237
  11.0 28.5 %all_gather.15.rows_ref.refs_0_.refs_6_ = bf16[32,7296]{1,0:T(8,128)(2,1)} all-gather(bf16[8,7296]{1,0:T(8,128)(2,1)} %shard_map.153), channel_id=1, replica_groups=mesh['x'=4,'y'=8,'e'=4,'l'=3,'c'=2] {'e'}, dimensions={0}, use_global_device_ids=true | all-gather | bytes 583680 | tf_op jit(solution)/shard_map/all_gather | solution.py:243
  39.5 0.0 copy-start
  39.5 2.3 %shard_map.154 = bf16[8,32,1024]{2,1,0:T(8,128)(2,1)} custom-call(bf16[32,7296]{1,0:T(8,128)(2,1)} %all_gather.15.rows_ref.refs_0_.refs_6_), custom_call_target="tpu_custom_call" | custom-call | tf_op jit(solution)/shard_map/pallas_call | solution.py:245
  41.8 7.4 %collective-permute-start.1 = (bf16[32,7296]{1,0:T(8,128)(2,1)}, bf16[32,7296]{1,0:T(8,128)(2,1)S(1)}, u32[]{:S(2)}, u32[]{:S(2)}) collective-permute-start(bf16[32,7296]{1,0:T(8,128)(2,1)} %all_gather.15.rows_ref.refs_0_.refs_6_), channel_id=1, source_target_pairs={{0,22},{2,0},{4,2},{6,4},{8,6},{10,8},{12,10},{14,12},{16,14},{18,... | collective-permute-start | bytes 1400840 | tf_op jit(solution)/shard_map/ppermute | solution.py:254
  49.2 1.9 %collective-permute-start = (bf16[32,7296]{1,0:T(8,128)(2,1)}, bf16[32,7296]{1,0:T(8,128)(2,1)S(1)}, u32[]{:S(2)}, u32[]{:S(2)}) collective-permute-start(bf16[32,7296]{1,0:T(8,128)(2,1)} %all_gather.15.rows_ref.refs_0_.refs_6_), channel_id=1, source_target_pairs={{0,2},{2,4},{4,6},{6,8},{8,10},{10,12},{12,14},{14,16},{16,18},{18... | collective-permute-start | bytes 1400840 | tf_op jit(solution)/shard_map/ppermute | solution.py:254
  51.1 6.8 %all-to-all-start = ((bf16[8,32,1024]{2,1,0:T(8,128)(2,1)}), bf16[8,32,1024]{2,1,0:T(8,128)(2,1)S(1)}, u32[]{:S(2)}, u32[]{:S(2)}) async-start(bf16[8,32,1024]{2,1,0:T(8,128)(2,1)} %shard_map.154), calls=%async_computation | async-start | bytes 1048576 | tf_op jit(solution)/shard_map/all_to_all | solution.py:251
  57.9 0.0 copy-done
  57.9 3.2 %collective-permute-start.2 = (bf16[32,7296]{1,0:T(8,128)(2,1)S(1)}, bf16[32,7296]{1,0:T(8,128)(2,1)S(1)}, u32[]{:S(2)}, u32[]{:S(2)}) collective-permute-start(bf16[32,7296]{1,0:T(8,128)(2,1)S(1)} %copy-done), channel_id=1, source_target_pairs={{0,1},{1,0},{2,3},{3,2},{4,5},{5,4},{6,7},{7,6},{8,9},{9,8},{10,11... | collective-permute-start | bytes 1400840 | tf_op jit(solution)/shard_map/ppermute | solution.py:255
  61.2 0.0 collective-permute-done.1.refs_2_.refs_8_
  61.2 0.0 copy-start.3
  61.2 1.9 %collective-permute-start.4 = (bf16[32,7296]{1,0:T(8,128)(2,1)S(1)}, bf16[32,7296]{1,0:T(8,128)(2,1)S(1)}, u32[]{:S(2)}, u32[]{:S(2)}) collective-permute-start(bf16[32,7296]{1,0:T(8,128)(2,1)S(1)} %collective-permute-done.1.refs_2_.refs_8_), channel_id=1, source_target_pairs={{0,1},{1,0},{2,3},{3,2},{4,5},{5,4},{6,7},{7,6},{8,9},{9,8},{10,11... | collective-permute-start | bytes 1400840 | tf_op jit(solution)/shard_map/ppermute | solution.py:255
  63.1 0.6 collective-permute-done.refs_1_.refs_7_
  63.7 0.0 copy-start.4
  63.7 3.8 %collective-permute-start.3 = (bf16[32,7296]{1,0:T(8,128)(2,1)S(1)}, bf16[32,7296]{1,0:T(8,128)(2,1)S(1)}, u32[]{:S(2)}, u32[]{:S(2)}) collective-permute-start(bf16[32,7296]{1,0:T(8,128)(2,1)S(1)} %collective-permute-done.refs_1_.refs_7_), channel_id=1, source_target_pairs={{0,1},{1,0},{2,3},{3,2},{4,5},{5,4},{6,7},{7,6},{8,9},{9,8},{10,11... | collective-permute-start | bytes 1400840 | tf_op jit(solution)/shard_map/ppermute | solution.py:255
  67.5 0.0 collective-permute-done.2.refs_3_.refs_9_
  67.5 0.0 copy-start.5
  67.5 7.2 %all-to-all-done.refs_0_ = bf16[8,32,1024]{2,1,0:T(8,128)(2,1)S(1)} async-done(((bf16[8,32,1024]{2,1,0:T(8,128)(2,1)}), bf16[8,32,1024]{2,1,0:T(8,128)(2,1)S(1)}, u32[]{:S(2)}, u32[]{:S(2)}) %all-to-all-start) | async-done | bytes 524320 | tf_op jit(solution)/shard_map/all_to_all | solution.py:251
  74.7 0.0 copy-start.2
  74.7 0.0 collective-permute-done.4.refs_5_.refs_11_
  74.8 0.0 copy-start.6
  74.8 0.0 collective-permute-done.3.refs_4_.refs_10_
  74.8 0.0 copy-start.7
  74.8 5.8 %collective-permute-start.6 = (bf16[8,32,1024]{2,1,0:T(8,128)(2,1)S(1)}, bf16[8,32,1024]{2,1,0:T(8,128)(2,1)S(1)}, u32[]{:S(2)}, u32[]{:S(2)}) collective-permute-start(bf16[8,32,1024]{2,1,0:T(8,128)(2,1)S(1)} %all-to-all-done.refs_0_), channel_id=1, source_target_pairs={{0,22},{2,0},{4,2},{6,4},{8,6},{10,8},{12,10},{14,12},{16,14},{18,... | collective-permute-start | bytes 1572872 | tf_op jit(solution)/shard_map/ppermute | solution.py:254
  80.5 1.9 %collective-permute-start.5 = (bf16[8,32,1024]{2,1,0:T(8,128)(2,1)S(1)}, bf16[8,32,1024]{2,1,0:T(8,128)(2,1)S(1)}, u32[]{:S(2)}, u32[]{:S(2)}) collective-permute-start(bf16[8,32,1024]{2,1,0:T(8,128)(2,1)S(1)} %all-to-all-done.refs_0_), channel_id=1, source_target_pairs={{0,2},{2,4},{4,6},{6,8},{8,10},{10,12},{12,14},{14,16},{16,18},{18... | collective-permute-start | bytes 1572872 | tf_op jit(solution)/shard_map/ppermute | solution.py:254
  82.5 3.5 %collective-permute-start.7 = (bf16[8,32,1024]{2,1,0:T(8,128)(2,1)S(1)}, bf16[8,32,1024]{2,1,0:T(8,128)(2,1)S(1)}, u32[]{:S(2)}, u32[]{:S(2)}) collective-permute-start(bf16[8,32,1024]{2,1,0:T(8,128)(2,1)S(1)} %all-to-all-done.refs_0_), channel_id=1, source_target_pairs={{0,1},{1,0},{2,3},{3,2},{4,5},{5,4},{6,7},{7,6},{8,9},{9,8},{10,11... | collective-permute-start | bytes 1572872 | tf_op jit(solution)/shard_map/ppermute | solution.py:255
  86.0 4.5 %collective-permute-done.6.refs_2_ = bf16[8,32,1024]{2,1,0:T(8,128)(2,1)S(1)} collective-permute-done((bf16[8,32,1024]{2,1,0:T(8,128)(2,1)S(1)}, bf16[8,32,1024]{2,1,0:T(8,128)(2,1)S(1)}, u32[]{:S(2)}, u32[]{:S(2)}) %collective-permute-start.6) | collective-permute-done | bytes 524320 | tf_op jit(solution)/shard_map/ppermute | solution.py:254
  90.4 0.0 copy-start.8
  90.4 4.1 %collective-permute-start.9 = (bf16[8,32,1024]{2,1,0:T(8,128)(2,1)S(1)}, bf16[8,32,1024]{2,1,0:T(8,128)(2,1)S(1)}, u32[]{:S(2)}, u32[]{:S(2)}) collective-permute-start(bf16[8,32,1024]{2,1,0:T(8,128)(2,1)S(1)} %collective-permute-done.6.refs_2_), channel_id=1, source_target_pairs={{0,1},{1,0},{2,3},{3,2},{4,5},{5,4},{6,7},{7,6},{8,9},{9,8},{10,11... | collective-permute-start | bytes 1572872 | tf_op jit(solution)/shard_map/ppermute | solution.py:255
  94.6 0.9 collective-permute-done.5.refs_1_
  95.5 0.0 copy-start.9
  95.5 4.4 %collective-permute-start.8 = (bf16[8,32,1024]{2,1,0:T(8,128)(2,1)S(1)}, bf16[8,32,1024]{2,1,0:T(8,128)(2,1)}, u32[]{:S(2)}, u32[]{:S(2)}) collective-permute-start(bf16[8,32,1024]{2,1,0:T(8,128)(2,1)S(1)} %collective-permute-done.5.refs_1_), channel_id=1, source_target_pairs={{0,1},{1,0},{2,3},{3,2},{4,5},{5,4},{6,7},{7,6},{8,9},{9,8},{10,11... | collective-permute-start | bytes 1572872 | tf_op jit(solution)/shard_map/ppermute | solution.py:255
  99.9 0.0 collective-permute-done.7.refs_3_
  99.9 0.0 copy-start.10
  99.9 0.0 collective-permute-done.9.refs_5_
  99.9 0.0 copy-done.9
  99.9 0.8 copy-done.10
  100.7 0.0 copy-start.11
  100.7 0.8 copy-done.11
  101.5 0.1 collective-permute-done.8.refs_4_
  101.5 0.0 all-gather.5.cloned.1.call-done
  101.5 0.0 copy-done.2
  101.5 0.0 copy-done.8
  101.5 6.8 %shard_map.156 = bf16[4,528,256]{2,1,0:T(8,128)(2,1)} custom-call(s32[1]{0:T(128)} %bitcast.expert_ref, bf16[8,32,1024]{2,1,0:T(8,128)(2,1)} %copy-done.2, bf16[8,32,1024]{2,1,0:T(8,128)(2,1)} %copy-done.9, bf16[8,32,1024]{2,1,0:T(8,128)(2,1)} %copy-done.8, bf16[8,32,1024]{2,1,0:T(8,128)(2,1)} %copy-done.10, ...), custom_call_target="tpu_custom_call" | custom-call | tf_op jit(solution)/shard_map/pallas_call | solution.py:264
  108.3 0.0 copy-done.6
  108.3 0.0 copy-done.7
  108.3 4.0 %all-to-all-start.1 = ((bf16[4,528,256]{2,1,0:T(8,128)(2,1)}), bf16[4,528,256]{2,1,0:T(8,128)(2,1)S(1)}, u32[]{:S(2)}, u32[]{:S(2)}) async-start(bf16[4,528,256]{2,1,0:T(8,128)(2,1)} %shard_map.156), calls=%async_computation.1 | async-start | bytes 2162688 | tf_op jit(solution)/shard_map/all_to_all | solution.py:276
  112.3 0.0 copy-done.3
  112.3 0.0 copy-done.4
  112.3 0.0 copy-done.5
  112.3 10.0 %shard_map.157 = (bf16[1,156,416]{2,1,0:T(8,128)(2,1)}, bf16[1,156,416]{2,1,0:T(8,128)(2,1)}, f32[1,156]{1,0:T(1,128)}, bf16[192,104]{1,0:T(8,128)(2,1)}, bf16[192,104]{1,0:T(8,128)(2,1)}) custom-call(s32[1]{0:T(128)} %bitcast.expert_ref, bf16[32,7296]{1,0:T(8,128)(2,1)} %all_gather.15.rows_ref.refs_0_.refs_6_, bf16[32,7296]{1,0:T(8,128)(2,1)} %copy-done.4, ...), custom_call_target="tpu_custom_call" | custom-call | tf_op jit(solution)/shard_map/pallas_call | solution.py:281
  122.3 7.1 %all-gather.2.dots_ref = f32[6,1,156]{2,1,0:T(1,128)} all-gather(f32[1,1,156]{2,1,0:T(1,128)} %bitcast.14), channel_id=3, replica_groups=mesh['x'=4,'y'=8,'e'=4,'l'=3,'c'=2] {'l','c'}, dimensions={0}, use_global_device_ids=true | all-gather | bytes 4368 | tf_op jit(solution)/shard_map/all_gather | solution.py:326
  129.4 0.0 all-to-all-done.1.in_ref
  129.4 0.0 copy-start.1
  129.4 1.0 copy-done.1
  130.4 2.1 %shard_map.158 = (bf16[416,224]{1,0:T(8,128)(2,1)}, bf16[104,224]{1,0:T(8,128)(2,1)}, f32[1,156]{1,0:T(1,128)}) custom-call(bf16[4,528,256]{2,1,0:T(8,128)(2,1)} %copy-done.1, f32[6,1,156]{2,1,0:T(1,128)} %all-gather.2.dots_ref), custom_call_target="tpu_custom_call" | custom-call | tf_op jit(solution)/shard_map/pallas_call | solution.py:327
Async XLA Ops:
  7.2 94.4 %all-gather.5.cloned.1.call-start = ((), (), s32[]{:S(2)}) async-start(), calls=%async_computation.2 | async-start | bytes 1916928 | tf_op jit(solution)/shard_map/all_gather | solution.py:234
  39.5 18.4 %copy-start = (bf16[32,7296]{1,0:T(8,128)(2,1)S(1)}, bf16[32,7296]{1,0:T(8,128)(2,1)}, u32[]{:S(2)}) copy-start(bf16[32,7296]{1,0:T(8,128)(2,1)} %all_gather.15.rows_ref.refs_0_.refs_6_) | copy-start | bytes 1400836
  41.8 19.4 %collective-permute-start.1 = (bf16[32,7296]{1,0:T(8,128)(2,1)}, bf16[32,7296]{1,0:T(8,128)(2,1)S(1)}, u32[]{:S(2)}, u32[]{:S(2)}) collective-permute-start(bf16[32,7296]{1,0:T(8,128)(2,1)} %all_gather.15.rows_ref.refs_0_.refs_6_), channel_id=1, source_target_pairs={{0,22},{2,0},{4,2},{6,4},{8,6},{10,8},{12,10},{14,12},{16,14},{18,... | collective-permute-start | bytes 1400840 | tf_op jit(solution)/shard_map/ppermute | solution.py:254
  49.2 14.5 %collective-permute-start = (bf16[32,7296]{1,0:T(8,128)(2,1)}, bf16[32,7296]{1,0:T(8,128)(2,1)S(1)}, u32[]{:S(2)}, u32[]{:S(2)}) collective-permute-start(bf16[32,7296]{1,0:T(8,128)(2,1)} %all_gather.15.rows_ref.refs_0_.refs_6_), channel_id=1, source_target_pairs={{0,2},{2,4},{4,6},{6,8},{8,10},{10,12},{12,14},{14,16},{16,18},{18... | collective-permute-start | bytes 1400840 | tf_op jit(solution)/shard_map/ppermute | solution.py:254
  51.1 23.7 %all-to-all-start = ((bf16[8,32,1024]{2,1,0:T(8,128)(2,1)}), bf16[8,32,1024]{2,1,0:T(8,128)(2,1)S(1)}, u32[]{:S(2)}, u32[]{:S(2)}) async-start(bf16[8,32,1024]{2,1,0:T(8,128)(2,1)} %shard_map.154), calls=%async_computation | async-start | bytes 1048576 | tf_op jit(solution)/shard_map/all_to_all | solution.py:251
  57.9 9.6 %collective-permute-start.2 = (bf16[32,7296]{1,0:T(8,128)(2,1)S(1)}, bf16[32,7296]{1,0:T(8,128)(2,1)S(1)}, u32[]{:S(2)}, u32[]{:S(2)}) collective-permute-start(bf16[32,7296]{1,0:T(8,128)(2,1)S(1)} %copy-done), channel_id=1, source_target_pairs={{0,1},{1,0},{2,3},{3,2},{4,5},{5,4},{6,7},{7,6},{8,9},{9,8},{10,11... | collective-permute-start | bytes 1400840 | tf_op jit(solution)/shard_map/ppermute | solution.py:255
  61.2 51.1 %copy-start.3 = (bf16[32,7296]{1,0:T(8,128)(2,1)}, bf16[32,7296]{1,0:T(8,128)(2,1)S(1)}, u32[]{:S(2)}) copy-start(bf16[32,7296]{1,0:T(8,128)(2,1)S(1)} %collective-permute-done.1.refs_2_.refs_8_) | copy-start | bytes 1400836
  61.2 13.6 %collective-permute-start.4 = (bf16[32,7296]{1,0:T(8,128)(2,1)S(1)}, bf16[32,7296]{1,0:T(8,128)(2,1)S(1)}, u32[]{:S(2)}, u32[]{:S(2)}) collective-permute-start(bf16[32,7296]{1,0:T(8,128)(2,1)S(1)} %collective-permute-done.1.refs_2_.refs_8_), channel_id=1, source_target_pairs={{0,1},{1,0},{2,3},{3,2},{4,5},{5,4},{6,7},{7,6},{8,9},{9,8},{10,11... | collective-permute-start | bytes 1400840 | tf_op jit(solution)/shard_map/ppermute | solution.py:255
  63.7 48.6 %copy-start.4 = (bf16[32,7296]{1,0:T(8,128)(2,1)}, bf16[32,7296]{1,0:T(8,128)(2,1)S(1)}, u32[]{:S(2)}) copy-start(bf16[32,7296]{1,0:T(8,128)(2,1)S(1)} %collective-permute-done.refs_1_.refs_7_) | copy-start | bytes 1400836
  63.7 11.0 %collective-permute-start.3 = (bf16[32,7296]{1,0:T(8,128)(2,1)S(1)}, bf16[32,7296]{1,0:T(8,128)(2,1)S(1)}, u32[]{:S(2)}, u32[]{:S(2)}) collective-permute-start(bf16[32,7296]{1,0:T(8,128)(2,1)S(1)} %collective-permute-done.refs_1_.refs_7_), channel_id=1, source_target_pairs={{0,1},{1,0},{2,3},{3,2},{4,5},{5,4},{6,7},{7,6},{8,9},{9,8},{10,11... | collective-permute-start | bytes 1400840 | tf_op jit(solution)/shard_map/ppermute | solution.py:255
  67.5 44.8 %copy-start.5 = (bf16[32,7296]{1,0:T(8,128)(2,1)}, bf16[32,7296]{1,0:T(8,128)(2,1)S(1)}, u32[]{:S(2)}) copy-start(bf16[32,7296]{1,0:T(8,128)(2,1)S(1)} %collective-permute-done.2.refs_3_.refs_9_) | copy-start | bytes 1400836
  74.7 26.8 %copy-start.2 = (bf16[8,32,1024]{2,1,0:T(8,128)(2,1)}, bf16[8,32,1024]{2,1,0:T(8,128)(2,1)S(1)}, u32[]{:S(2)}) copy-start(bf16[8,32,1024]{2,1,0:T(8,128)(2,1)S(1)} %all-to-all-done.refs_0_) | copy-start | bytes 1572868
  74.8 33.6 %copy-start.6 = (bf16[32,7296]{1,0:T(8,128)(2,1)}, bf16[32,7296]{1,0:T(8,128)(2,1)S(1)}, u32[]{:S(2)}) copy-start(bf16[32,7296]{1,0:T(8,128)(2,1)S(1)} %collective-permute-done.4.refs_5_.refs_11_) | copy-start | bytes 1400836
  74.8 33.6 %copy-start.7 = (bf16[32,7296]{1,0:T(8,128)(2,1)}, bf16[32,7296]{1,0:T(8,128)(2,1)S(1)}, u32[]{:S(2)}) copy-start(bf16[32,7296]{1,0:T(8,128)(2,1)S(1)} %collective-permute-done.3.refs_4_.refs_10_) | copy-start | bytes 1400836
  74.8 15.7 %collective-permute-start.6 = (bf16[8,32,1024]{2,1,0:T(8,128)(2,1)S(1)}, bf16[8,32,1024]{2,1,0:T(8,128)(2,1)S(1)}, u32[]{:S(2)}, u32[]{:S(2)}) collective-permute-start(bf16[8,32,1024]{2,1,0:T(8,128)(2,1)S(1)} %all-to-all-done.refs_0_), channel_id=1, source_target_pairs={{0,22},{2,0},{4,2},{6,4},{8,6},{10,8},{12,10},{14,12},{16,14},{18,... | collective-permute-start | bytes 1572872 | tf_op jit(solution)/shard_map/ppermute | solution.py:254
  80.5 14.9 %collective-permute-start.5 = (bf16[8,32,1024]{2,1,0:T(8,128)(2,1)S(1)}, bf16[8,32,1024]{2,1,0:T(8,128)(2,1)S(1)}, u32[]{:S(2)}, u32[]{:S(2)}) collective-permute-start(bf16[8,32,1024]{2,1,0:T(8,128)(2,1)S(1)} %all-to-all-done.refs_0_), channel_id=1, source_target_pairs={{0,2},{2,4},{4,6},{6,8},{8,10},{10,12},{12,14},{14,16},{16,18},{18... | collective-permute-start | bytes 1572872 | tf_op jit(solution)/shard_map/ppermute | solution.py:254
  82.5 17.4 %collective-permute-start.7 = (bf16[8,32,1024]{2,1,0:T(8,128)(2,1)S(1)}, bf16[8,32,1024]{2,1,0:T(8,128)(2,1)S(1)}, u32[]{:S(2)}, u32[]{:S(2)}) collective-permute-start(bf16[8,32,1024]{2,1,0:T(8,128)(2,1)S(1)} %all-to-all-done.refs_0_), channel_id=1, source_target_pairs={{0,1},{1,0},{2,3},{3,2},{4,5},{5,4},{6,7},{7,6},{8,9},{9,8},{10,11... | collective-permute-start | bytes 1572872 | tf_op jit(solution)/shard_map/ppermute | solution.py:255
  90.4 11.1 %copy-start.8 = (bf16[8,32,1024]{2,1,0:T(8,128)(2,1)}, bf16[8,32,1024]{2,1,0:T(8,128)(2,1)S(1)}, u32[]{:S(2)}) copy-start(bf16[8,32,1024]{2,1,0:T(8,128)(2,1)S(1)} %collective-permute-done.6.refs_2_) | copy-start | bytes 1572868
  90.4 9.5 %collective-permute-start.9 = (bf16[8,32,1024]{2,1,0:T(8,128)(2,1)S(1)}, bf16[8,32,1024]{2,1,0:T(8,128)(2,1)S(1)}, u32[]{:S(2)}, u32[]{:S(2)}) collective-permute-start(bf16[8,32,1024]{2,1,0:T(8,128)(2,1)S(1)} %collective-permute-done.6.refs_2_), channel_id=1, source_target_pairs={{0,1},{1,0},{2,3},{3,2},{4,5},{5,4},{6,7},{7,6},{8,9},{9,8},{10,11... | collective-permute-start | bytes 1572872 | tf_op jit(solution)/shard_map/ppermute | solution.py:255
  95.5 4.4 %copy-start.9 = (bf16[8,32,1024]{2,1,0:T(8,128)(2,1)}, bf16[8,32,1024]{2,1,0:T(8,128)(2,1)S(1)}, u32[]{:S(2)}) copy-start(bf16[8,32,1024]{2,1,0:T(8,128)(2,1)S(1)} %collective-permute-done.5.refs_1_) | copy-start | bytes 1572868
  95.5 6.0 %collective-permute-start.8 = (bf16[8,32,1024]{2,1,0:T(8,128)(2,1)S(1)}, bf16[8,32,1024]{2,1,0:T(8,128)(2,1)}, u32[]{:S(2)}, u32[]{:S(2)}) collective-permute-start(bf16[8,32,1024]{2,1,0:T(8,128)(2,1)S(1)} %collective-permute-done.5.refs_1_), channel_id=1, source_target_pairs={{0,1},{1,0},{2,3},{3,2},{4,5},{5,4},{6,7},{7,6},{8,9},{9,8},{10,11... | collective-permute-start | bytes 1572872 | tf_op jit(solution)/shard_map/ppermute | solution.py:255
  99.9 0.8 copy-start.10
  100.7 0.8 copy-start.11
  108.3 21.1 %all-to-all-start.1 = ((bf16[4,528,256]{2,1,0:T(8,128)(2,1)}), bf16[4,528,256]{2,1,0:T(8,128)(2,1)S(1)}, u32[]{:S(2)}, u32[]{:S(2)}) async-start(bf16[4,528,256]{2,1,0:T(8,128)(2,1)} %shard_map.156), calls=%async_computation.1 | async-start | bytes 2162688 | tf_op jit(solution)/shard_map/all_to_all | solution.py:276
  129.4 1.0 copy-start.1
Sparse Core Ops, SparseCore 0:
  10.9 49.3 all-gather.4

commit v5 on v3

--- a/solution.py
+++ b/solution.py
@@ -80,13 +80,6 @@
             cols_ref[y, :, x * stride + block : (x + 1) * stride] = meta[:, : stride - block]
 
 
-def pack_kernel(cols_ref, rows_ref, out_ref):
-    ny, _, span = cols_ref.shape
-    for y in range(ny):
-        out_ref[:, y * span : (y + 1) * span] = cols_ref[y]
-    out_ref[:, ny * span :] = rows_ref[...]
-
-
 def routing(meta, expert):
     hit0 = meta[:, 0:1] == expert
     hit1 = meta[:, 1:2] == expert
@@ -250,39 +243,41 @@
         compiler_params=params(),
     )(expert_arr, part_arr, grad_out, gate_prob.T, expert_ids.T, slot_positions.T)
     cols = lax.all_to_all(cols, "y", split_axis=0, concat_axis=0, tiled=True)
-    packed = pl.pallas_call(
-        pack_kernel,
-        out_shape=jax.ShapeDtypeStruct((eighth, ny * span + width + LANES), bf16),
-        compiler_params=params(),
-    )(cols, mine)
-    packed = lax.all_gather(packed, "e", axis=0, tiled=True)
-    pieces = [packed] + [lax.ppermute(packed, ("e", "l"), ring(ne * RUN, d)) for d in (1, -1)]
-    pieces += [lax.ppermute(p, "c", ring(CORES, 1)) for p in pieces]
+    rows = lax.all_gather(mine, "e", axis=0, tiled=True)
+    cols, rows = lax.optimization_barrier((cols, rows))
+    cols = lax.all_gather(
+        cols.transpose(1, 0, 2).reshape(eighth, ny * span), "e", axis=0, tiled=True
+    )
+    cols, rows = lax.optimization_barrier((cols, rows))
+
+    def along(piece):
+        return [piece] + [lax.ppermute(piece, ("e", "l"), ring(ne * RUN, d)) for d in (1, -1)]
+
+    def other(pieces):
+        return pieces + [lax.ppermute(p, "c", ring(CORES, 1)) for p in pieces]
+
+    chunk_pieces = other(along(cols))
+    row_pieces = other(along(rows))
 
     height = hwidth + -(-dwidth // 16) * 16
     ktotal = ny * ne * tokens
     partial_sums = pl.pallas_call(
         functools.partial(weight_kernel, block, ny),
-        grid=(1,),
         out_shape=jax.ShapeDtypeStruct((nx, height, stride), bf16),
-        in_specs=[smem]
-        + [pl.BlockSpec((ne * eighth, ny * span), lambda k: (0, 0))] * 6
-        + [whole(*hiddens.shape)],
-        out_specs=whole(nx, height, stride),
+        in_specs=[smem] + [vmem] * 7,
         scratch_shapes=[
             pltpu.VMEM((ktotal, span), bf16),
             pltpu.VMEM((ktotal, hwidth), bf16),
             pltpu.VMEM((ktotal, LANES), bf16),
         ],
         compiler_params=params(),
-    )(expert_arr, *pieces, hiddens)
+    )(expert_arr, *chunk_pieces, hiddens)
     partial_sums, expert_arr = lax.optimization_barrier((partial_sums, expert_arr))
     landed = lax.all_to_all(partial_sums, "x", split_axis=0, concat_axis=0, tiled=True)
 
-    depth = math.gcd(ny * span, width)
-    base = ny * span // depth
-    data_spec = pl.BlockSpec((ne * eighth, depth), lambda k: (0, base + k))
-    meta_spec = pl.BlockSpec((ne * eighth, LANES), lambda k: (0, (ny * span + width) // LANES))
+    depth = math.gcd(1024, width)
+    data_spec = pl.BlockSpec((ne * eighth, depth), lambda k: (0, k))
+    meta_spec = pl.BlockSpec((ne * eighth, LANES), lambda k: (0, width // LANES))
     gate_grad, up_grad, dots, dense_gate_grad, dense_up_grad = pl.pallas_call(
         back_kernel,
         grid=(width // depth,),
@@ -318,8 +313,8 @@
         compiler_params=params(),
     )(
         expert_arr,
-        *pieces,
-        *pieces,
+        *row_pieces,
+        *row_pieces,
         expert_down,
         dense_down,
         expert_gate_pre,

time: 141 us -> 145 us (1.028)
  starting transfers between devices: 33.8 us -> 54.6 us
  waiting for transfers between devices: 10.5 us -> 1.46 us
  blocking collectives: 54.7 us -> 48.8 us
  Pallas kernels: 24.4 us -> 22.7 us
    all_to_all x1 -> x0, blocking collectives: 15.7 us -> none  [local(): cols = lax.all_to_all(cols, 'y', split_axis=0, concat_axis=0, tiled=True)]
    ppermute x5 -> x10, starting transfers between devices: 28.6 us -> 42.5 us  [the longest x6 24.8 us: other(): return pieces + [lax.ppermute(p, 'c', ring(CORES, 1)) for p in pieces]]
    all_gather x1 -> x2, blocking collectives: 32 us -> 42 us  [the longest x1 27.7 us: local(): rows = lax.all_gather(mine, 'e', axis=0, tiled=True)]
    ppermute x5 -> x10, waiting for transfers between devices: 10.4 us -> 1.44 us  [the longest x6 1.4 us: other(): return pieces + [lax.ppermute(p, 'c', ring(CORES, 1)) for p in pieces]]
    all_to_all x0 -> x1, starting transfers between devices: none -> 7.65 us  [local(): cols = lax.all_to_all(cols, 'y', split_axis=0, concat_axis=0, tiled=True)]
    pallas_call x2 -> x1, Pallas kernels: 8.44 us -> 6.75 us  [local(): pl.pallas_call(functools.partial(weight_kernel, block, ny), out_shape=jax...]
    unnamed x12 -> x24, local copies, waits for them, and re-layouts: 3 us -> 2.76 us
  transfers between devices with their start and end apart: 7 -> 13, of which waited for: 3 -> 1; matrix products, arithmetic and copies ran while one was open for 0% -> 0% of each run, Pallas kernels for 10% -> 13%
where the time goes in v5:
time: 145 us
  starting transfers between devices  54.6 us (38%)
  blocking collectives  48.8 us (34%)
  Pallas kernels  22.7 us (16%)
  between operations  14.3 us (10%)
  local copies, waits for them, and re-layouts  2.76 us (2%)
  waiting for transfers between devices  1.46 us (1%)
    all_gather x1, blocking collectives, local(): rows = lax.all_gather(mine, 'e', axis=0, tiled=True)  27.7 us
    ppermute x6, starting transfers between devices, other(): return pieces + [lax.ppermute(p, 'c', ring(CORES, 1)) for p in pieces]  24.8 us
    ppermute x4, starting transfers between devices, along(): lax.ppermute(piece, ('e', 'l'), ring(ne * RUN, d))  17.8 us
    all_gather x1, blocking collectives, local(): lax.all_gather(cols.transpose(1, 0, 2).reshape(eighth, ny * span), 'e', a...  14.3 us
    pallas_call x1, Pallas kernels, local(): pl.pallas_call(back_kernel, grid=(width // depth,), out_shape=(jax.ShapeD...  9.98 us
    all_to_all x1, starting transfers between devices, local(): cols = lax.all_to_all(cols, 'y', split_axis=0, concat_axis=0, tiled=True)  7.65 us
    all_gather x1, blocking collectives, local(): all_dots = lax.all_gather(dots, ('l', 'c'), axis=0)  6.79 us
    pallas_call x1, Pallas kernels, local(): pl.pallas_call(functools.partial(weight_kernel, block, ny), out_shape=jax...  6.75 us
  transfers between devices with their start and end apart: 13, of which 1 were waited for; matrix products, arithmetic and copies ran while one was open for 0% of the time, Pallas kernels for 13%

profile of v5, /device:TPU:1, one launch (start us, length us, event | category | flops | bytes accessed | tf_op | source)
XLA Modules:
  0.0 144.5 jit_solution(11465221153206130261)
XLA Ops:
  7.2 0.0 all-gather.5.cloned.1.call-start
  7.2 1.8 %shard_map.154 = bf16[208,512]{1,0:T(8,128)(2,1)} custom-call(bf16[1,156,416]{2,1,0:T(8,128)(2,1)} %refs_14_.1, bf16[1,156,416]{2,1,0:T(8,128)(2,1)} %refs_15_.1, bf16[192,104]{1,0:T(8,128)(2,1)} %refs_16_.1, bf16[192,104]{1,0:T(8,128)(2,1)} %refs_17_.1), custom_call_target="tpu_custom_call" | custom-call | tf_op jit(solution)/shard_map/pallas_call | solution.py:227
  9.0 0.0 all-gather.5.cloned.1.call-update
  9.0 2.1 %shard_map.153 = (bf16[8,7296]{1,0:T(8,128)(2,1)}, bf16[8,8,1024]{2,1,0:T(8,128)(2,1)}) custom-call(s32[1]{0:T(128)} %bitcast.expert_ref, s32[1]{0:T(128)} %bitcast.1.part_ref, bf16[48,7168]{1,0:T(8,128)(2,1)} %rows_ref.1, bf16[2,48]{1,0:T(2,128)(2,1)} %bitcast.19, s32[2,48]{1,0:T(2,128)} %bitcast.16, s32[2,48]{1,0:T(2,128)} %bitcast.17), custom_call_target="tpu_custom_call" | custom-call | tf_op jit(solution)/shard_map/pallas_call | solution.py:236
  11.1 7.7 %all-to-all-start = ((bf16[8,8,1024]{2,1,0:T(8,128)(2,1)}), bf16[8,8,1024]{2,1,0:T(8,128)(2,1)S(1)}, u32[]{:S(2)}, u32[]{:S(2)}) async-start(bf16[8,8,1024]{2,1,0:T(8,128)(2,1)} %get-tuple-element.23), calls=%async_computation | async-start | bytes 262144 | tf_op jit(solution)/shard_map/all_to_all | solution.py:245
  18.8 27.7 %all_gather.18.refs_0_.refs_6_ = bf16[32,7296]{1,0:T(8,128)(2,1)S(1)} all-gather(bf16[8,7296]{1,0:T(8,128)(2,1)} %get-tuple-element.24), channel_id=1, replica_groups=mesh['x'=4,'y'=8,'e'=4,'l'=3,'c'=2] {'e'}, dimensions={0}, use_global_device_ids=true | all-gather | bytes 583680 | tf_op jit(solution)/shard_map/all_gather | solution.py:246
  46.4 0.0 copy-start.1
  46.4 0.0 all-to-all-done
  46.4 14.3 %all_gather.19.refs_0_ = bf16[32,8192]{1,0:T(8,128)(2,1)S(1)} all-gather(bf16[8,8192]{1,0:T(8,128)(2,1)S(1)} %bitcast.15), channel_id=1, replica_groups=mesh['x'=4,'y'=8,'e'=4,'l'=3,'c'=2] {'e'}, dimensions={0}, use_global_device_ids=true | all-gather | bytes 655360 | tf_op jit(solution)/shard_map/all_gather | solution.py:248
  60.8 0.0 copy-start.2
  60.8 9.3 %collective-permute-start = (bf16[32,8192]{1,0:T(8,128)(2,1)S(1)}, bf16[32,8192]{1,0:T(8,128)(2,1)S(1)}, u32[]{:S(2)}, u32[]{:S(2)}) collective-permute-start(bf16[32,8192]{1,0:T(8,128)(2,1)S(1)} %all_gather.19.refs_0_), channel_id=1, source_target_pairs={{0,2},{2,4},{4,6},{6,8},{8,10},{10,12},{12,14},{14,16},{16,18},{18... | collective-permute-start | bytes 1572872 | tf_op jit(solution)/shard_map/ppermute | solution.py:254
  70.1 1.9 %collective-permute-start.1 = (bf16[32,8192]{1,0:T(8,128)(2,1)S(1)}, bf16[32,8192]{1,0:T(8,128)(2,1)S(1)}, u32[]{:S(2)}, u32[]{:S(2)}) collective-permute-start(bf16[32,8192]{1,0:T(8,128)(2,1)S(1)} %all_gather.19.refs_0_), channel_id=1, source_target_pairs={{0,22},{2,0},{4,2},{6,4},{8,6},{10,8},{12,10},{14,12},{16,14},{18,... | collective-permute-start | bytes 1572872 | tf_op jit(solution)/shard_map/ppermute | solution.py:254
  72.1 6.6 %collective-permute-start.2 = (bf16[32,8192]{1,0:T(8,128)(2,1)S(1)}, bf16[32,8192]{1,0:T(8,128)(2,1)S(1)}, u32[]{:S(2)}, u32[]{:S(2)}) collective-permute-start(bf16[32,8192]{1,0:T(8,128)(2,1)S(1)} %all_gather.19.refs_0_), channel_id=1, source_target_pairs={{0,1},{1,0},{2,3},{3,2},{4,5},{5,4},{6,7},{7,6},{8,9},{9,8},{10,11... | collective-permute-start | bytes 1572872 | tf_op jit(solution)/shard_map/ppermute | solution.py:257
  78.7 0.0 collective-permute-done.refs_1_
  78.7 0.0 copy-start.8
  78.7 5.5 %collective-permute-start.3 = (bf16[32,8192]{1,0:T(8,128)(2,1)S(1)}, bf16[32,8192]{1,0:T(8,128)(2,1)S(1)}, u32[]{:S(2)}, u32[]{:S(2)}) collective-permute-start(bf16[32,8192]{1,0:T(8,128)(2,1)S(1)} %collective-permute-done.refs_1_), channel_id=1, source_target_pairs={{0,1},{1,0},{2,3},{3,2},{4,5},{5,4},{6,7},{7,6},{8,9},{9,8},{10,11... | collective-permute-start | bytes 1572872 | tf_op jit(solution)/shard_map/ppermute | solution.py:257
  84.2 0.0 collective-permute-done.1.refs_2_
  84.2 0.0 copy-start.9
  84.2 5.6 %collective-permute-start.4 = (bf16[32,8192]{1,0:T(8,128)(2,1)S(1)}, bf16[32,8192]{1,0:T(8,128)(2,1)}, u32[]{:S(2)}, u32[]{:S(2)}) collective-permute-start(bf16[32,8192]{1,0:T(8,128)(2,1)S(1)} %collective-permute-done.1.refs_2_), channel_id=1, source_target_pairs={{0,1},{1,0},{2,3},{3,2},{4,5},{5,4},{6,7},{7,6},{8,9},{9,8},{10,11... | collective-permute-start | bytes 1572872 | tf_op jit(solution)/shard_map/ppermute | solution.py:257
  89.8 3.4 %collective-permute-start.5 = (bf16[32,7296]{1,0:T(8,128)(2,1)S(1)}, bf16[32,7296]{1,0:T(8,128)(2,1)S(1)}, u32[]{:S(2)}, u32[]{:S(2)}) collective-permute-start(bf16[32,7296]{1,0:T(8,128)(2,1)S(1)} %all_gather.18.refs_0_.refs_6_), channel_id=1, source_target_pairs={{0,2},{2,4},{4,6},{6,8},{8,10},{10,12},{12,14},{14,16},{16,18},{18... | collective-permute-start | bytes 1400840 | tf_op jit(solution)/shard_map/ppermute | solution.py:254
  93.2 3.1 %collective-permute-start.6 = (bf16[32,7296]{1,0:T(8,128)(2,1)S(1)}, bf16[32,7296]{1,0:T(8,128)(2,1)S(1)}, u32[]{:S(2)}, u32[]{:S(2)}) collective-permute-start(bf16[32,7296]{1,0:T(8,128)(2,1)S(1)} %all_gather.18.refs_0_.refs_6_), channel_id=1, source_target_pairs={{0,22},{2,0},{4,2},{6,4},{8,6},{10,8},{12,10},{14,12},{16,14},{18,... | collective-permute-start | bytes 1400840 | tf_op jit(solution)/shard_map/ppermute | solution.py:254
  96.3 0.0 collective-permute-done.2.refs_3_
  96.3 0.0 copy-start.10
  96.4 0.0 collective-permute-done.3.refs_4_
  96.4 0.0 copy-start.11
  96.4 0.9 copy-done.11
  97.2 0.0 collective-permute-done.4.refs_5_
  97.2 0.0 all-gather.5.cloned.1.call-done
  97.2 0.0 copy-done.2
  97.2 0.0 copy-done.8
  97.2 0.0 copy-done.9
  97.3 0.1 copy-done.10
  97.4 6.8 %shard_map.155 = bf16[4,528,256]{2,1,0:T(8,128)(2,1)} custom-call(s32[1]{0:T(128)} %bitcast.expert_ref, bf16[32,8192]{1,0:T(8,128)(2,1)} %copy-done.2, bf16[32,8192]{1,0:T(8,128)(2,1)} %copy-done.8, bf16[32,8192]{1,0:T(8,128)(2,1)} %copy-done.9, bf16[32,8192]{1,0:T(8,128)(2,1)} %copy-done.10, bf16[32,8192]{1,0:T(8,128)(2,1)} %copy-done.11, ...), custom_call_target="tpu_custom_call" | custom-call | tf_op jit(solution)/shard_map/pallas_call | solution.py:264
  104.1 4.3 %all-to-all-start.1 = ((bf16[4,528,256]{2,1,0:T(8,128)(2,1)}), bf16[4,528,256]{2,1,0:T(8,128)(2,1)S(1)}, u32[]{:S(2)}, u32[]{:S(2)}) async-start(bf16[4,528,256]{2,1,0:T(8,128)(2,1)} %shard_map.155), calls=%async_computation.1 | async-start | bytes 2162688 | tf_op jit(solution)/shard_map/all_to_all | solution.py:276
  108.5 0.0 copy-done.1
  108.5 2.7 %collective-permute-start.7 = (bf16[32,7296]{1,0:T(8,128)(2,1)S(1)}, bf16[32,7296]{1,0:T(8,128)(2,1)S(1)}, u32[]{:S(2)}, u32[]{:S(2)}) collective-permute-start(bf16[32,7296]{1,0:T(8,128)(2,1)S(1)} %all_gather.18.refs_0_.refs_6_), channel_id=1, source_target_pairs={{0,1},{1,0},{2,3},{3,2},{4,5},{5,4},{6,7},{7,6},{8,9},{9,8},{10,11... | collective-permute-start | bytes 1400840 | tf_op jit(solution)/shard_map/ppermute | solution.py:257
  111.2 0.0 collective-permute-done.5.refs_1_.refs_7_
  111.2 0.0 copy-start.3
  111.2 1.9 %collective-permute-start.8 = (bf16[32,7296]{1,0:T(8,128)(2,1)S(1)}, bf16[32,7296]{1,0:T(8,128)(2,1)S(1)}, u32[]{:S(2)}, u32[]{:S(2)}) collective-permute-start(bf16[32,7296]{1,0:T(8,128)(2,1)S(1)} %collective-permute-done.5.refs_1_.refs_7_), channel_id=1, source_target_pairs={{0,1},{1,0},{2,3},{3,2},{4,5},{5,4},{6,7},{7,6},{8,9},{9,8},{10,11... | collective-permute-start | bytes 1400840 | tf_op jit(solution)/shard_map/ppermute | solution.py:257
  113.2 0.0 collective-permute-done.6.refs_2_.refs_8_
  113.2 0.0 copy-start.4
  113.2 2.4 %collective-permute-start.9 = (bf16[32,7296]{1,0:T(8,128)(2,1)S(1)}, bf16[32,7296]{1,0:T(8,128)(2,1)S(1)}, u32[]{:S(2)}, u32[]{:S(2)}) collective-permute-start(bf16[32,7296]{1,0:T(8,128)(2,1)S(1)} %collective-permute-done.6.refs_2_.refs_8_), channel_id=1, source_target_pairs={{0,1},{1,0},{2,3},{3,2},{4,5},{5,4},{6,7},{7,6},{8,9},{9,8},{10,11... | collective-permute-start | bytes 1400840 | tf_op jit(solution)/shard_map/ppermute | solution.py:257
  115.6 0.0 collective-permute-done.7.refs_3_.refs_9_
  115.6 0.0 copy-start.5
  115.6 0.0 collective-permute-done.8.refs_4_.refs_10_
  115.6 0.0 copy-start.6
  115.6 1.4 collective-permute-done.9.refs_5_.refs_11_
  117.0 0.0 copy-done.3
  117.0 0.0 copy-done.4
  117.0 0.0 copy-done.5
  117.0 0.0 copy-done.6
  117.0 0.0 copy-start.7
  117.1 0.8 copy-done.7
  117.8 10.0 %shard_map.156 = (bf16[1,156,416]{2,1,0:T(8,128)(2,1)}, bf16[1,156,416]{2,1,0:T(8,128)(2,1)}, f32[1,156]{1,0:T(1,128)}, bf16[192,104]{1,0:T(8,128)(2,1)}, bf16[192,104]{1,0:T(8,128)(2,1)}) custom-call(s32[1]{0:T(128)} %bitcast.expert_ref, bf16[32,7296]{1,0:T(8,128)(2,1)} %copy-done.1, bf16[32,7296]{1,0:T(8,128)(2,1)} %copy-done.3, ...), custom_call_target="tpu_custom_call" | custom-call | tf_op jit(solution)/shard_map/pallas_call | solution.py:281
  127.8 6.8 %all-gather.2.dots_ref = f32[6,1,156]{2,1,0:T(1,128)} all-gather(f32[1,1,156]{2,1,0:T(1,128)} %bitcast.18), channel_id=3, replica_groups=mesh['x'=4,'y'=8,'e'=4,'l'=3,'c'=2] {'l','c'}, dimensions={0}, use_global_device_ids=true | all-gather | bytes 4368 | tf_op jit(solution)/shard_map/all_gather | solution.py:326
  134.6 0.0 all-to-all-done.1.in_ref
  134.6 0.0 copy-start
  134.6 1.0 copy-done
  135.6 2.1 %shard_map.157 = (bf16[416,224]{1,0:T(8,128)(2,1)}, bf16[104,224]{1,0:T(8,128)(2,1)}, f32[1,156]{1,0:T(1,128)}) custom-call(bf16[4,528,256]{2,1,0:T(8,128)(2,1)} %copy-done, f32[6,1,156]{2,1,0:T(1,128)} %all-gather.2.dots_ref), custom_call_target="tpu_custom_call" | custom-call | tf_op jit(solution)/shard_map/pallas_call | solution.py:327
Async XLA Ops:
  7.2 90.1 %all-gather.5.cloned.1.call-start = ((), (), s32[]{:S(2)}) async-start(), calls=%async_computation.2 | async-start | bytes 1916928 | tf_op jit(solution)/shard_map/all_gather | solution.py:232
  11.1 35.3 %all-to-all-start = ((bf16[8,8,1024]{2,1,0:T(8,128)(2,1)}), bf16[8,8,1024]{2,1,0:T(8,128)(2,1)S(1)}, u32[]{:S(2)}, u32[]{:S(2)}) async-start(bf16[8,8,1024]{2,1,0:T(8,128)(2,1)} %get-tuple-element.23), calls=%async_computation | async-start | bytes 262144 | tf_op jit(solution)/shard_map/all_to_all | solution.py:245
  46.4 62.0 %copy-start.1 = (bf16[32,7296]{1,0:T(8,128)(2,1)}, bf16[32,7296]{1,0:T(8,128)(2,1)S(1)}, u32[]{:S(2)}) copy-start(bf16[32,7296]{1,0:T(8,128)(2,1)S(1)} %all_gather.18.refs_0_.refs_6_) | copy-start | bytes 1400836
  60.8 36.5 %copy-start.2 = (bf16[32,8192]{1,0:T(8,128)(2,1)}, bf16[32,8192]{1,0:T(8,128)(2,1)S(1)}, u32[]{:S(2)}) copy-start(bf16[32,8192]{1,0:T(8,128)(2,1)S(1)} %all_gather.19.refs_0_) | copy-start | bytes 1572868
  60.8 17.9 %collective-permute-start = (bf16[32,8192]{1,0:T(8,128)(2,1)S(1)}, bf16[32,8192]{1,0:T(8,128)(2,1)S(1)}, u32[]{:S(2)}, u32[]{:S(2)}) collective-permute-start(bf16[32,8192]{1,0:T(8,128)(2,1)S(1)} %all_gather.19.refs_0_), channel_id=1, source_target_pairs={{0,2},{2,4},{4,6},{6,8},{8,10},{10,12},{12,14},{14,16},{16,18},{18... | collective-permute-start | bytes 1572872 | tf_op jit(solution)/shard_map/ppermute | solution.py:254
  70.1 14.1 %collective-permute-start.1 = (bf16[32,8192]{1,0:T(8,128)(2,1)S(1)}, bf16[32,8192]{1,0:T(8,128)(2,1)S(1)}, u32[]{:S(2)}, u32[]{:S(2)}) collective-permute-start(bf16[32,8192]{1,0:T(8,128)(2,1)S(1)} %all_gather.19.refs_0_), channel_id=1, source_target_pairs={{0,22},{2,0},{4,2},{6,4},{8,6},{10,8},{12,10},{14,12},{16,14},{18,... | collective-permute-start | bytes 1572872 | tf_op jit(solution)/shard_map/ppermute | solution.py:254
  72.1 24.3 %collective-permute-start.2 = (bf16[32,8192]{1,0:T(8,128)(2,1)S(1)}, bf16[32,8192]{1,0:T(8,128)(2,1)S(1)}, u32[]{:S(2)}, u32[]{:S(2)}) collective-permute-start(bf16[32,8192]{1,0:T(8,128)(2,1)S(1)} %all_gather.19.refs_0_), channel_id=1, source_target_pairs={{0,1},{1,0},{2,3},{3,2},{4,5},{5,4},{6,7},{7,6},{8,9},{9,8},{10,11... | collective-permute-start | bytes 1572872 | tf_op jit(solution)/shard_map/ppermute | solution.py:257
  78.7 18.6 %copy-start.8 = (bf16[32,8192]{1,0:T(8,128)(2,1)}, bf16[32,8192]{1,0:T(8,128)(2,1)S(1)}, u32[]{:S(2)}) copy-start(bf16[32,8192]{1,0:T(8,128)(2,1)S(1)} %collective-permute-done.refs_1_) | copy-start | bytes 1572868
  78.7 17.7 %collective-permute-start.3 = (bf16[32,8192]{1,0:T(8,128)(2,1)S(1)}, bf16[32,8192]{1,0:T(8,128)(2,1)S(1)}, u32[]{:S(2)}, u32[]{:S(2)}) collective-permute-start(bf16[32,8192]{1,0:T(8,128)(2,1)S(1)} %collective-permute-done.refs_1_), channel_id=1, source_target_pairs={{0,1},{1,0},{2,3},{3,2},{4,5},{5,4},{6,7},{7,6},{8,9},{9,8},{10,11... | collective-permute-start | bytes 1572872 | tf_op jit(solution)/shard_map/ppermute | solution.py:257
  84.2 13.1 %copy-start.9 = (bf16[32,8192]{1,0:T(8,128)(2,1)}, bf16[32,8192]{1,0:T(8,128)(2,1)S(1)}, u32[]{:S(2)}) copy-start(bf16[32,8192]{1,0:T(8,128)(2,1)S(1)} %collective-permute-done.1.refs_2_) | copy-start | bytes 1572868
  84.2 13.1 %collective-permute-start.4 = (bf16[32,8192]{1,0:T(8,128)(2,1)S(1)}, bf16[32,8192]{1,0:T(8,128)(2,1)}, u32[]{:S(2)}, u32[]{:S(2)}) collective-permute-start(bf16[32,8192]{1,0:T(8,128)(2,1)S(1)} %collective-permute-done.1.refs_2_), channel_id=1, source_target_pairs={{0,1},{1,0},{2,3},{3,2},{4,5},{5,4},{6,7},{7,6},{8,9},{9,8},{10,11... | collective-permute-start | bytes 1572872 | tf_op jit(solution)/shard_map/ppermute | solution.py:257
  89.8 21.4 %collective-permute-start.5 = (bf16[32,7296]{1,0:T(8,128)(2,1)S(1)}, bf16[32,7296]{1,0:T(8,128)(2,1)S(1)}, u32[]{:S(2)}, u32[]{:S(2)}) collective-permute-start(bf16[32,7296]{1,0:T(8,128)(2,1)S(1)} %all_gather.18.refs_0_.refs_6_), channel_id=1, source_target_pairs={{0,2},{2,4},{4,6},{6,8},{8,10},{10,12},{12,14},{14,16},{16,18},{18... | collective-permute-start | bytes 1400840 | tf_op jit(solution)/shard_map/ppermute | solution.py:254
  93.2 20.0 %collective-permute-start.6 = (bf16[32,7296]{1,0:T(8,128)(2,1)S(1)}, bf16[32,7296]{1,0:T(8,128)(2,1)S(1)}, u32[]{:S(2)}, u32[]{:S(2)}) collective-permute-start(bf16[32,7296]{1,0:T(8,128)(2,1)S(1)} %all_gather.18.refs_0_.refs_6_), channel_id=1, source_target_pairs={{0,22},{2,0},{4,2},{6,4},{8,6},{10,8},{12,10},{14,12},{16,14},{18,... | collective-permute-start | bytes 1400840 | tf_op jit(solution)/shard_map/ppermute | solution.py:254
  96.3 1.0 copy-start.10
  96.4 0.9 copy-start.11
  104.1 30.5 %all-to-all-start.1 = ((bf16[4,528,256]{2,1,0:T(8,128)(2,1)}), bf16[4,528,256]{2,1,0:T(8,128)(2,1)S(1)}, u32[]{:S(2)}, u32[]{:S(2)}) async-start(bf16[4,528,256]{2,1,0:T(8,128)(2,1)} %shard_map.155), calls=%async_computation.1 | async-start | bytes 2162688 | tf_op jit(solution)/shard_map/all_to_all | solution.py:276
  108.5 7.1 %collective-permute-start.7 = (bf16[32,7296]{1,0:T(8,128)(2,1)S(1)}, bf16[32,7296]{1,0:T(8,128)(2,1)S(1)}, u32[]{:S(2)}, u32[]{:S(2)}) collective-permute-start(bf16[32,7296]{1,0:T(8,128)(2,1)S(1)} %all_gather.18.refs_0_.refs_6_), channel_id=1, source_target_pairs={{0,1},{1,0},{2,3},{3,2},{4,5},{5,4},{6,7},{7,6},{8,9},{9,8},{10,11... | collective-permute-start | bytes 1400840 | tf_op jit(solution)/shard_map/ppermute | solution.py:257
  111.2 5.8 %copy-start.3 = (bf16[32,7296]{1,0:T(8,128)(2,1)}, bf16[32,7296]{1,0:T(8,128)(2,1)S(1)}, u32[]{:S(2)}) copy-start(bf16[32,7296]{1,0:T(8,128)(2,1)S(1)} %collective-permute-done.5.refs_1_.refs_7_) | copy-start | bytes 1400836
  111.2 4.4 %collective-permute-start.8 = (bf16[32,7296]{1,0:T(8,128)(2,1)S(1)}, bf16[32,7296]{1,0:T(8,128)(2,1)S(1)}, u32[]{:S(2)}, u32[]{:S(2)}) collective-permute-start(bf16[32,7296]{1,0:T(8,128)(2,1)S(1)} %collective-permute-done.5.refs_1_.refs_7_), channel_id=1, source_target_pairs={{0,1},{1,0},{2,3},{3,2},{4,5},{5,4},{6,7},{7,6},{8,9},{9,8},{10,11... | collective-permute-start | bytes 1400840 | tf_op jit(solution)/shard_map/ppermute | solution.py:257
  113.2 3.9 %copy-start.4 = (bf16[32,7296]{1,0:T(8,128)(2,1)}, bf16[32,7296]{1,0:T(8,128)(2,1)S(1)}, u32[]{:S(2)}) copy-start(bf16[32,7296]{1,0:T(8,128)(2,1)S(1)} %collective-permute-done.6.refs_2_.refs_8_) | copy-start | bytes 1400836
  113.2 3.8 %collective-permute-start.9 = (bf16[32,7296]{1,0:T(8,128)(2,1)S(1)}, bf16[32,7296]{1,0:T(8,128)(2,1)S(1)}, u32[]{:S(2)}, u32[]{:S(2)}) collective-permute-start(bf16[32,7296]{1,0:T(8,128)(2,1)S(1)} %collective-permute-done.6.refs_2_.refs_8_), channel_id=1, source_target_pairs={{0,1},{1,0},{2,3},{3,2},{4,5},{5,4},{6,7},{7,6},{8,9},{9,8},{10,11... | collective-permute-start | bytes 1400840 | tf_op jit(solution)/shard_map/ppermute | solution.py:257
  115.6 1.4 copy-start.5
  115.6 1.4 copy-start.6
  117.0 0.8 copy-start.7
  134.6 1.0 copy-start
Sparse Core Ops, SparseCore 0:
  10.9 49.2 all-gather.4

commit v6 on v4

--- a/solution.py
+++ b/solution.py
@@ -131,17 +131,6 @@
         out_ref[x, width:, :] = dsummed[: height - width, x * stride : (x + 1) * stride]
 
 
-def sum_kernel(scale, in_ref, dots_ref, expert_ref, dense_ref, dots_out):
-    dots_out[...] = jnp.sum(dots_ref[...], axis=0)
-    summed = in_ref[0].astype(jnp.float32)
-    for x in range(1, in_ref.shape[0]):
-        summed = summed + in_ref[x].astype(jnp.float32)
-    summed = (summed * scale).astype(jnp.bfloat16)
-    width, block = expert_ref.shape
-    expert_ref[...] = summed[:width, :block]
-    dense_ref[...] = summed[width : width + dense_ref.shape[0], :block]
-
-
 def place(onehot, values):
     high = values.astype(jnp.bfloat16)
     rest = values - high.astype(jnp.float32)
@@ -151,14 +140,10 @@
     return dot(onehot, high, dims) + dot(onehot, middle, dims) + dot(onehot, low, dims)
 
 
-def back_kernel(expert_ref, *refs):
-    datas, metas = refs[:6], refs[6:12]
-    we_ref, wd_ref, gate_ref, up_ref, dgate_ref, dup_ref = refs[12:18]
-    gate_out, up_out, dots_out, dgate_out, dup_out = refs[18:23]
-    acc_e, acc_d = refs[23:25]
-    step = pl.program_id(0)
-
-    @pl.when(step == 0)
+def product_kernel(*refs):
+    datas, we_ref, wd_ref, acc_e, acc_d = refs[:6], *refs[6:10]
+
+    @pl.when(pl.program_id(0) == 0)
     def _():
         acc_e[...] = jnp.zeros_like(acc_e)
         acc_d[...] = jnp.zeros_like(acc_d)
@@ -167,33 +152,36 @@
     acc_e[...] += dot(rows, we_ref[0], ((1,), (1,)))
     acc_d[...] += dot(rows, wd_ref[...], ((1,), (1,)))
 
-    @pl.when(step == pl.num_programs(0) - 1)
-    def _():
-        meta = jnp.concatenate([m[...] for m in metas], axis=0).astype(jnp.float32)
-        slot, prob, token = routing(meta, expert_ref[0].astype(jnp.float32))
-        slots = gate_ref.shape[1]
-        hot = one_hot(slot, slots)
-        back = place(hot, acc_e[...])
-        wide = jnp.broadcast_to(prob, (prob.shape[0], LANES)).astype(jnp.bfloat16)
-        slot_prob = dot(hot, wide, ((0,), (0,)))[:, :1]
-        up_val = up_ref[0].astype(jnp.float32)
-        activated, slope = silu_parts(gate_ref[0].astype(jnp.float32))
-        product = back * (activated * up_val)
-        ones = jnp.ones((8, product.shape[1]), jnp.float32)
-        dots_out[...] = lax.dot_general(
-            ones,
-            product,
-            (((1,), (1,)), ((), ())),
-            precision=lax.Precision.HIGHEST,
-            preferred_element_type=jnp.float32,
-        )[:1]
-        scaled = slot_prob * back
-        gate_out[0] = (scaled * up_val * slope).astype(jnp.bfloat16)
-        up_out[0] = (scaled * activated).astype(jnp.bfloat16)
-        dback = place(one_hot(token, dgate_ref.shape[0]), acc_d[...])
-        dactivated, dslope = silu_parts(dgate_ref[...].astype(jnp.float32))
-        dgate_out[...] = (dback * dup_ref[...].astype(jnp.float32) * dslope).astype(jnp.bfloat16)
-        dup_out[...] = (dback * dactivated).astype(jnp.bfloat16)
+
+def back_kernel(expert_ref, *refs):
+    metas = refs[:6]
+    acc_e, acc_d, gate_ref, up_ref, dgate_ref, dup_ref = refs[6:12]
+    gate_out, up_out, dots_out, dgate_out, dup_out = refs[12:17]
+    meta = jnp.concatenate([m[...] for m in metas], axis=0).astype(jnp.float32)
+    slot, prob, token = routing(meta, expert_ref[0].astype(jnp.float32))
+    slots = gate_ref.shape[1]
+    hot = one_hot(slot, slots)
+    back = place(hot, acc_e[...])
+    wide = jnp.broadcast_to(prob, (prob.shape[0], LANES)).astype(jnp.bfloat16)
+    slot_prob = dot(hot, wide, ((0,), (0,)))[:, :1]
+    up_val = up_ref[0].astype(jnp.float32)
+    activated, slope = silu_parts(gate_ref[0].astype(jnp.float32))
+    product = back * (activated * up_val)
+    ones = jnp.ones((8, product.shape[1]), jnp.float32)
+    dots_out[...] = lax.dot_general(
+        ones,
+        product,
+        (((1,), (1,)), ((), ())),
+        precision=lax.Precision.HIGHEST,
+        preferred_element_type=jnp.float32,
+    )[:1]
+    scaled = slot_prob * back
+    gate_out[0] = (scaled * up_val * slope).astype(jnp.bfloat16)
+    up_out[0] = (scaled * activated).astype(jnp.bfloat16)
+    dback = place(one_hot(token, dgate_ref.shape[0]), acc_d[...])
+    dactivated, dslope = silu_parts(dgate_ref[...].astype(jnp.float32))
+    dgate_out[...] = (dback * dup_ref[...].astype(jnp.float32) * dslope).astype(jnp.bfloat16)
+    dup_out[...] = (dback * dactivated).astype(jnp.bfloat16)
 
 
 def ring(count, step):
@@ -250,14 +238,35 @@
     rows, chunks = lax.optimization_barrier((rows, chunks))
     chunks = lax.all_to_all(chunks, "y", split_axis=0, concat_axis=0, tiled=True)
 
-    def spread(piece):
-        along = [piece] + [lax.ppermute(piece, ("e", "l"), ring(ne * RUN, d)) for d in (1, -1)]
-        other = [lax.ppermute(p, "c", ring(CORES, 1)) for p in along]
-        return along + other
-
-    row_pieces = spread(rows)
+    def along(piece):
+        return [piece] + [lax.ppermute(piece, ("e", "l"), ring(ne * RUN, d)) for d in (1, -1)]
+
+    def other(pieces):
+        return pieces + [lax.ppermute(p, "c", ring(CORES, 1)) for p in pieces]
+
+    row_pieces = other(along(rows))
     chunks, *row_pieces = lax.optimization_barrier((chunks, *row_pieces))
-    chunk_pieces = spread(chunks)
+
+    depth = math.gcd(1024, width)
+    acc_e, acc_d = pl.pallas_call(
+        product_kernel,
+        grid=(width // depth,),
+        out_shape=(
+            jax.ShapeDtypeStruct((ne * tokens, hwidth), jnp.float32),
+            jax.ShapeDtypeStruct((ne * tokens, dwidth), jnp.float32),
+        ),
+        in_specs=[pl.BlockSpec((ne * eighth, depth), lambda k: (0, k))] * 6
+        + [
+            pl.BlockSpec((1, hwidth, depth), lambda k: (0, 0, k)),
+            pl.BlockSpec((dwidth, depth), lambda k: (0, k)),
+        ],
+        out_specs=(whole(ne * tokens, hwidth), whole(ne * tokens, dwidth)),
+        compiler_params=params(),
+    )(*row_pieces, expert_down, dense_down)
+
+    near, up, down = along(chunks)
+    up, down, acc_e, acc_d = lax.optimization_barrier((up, down, acc_e, acc_d))
+    chunk_pieces = other([near, up, down])
 
     height = hwidth + -(-dwidth // 16) * 16
     ktotal = ny * ne * tokens
@@ -275,12 +284,10 @@
     partial_sums, expert_arr = lax.optimization_barrier((partial_sums, expert_arr))
     landed = lax.all_to_all(partial_sums, "x", split_axis=0, concat_axis=0, tiled=True)
 
-    depth = math.gcd(1024, width)
-    data_spec = pl.BlockSpec((ne * eighth, depth), lambda k: (0, k))
     meta_spec = pl.BlockSpec((ne * eighth, LANES), lambda k: (0, width // LANES))
     gate_grad, up_grad, dots, dense_gate_grad, dense_up_grad = pl.pallas_call(
         back_kernel,
-        grid=(width // depth,),
+        grid=(1,),
         out_shape=(
             jax.ShapeDtypeStruct((1, slots, hwidth), bf16),
             jax.ShapeDtypeStruct((1, slots, hwidth), bf16),
@@ -289,11 +296,10 @@
             jax.ShapeDtypeStruct((ne * tokens, dwidth), bf16),
         ),
         in_specs=[smem]
-        + [data_spec] * 6
         + [meta_spec] * 6
         + [
-            pl.BlockSpec((1, hwidth, depth), lambda k: (0, 0, k)),
-            pl.BlockSpec((dwidth, depth), lambda k: (0, k)),
+            whole(ne * tokens, hwidth),
+            whole(ne * tokens, dwidth),
             whole(1, slots, hwidth),
             whole(1, slots, hwidth),
             whole(ne * tokens, dwidth),
@@ -306,33 +312,26 @@
             whole(ne * tokens, dwidth),
             whole(ne * tokens, dwidth),
         ),
-        scratch_shapes=[
-            pltpu.VMEM((ne * tokens, hwidth), jnp.float32),
-            pltpu.VMEM((ne * tokens, dwidth), jnp.float32),
-        ],
         compiler_params=params(),
     )(
         expert_arr,
         *row_pieces,
-        *row_pieces,
-        expert_down,
-        dense_down,
+        acc_e,
+        acc_d,
         expert_gate_pre,
         expert_up_pre,
         dense_gate_pre,
         dense_up_pre,
     )
-
     all_dots = lax.all_gather(dots, ("l", "c"), axis=0)
-    expert_down_grad, dense_down_grad, slot_prob_grad = pl.pallas_call(
-        functools.partial(sum_kernel, 1.0 / (nx * ny)),
-        out_shape=(
-            jax.ShapeDtypeStruct((hwidth, block), bf16),
-            jax.ShapeDtypeStruct((dwidth, block), bf16),
-            jax.ShapeDtypeStruct((1, slots), jnp.float32),
-        ),
-        compiler_params=params(),
-    )(landed, all_dots)
+
+    def total(top, count):
+        parts = [landed[x, top : top + count, :block].astype(jnp.float32) for x in range(nx)]
+        return (sum(parts[1:], parts[0]) * (1.0 / (nx * ny))).astype(bf16)
+
+    expert_down_grad = total(0, hwidth)
+    dense_down_grad = total(hwidth, dwidth)
+    slot_prob_grad = jnp.sum(all_dots, axis=0)
     return (
         gate_grad,
         up_grad,

time: 140 us -> 140 us (level)
  starting transfers between devices: 48.7 us -> 46.6 us
  other arithmetic: 0 us -> 2.04 us
  waiting for transfers between devices: 13.3 us -> 15 us
    all_to_all x1, waiting for transfers between devices: 0.01 us -> 5.08 us  [local(): lax.all_to_all(partial_sums, 'x', split_axis=0, concat_axis=0, tiled=True)]
    ppermute x10, waiting for transfers between devices: 6.06 us -> 2.71 us  [the longest x4 1.64 us: along(): lax.ppermute(piece, ('e', 'l'), ring(ne * RUN, d))]
    ppermute x10, starting transfers between devices: 37.9 us -> 35.7 us  [the longest x6 18.7 us: other(): return pieces + [lax.ppermute(p, 'c', ring(CORES, 1)) for p in pieces]]
  transfers between devices with their start and end apart: 13 -> 13, of which waited for: 5 -> 5; matrix products, arithmetic and copies ran while one was open for 0% -> 0% of each run, Pallas kernels for 10% -> 11%
where the time goes in v6:
time: 140 us; the launch traced here: 139 us
  starting transfers between devices  46.6 us (33%)
  blocking collectives  34.9 us (25%)
  Pallas kernels  24.3 us (17%)
  waiting for transfers between devices  15 us (11%)
  between operations  14.3 us (10%)
  other arithmetic  2.04 us (1%)
  local copies, waits for them, and re-layouts  1.61 us (1%)
    all_gather x1, blocking collectives, local(): rows = lax.all_gather(mine, 'e', axis=0, tiled=True)  28.5 us
    ppermute x6, starting transfers between devices, other(): return pieces + [lax.ppermute(p, 'c', ring(CORES, 1)) for p in pieces]  18.7 us
    ppermute x4, starting transfers between devices, along(): lax.ppermute(piece, ('e', 'l'), ring(ne * RUN, d))  17 us
    pallas_call x1, Pallas kernels, local(): pl.pallas_call(product_kernel, grid=(width // depth,), out_shape=(jax.Sha...  8.43 us
    all_to_all x1, waiting for transfers between devices, local(): lax.all_to_all(chunks, 'y', split_axis=0, concat_axis=0, tiled=True)  7.22 us
    all_to_all x1, starting transfers between devices, local(): lax.all_to_all(chunks, 'y', split_axis=0, concat_axis=0, tiled=True)  6.83 us
    pallas_call x1, Pallas kernels, local(): pl.pallas_call(functools.partial(weight_kernel, block), out_shape=jax.Sha...  6.77 us
    all_gather x1, blocking collectives, local(): all_dots = lax.all_gather(dots, ('l', 'c'), axis=0)  6.38 us
  transfers between devices with their start and end apart: 13, of which 5 were waited for; matrix products, arithmetic and copies ran while one was open for 0% of the time, Pallas kernels for 11%

profile of v6, /device:TPU:1, one launch (start us, length us, event | category | flops | bytes accessed | tf_op | source)
XLA Modules:
  0.0 138.7 jit_solution(18326380542280621255)
XLA Ops:
  7.2 0.0 all-gather.5.cloned.1.call-start
  7.2 1.8 %shard_map.156 = bf16[208,512]{1,0:T(8,128)(2,1)} custom-call(bf16[1,156,416]{2,1,0:T(8,128)(2,1)} %refs_8_.1, bf16[1,156,416]{2,1,0:T(8,128)(2,1)} %refs_9_.1, bf16[192,104]{1,0:T(8,128)(2,1)} %refs_10_.1, bf16[192,104]{1,0:T(8,128)(2,1)} %refs_11_.1), custom_call_target="tpu_custom_call" | custom-call | tf_op jit(solution)/shard_map/pallas_call | solution.py:217
  9.0 0.0 all-gather.5.cloned.1.call-update
  9.0 2.0 %shard_map.153 = bf16[8,7296]{1,0:T(8,128)(2,1)} custom-call(s32[1]{0:T(128)} %bitcast.expert_ref, s32[1]{0:T(128)} %bitcast.1.part_ref, bf16[48,7168]{1,0:T(8,128)(2,1)} %rows_ref.1, bf16[2,48]{1,0:T(2,128)(2,1)} %bitcast.23, s32[2,48]{1,0:T(2,128)} %bitcast.19, s32[2,48]{1,0:T(2,128)} %bitcast.20), custom_call_target="tpu_custom_call" | custom-call | tf_op jit(solution)/shard_map/pallas_call | solution.py:225
  11.0 28.5 %all_gather.15.rows_ref.refs_0_ = bf16[32,7296]{1,0:T(8,128)(2,1)} all-gather(bf16[8,7296]{1,0:T(8,128)(2,1)} %shard_map.153), channel_id=1, replica_groups=mesh['x'=4,'y'=8,'e'=4,'l'=3,'c'=2] {'e'}, dimensions={0}, use_global_device_ids=true | all-gather | bytes 583680 | tf_op jit(solution)/shard_map/all_gather | solution.py:231
  39.5 0.0 copy-start
  39.5 2.3 %shard_map.154 = bf16[8,32,1024]{2,1,0:T(8,128)(2,1)} custom-call(bf16[32,7296]{1,0:T(8,128)(2,1)} %all_gather.15.rows_ref.refs_0_), custom_call_target="tpu_custom_call" | custom-call | tf_op jit(solution)/shard_map/pallas_call | solution.py:233
  41.8 7.3 %collective-permute-start.1 = (bf16[32,7296]{1,0:T(8,128)(2,1)}, bf16[32,7296]{1,0:T(8,128)(2,1)S(1)}, u32[]{:S(2)}, u32[]{:S(2)}) collective-permute-start(bf16[32,7296]{1,0:T(8,128)(2,1)} %all_gather.15.rows_ref.refs_0_), channel_id=1, source_target_pairs={{0,22},{2,0},{4,2},{6,4},{8,6},{10,8},{12,10},{14,12},{16,14},{18,... | collective-permute-start | bytes 1400840 | tf_op jit(solution)/shard_map/ppermute | solution.py:242
  49.1 1.9 %collective-permute-start = (bf16[32,7296]{1,0:T(8,128)(2,1)}, bf16[32,7296]{1,0:T(8,128)(2,1)S(1)}, u32[]{:S(2)}, u32[]{:S(2)}) collective-permute-start(bf16[32,7296]{1,0:T(8,128)(2,1)} %all_gather.15.rows_ref.refs_0_), channel_id=1, source_target_pairs={{0,2},{2,4},{4,6},{6,8},{8,10},{10,12},{12,14},{14,16},{16,18},{18... | collective-permute-start | bytes 1400840 | tf_op jit(solution)/shard_map/ppermute | solution.py:242
  51.1 6.8 %all-to-all-start = ((bf16[8,32,1024]{2,1,0:T(8,128)(2,1)}), bf16[8,32,1024]{2,1,0:T(8,128)(2,1)S(1)}, u32[]{:S(2)}, u32[]{:S(2)}) async-start(bf16[8,32,1024]{2,1,0:T(8,128)(2,1)} %shard_map.154), calls=%async_computation | async-start | bytes 1048576 | tf_op jit(solution)/shard_map/all_to_all | solution.py:239
  57.9 0.0 copy-done
  57.9 3.3 %collective-permute-start.2 = (bf16[32,7296]{1,0:T(8,128)(2,1)S(1)}, bf16[32,7296]{1,0:T(8,128)(2,1)S(1)}, u32[]{:S(2)}, u32[]{:S(2)}) collective-permute-start(bf16[32,7296]{1,0:T(8,128)(2,1)S(1)} %copy-done), channel_id=1, source_target_pairs={{0,1},{1,0},{2,3},{3,2},{4,5},{5,4},{6,7},{7,6},{8,9},{9,8},{10,11... | collective-permute-start | bytes 1400840 | tf_op jit(solution)/shard_map/ppermute | solution.py:245
  61.2 0.0 collective-permute-done.1.refs_2_
  61.2 0.0 copy-start.2
  61.2 1.9 %collective-permute-start.4 = (bf16[32,7296]{1,0:T(8,128)(2,1)S(1)}, bf16[32,7296]{1,0:T(8,128)(2,1)S(1)}, u32[]{:S(2)}, u32[]{:S(2)}) collective-permute-start(bf16[32,7296]{1,0:T(8,128)(2,1)S(1)} %collective-permute-done.1.refs_2_), channel_id=1, source_target_pairs={{0,1},{1,0},{2,3},{3,2},{4,5},{5,4},{6,7},{7,6},{8,9},{9,8},{10,11... | collective-permute-start | bytes 1400840 | tf_op jit(solution)/shard_map/ppermute | solution.py:245
  63.1 0.6 collective-permute-done.refs_1_
  63.7 0.0 copy-start.3
  63.7 3.8 %collective-permute-start.3 = (bf16[32,7296]{1,0:T(8,128)(2,1)S(1)}, bf16[32,7296]{1,0:T(8,128)(2,1)S(1)}, u32[]{:S(2)}, u32[]{:S(2)}) collective-permute-start(bf16[32,7296]{1,0:T(8,128)(2,1)S(1)} %collective-permute-done.refs_1_), channel_id=1, source_target_pairs={{0,1},{1,0},{2,3},{3,2},{4,5},{5,4},{6,7},{7,6},{8,9},{9,8},{10,11... | collective-permute-start | bytes 1400840 | tf_op jit(solution)/shard_map/ppermute | solution.py:245
  67.5 0.0 collective-permute-done.2.refs_3_
  67.5 0.0 copy-start.4
  67.5 7.2 %all-to-all-done.refs_0_ = bf16[8,32,1024]{2,1,0:T(8,128)(2,1)S(1)} async-done(((bf16[8,32,1024]{2,1,0:T(8,128)(2,1)}), bf16[8,32,1024]{2,1,0:T(8,128)(2,1)S(1)}, u32[]{:S(2)}, u32[]{:S(2)}) %all-to-all-start) | async-done | bytes 524320 | tf_op jit(solution)/shard_map/all_to_all | solution.py:239
  74.7 0.0 copy-start.1
  74.7 0.0 collective-permute-done.4.refs_5_
  74.7 0.0 copy-start.5
  74.7 0.0 collective-permute-done.3.refs_4_
  74.7 0.0 copy-start.6
  74.7 5.8 %collective-permute-start.6 = (bf16[8,32,1024]{2,1,0:T(8,128)(2,1)S(1)}, bf16[8,32,1024]{2,1,0:T(8,128)(2,1)S(1)}, u32[]{:S(2)}, u32[]{:S(2)}) collective-permute-start(bf16[8,32,1024]{2,1,0:T(8,128)(2,1)S(1)} %all-to-all-done.refs_0_), channel_id=1, source_target_pairs={{0,22},{2,0},{4,2},{6,4},{8,6},{10,8},{12,10},{14,12},{16,14},{18,... | collective-permute-start | bytes 1572872 | tf_op jit(solution)/shard_map/ppermute | solution.py:242
  80.5 1.9 %collective-permute-start.5 = (bf16[8,32,1024]{2,1,0:T(8,128)(2,1)S(1)}, bf16[8,32,1024]{2,1,0:T(8,128)(2,1)S(1)}, u32[]{:S(2)}, u32[]{:S(2)}) collective-permute-start(bf16[8,32,1024]{2,1,0:T(8,128)(2,1)S(1)} %all-to-all-done.refs_0_), channel_id=1, source_target_pairs={{0,2},{2,4},{4,6},{6,8},{8,10},{10,12},{12,14},{14,16},{16,18},{18... | collective-permute-start | bytes 1572872 | tf_op jit(solution)/shard_map/ppermute | solution.py:242
  82.5 3.5 %collective-permute-start.7 = (bf16[8,32,1024]{2,1,0:T(8,128)(2,1)S(1)}, bf16[8,32,1024]{2,1,0:T(8,128)(2,1)S(1)}, u32[]{:S(2)}, u32[]{:S(2)}) collective-permute-start(bf16[8,32,1024]{2,1,0:T(8,128)(2,1)S(1)} %all-to-all-done.refs_0_), channel_id=1, source_target_pairs={{0,1},{1,0},{2,3},{3,2},{4,5},{5,4},{6,7},{7,6},{8,9},{9,8},{10,11... | collective-permute-start | bytes 1572872 | tf_op jit(solution)/shard_map/ppermute | solution.py:245
  85.9 0.0 copy-done.2
  85.9 0.0 copy-done.3
  85.9 0.0 copy-done.4
  86.0 0.0 copy-done.5
  86.0 0.0 copy-done.6
  86.0 8.4 %shard_map.155 = (f32[192,416]{1,0:T(8,128)}, f32[192,104]{1,0:T(8,128)}) custom-call(bf16[32,7296]{1,0:T(8,128)(2,1)} %all_gather.15.rows_ref.refs_0_, bf16[32,7296]{1,0:T(8,128)(2,1)} %copy-done.3, bf16[32,7296]{1,0:T(8,128)(2,1)} %copy-done.2, bf16[32,7296]{1,0:T(8,128)(2,1)} %copy-done.4, bf16[32,7296]{1,0:T(8,128)(2,1)} %copy-done.6, ...), custom_call_target="tpu_custom_call" | custom-call | tf_op jit(solution)/shard_map/pallas_call | solution.py:251
  94.4 0.0 copy-done.1
  94.4 0.0 collective-permute-done.6.refs_2_
  94.4 0.0 copy-start.7
  94.4 1.1 collective-permute-done.5.refs_1_
  95.5 0.0 copy-start.8
  95.5 4.4 %collective-permute-start.8 = (bf16[8,32,1024]{2,1,0:T(8,128)(2,1)S(1)}, bf16[8,32,1024]{2,1,0:T(8,128)(2,1)S(1)}, u32[]{:S(2)}, u32[]{:S(2)}) collective-permute-start(bf16[8,32,1024]{2,1,0:T(8,128)(2,1)S(1)} %collective-permute-done.5.refs_1_), channel_id=1, source_target_pairs={{0,1},{1,0},{2,3},{3,2},{4,5},{5,4},{6,7},{7,6},{8,9},{9,8},{10,11... | collective-permute-start | bytes 1572872 | tf_op jit(solution)/shard_map/ppermute | solution.py:245
  99.9 1.9 %collective-permute-start.9 = (bf16[8,32,1024]{2,1,0:T(8,128)(2,1)S(1)}, bf16[8,32,1024]{2,1,0:T(8,128)(2,1)S(1)}, u32[]{:S(2)}, u32[]{:S(2)}) collective-permute-start(bf16[8,32,1024]{2,1,0:T(8,128)(2,1)S(1)} %collective-permute-done.6.refs_2_), channel_id=1, source_target_pairs={{0,1},{1,0},{2,3},{3,2},{4,5},{5,4},{6,7},{7,6},{8,9},{9,8},{10,11... | collective-permute-start | bytes 1572872 | tf_op jit(solution)/shard_map/ppermute | solution.py:245
  101.8 0.0 collective-permute-done.7.refs_3_
  101.8 0.0 copy-done.8
  101.8 0.0 copy-start.9
  101.8 0.0 collective-permute-done.8.refs_4_
  101.8 0.8 copy-done.9
  102.6 0.0 copy-start.10
  102.6 1.1 collective-permute-done.9.refs_5_
  103.7 0.0 copy-start.11
  103.7 0.0 all-gather.5.cloned.1.call-done
  103.7 0.0 copy-done.7
  103.7 0.0 copy-done.10
  103.7 0.8 copy-done.11
  104.5 6.8 %shard_map.157 = bf16[4,528,256]{2,1,0:T(8,128)(2,1)} custom-call(s32[1]{0:T(128)} %bitcast.expert_ref, bf16[8,32,1024]{2,1,0:T(8,128)(2,1)} %copy-done.1, bf16[8,32,1024]{2,1,0:T(8,128)(2,1)} %copy-done.8, bf16[8,32,1024]{2,1,0:T(8,128)(2,1)} %copy-done.7, bf16[8,32,1024]{2,1,0:T(8,128)(2,1)} %copy-done.9, bf16[8,32,1024]{2,1,0:T(8,128)(2,1)} %copy-done.10, ...), custom_call_target="tpu_custom_call" | custom-call | tf_op jit(solution)/shard_map/pallas_call | solution.py:273
  111.3 4.0 %all-to-all-start.1 = ((bf16[4,528,256]{2,1,0:T(8,128)(2,1)}), bf16[4,528,256]{2,1,0:T(8,128)(2,1)S(1)}, u32[]{:S(2)}, u32[]{:S(2)}) async-start(bf16[4,528,256]{2,1,0:T(8,128)(2,1)} %shard_map.157), calls=%async_computation.1 | async-start | bytes 2162688 | tf_op jit(solution)/shard_map/all_to_all | solution.py:285
  115.3 3.1 %shard_map.158 = (bf16[1,156,416]{2,1,0:T(8,128)(2,1)}, bf16[1,156,416]{2,1,0:T(8,128)(2,1)}, f32[1,156]{1,0:T(1,128)}, bf16[192,104]{1,0:T(8,128)(2,1)}, bf16[192,104]{1,0:T(8,128)(2,1)}) custom-call(s32[1]{0:T(128)} %bitcast.expert_ref, bf16[32,7296]{1,0:T(8,128)(2,1)} %all_gather.15.rows_ref.refs_0_, bf16[32,7296]{1,0:T(8,128)(2,1)} %copy-done.3, ...), custom_call_target="tpu_custom_call" | custom-call | tf_op jit(solution)/shard_map/pallas_call | solution.py:288
  118.4 6.4 %all-gather.2 = f32[6,1,156]{2,1,0:T(1,128)S(1)} all-gather(f32[1,1,156]{2,1,0:T(1,128)} %bitcast.22), channel_id=3, replica_groups=mesh['x'=4,'y'=8,'e'=4,'l'=3,'c'=2] {'l','c'}, dimensions={0}, use_global_device_ids=true | all-gather | bytes 4368 | tf_op jit(solution)/shard_map/all_gather | solution.py:326
  124.7 0.6 reduce.1
  125.3 5.1 %all-to-all-done.1 = bf16[4,528,256]{2,1,0:T(8,128)(2,1)S(1)} async-done(((bf16[4,528,256]{2,1,0:T(8,128)(2,1)}), bf16[4,528,256]{2,1,0:T(8,128)(2,1)S(1)}, u32[]{:S(2)}, u32[]{:S(2)}) %all-to-all-start.1) | async-done | bytes 1081376 | tf_op jit(solution)/shard_map/all_to_all | solution.py:285
  130.4 0.7 fusion.1
  131.1 0.8 fusion
Async XLA Ops:
  7.2 96.5 %all-gather.5.cloned.1.call-start = ((), (), s32[]{:S(2)}) async-start(), calls=%async_computation.2 | async-start | bytes 1916928 | tf_op jit(solution)/shard_map/all_gather | solution.py:222
  39.5 18.4 %copy-start = (bf16[32,7296]{1,0:T(8,128)(2,1)S(1)}, bf16[32,7296]{1,0:T(8,128)(2,1)}, u32[]{:S(2)}) copy-start(bf16[32,7296]{1,0:T(8,128)(2,1)} %all_gather.15.rows_ref.refs_0_) | copy-start | bytes 1400836
  41.8 19.4 %collective-permute-start.1 = (bf16[32,7296]{1,0:T(8,128)(2,1)}, bf16[32,7296]{1,0:T(8,128)(2,1)S(1)}, u32[]{:S(2)}, u32[]{:S(2)}) collective-permute-start(bf16[32,7296]{1,0:T(8,128)(2,1)} %all_gather.15.rows_ref.refs_0_), channel_id=1, source_target_pairs={{0,22},{2,0},{4,2},{6,4},{8,6},{10,8},{12,10},{14,12},{16,14},{18,... | collective-permute-start | bytes 1400840 | tf_op jit(solution)/shard_map/ppermute | solution.py:242
  49.1 14.5 %collective-permute-start = (bf16[32,7296]{1,0:T(8,128)(2,1)}, bf16[32,7296]{1,0:T(8,128)(2,1)S(1)}, u32[]{:S(2)}, u32[]{:S(2)}) collective-permute-start(bf16[32,7296]{1,0:T(8,128)(2,1)} %all_gather.15.rows_ref.refs_0_), channel_id=1, source_target_pairs={{0,2},{2,4},{4,6},{6,8},{8,10},{10,12},{12,14},{14,16},{16,18},{18... | collective-permute-start | bytes 1400840 | tf_op jit(solution)/shard_map/ppermute | solution.py:242
  51.1 23.6 %all-to-all-start = ((bf16[8,32,1024]{2,1,0:T(8,128)(2,1)}), bf16[8,32,1024]{2,1,0:T(8,128)(2,1)S(1)}, u32[]{:S(2)}, u32[]{:S(2)}) async-start(bf16[8,32,1024]{2,1,0:T(8,128)(2,1)} %shard_map.154), calls=%async_computation | async-start | bytes 1048576 | tf_op jit(solution)/shard_map/all_to_all | solution.py:239
  57.9 9.6 %collective-permute-start.2 = (bf16[32,7296]{1,0:T(8,128)(2,1)S(1)}, bf16[32,7296]{1,0:T(8,128)(2,1)S(1)}, u32[]{:S(2)}, u32[]{:S(2)}) collective-permute-start(bf16[32,7296]{1,0:T(8,128)(2,1)S(1)} %copy-done), channel_id=1, source_target_pairs={{0,1},{1,0},{2,3},{3,2},{4,5},{5,4},{6,7},{7,6},{8,9},{9,8},{10,11... | collective-permute-start | bytes 1400840 | tf_op jit(solution)/shard_map/ppermute | solution.py:245
  61.2 24.8 %copy-start.2 = (bf16[32,7296]{1,0:T(8,128)(2,1)}, bf16[32,7296]{1,0:T(8,128)(2,1)S(1)}, u32[]{:S(2)}) copy-start(bf16[32,7296]{1,0:T(8,128)(2,1)S(1)} %collective-permute-done.1.refs_2_) | copy-start | bytes 1400836
  61.2 13.5 %collective-permute-start.4 = (bf16[32,7296]{1,0:T(8,128)(2,1)S(1)}, bf16[32,7296]{1,0:T(8,128)(2,1)S(1)}, u32[]{:S(2)}, u32[]{:S(2)}) collective-permute-start(bf16[32,7296]{1,0:T(8,128)(2,1)S(1)} %collective-permute-done.1.refs_2_), channel_id=1, source_target_pairs={{0,1},{1,0},{2,3},{3,2},{4,5},{5,4},{6,7},{7,6},{8,9},{9,8},{10,11... | collective-permute-start | bytes 1400840 | tf_op jit(solution)/shard_map/ppermute | solution.py:245
  63.7 22.3 %copy-start.3 = (bf16[32,7296]{1,0:T(8,128)(2,1)}, bf16[32,7296]{1,0:T(8,128)(2,1)S(1)}, u32[]{:S(2)}) copy-start(bf16[32,7296]{1,0:T(8,128)(2,1)S(1)} %collective-permute-done.refs_1_) | copy-start | bytes 1400836
  63.7 11.0 %collective-permute-start.3 = (bf16[32,7296]{1,0:T(8,128)(2,1)S(1)}, bf16[32,7296]{1,0:T(8,128)(2,1)S(1)}, u32[]{:S(2)}, u32[]{:S(2)}) collective-permute-start(bf16[32,7296]{1,0:T(8,128)(2,1)S(1)} %collective-permute-done.refs_1_), channel_id=1, source_target_pairs={{0,1},{1,0},{2,3},{3,2},{4,5},{5,4},{6,7},{7,6},{8,9},{9,8},{10,11... | collective-permute-start | bytes 1400840 | tf_op jit(solution)/shard_map/ppermute | solution.py:245
  67.5 18.5 %copy-start.4 = (bf16[32,7296]{1,0:T(8,128)(2,1)}, bf16[32,7296]{1,0:T(8,128)(2,1)S(1)}, u32[]{:S(2)}) copy-start(bf16[32,7296]{1,0:T(8,128)(2,1)S(1)} %collective-permute-done.2.refs_3_) | copy-start | bytes 1400836
  74.7 19.7 %copy-start.1 = (bf16[8,32,1024]{2,1,0:T(8,128)(2,1)}, bf16[8,32,1024]{2,1,0:T(8,128)(2,1)S(1)}, u32[]{:S(2)}) copy-start(bf16[8,32,1024]{2,1,0:T(8,128)(2,1)S(1)} %all-to-all-done.refs_0_) | copy-start | bytes 1572868
  74.7 11.3 %copy-start.5 = (bf16[32,7296]{1,0:T(8,128)(2,1)}, bf16[32,7296]{1,0:T(8,128)(2,1)S(1)}, u32[]{:S(2)}) copy-start(bf16[32,7296]{1,0:T(8,128)(2,1)S(1)} %collective-permute-done.4.refs_5_) | copy-start | bytes 1400836
  74.7 11.3 %copy-start.6 = (bf16[32,7296]{1,0:T(8,128)(2,1)}, bf16[32,7296]{1,0:T(8,128)(2,1)S(1)}, u32[]{:S(2)}) copy-start(bf16[32,7296]{1,0:T(8,128)(2,1)S(1)} %collective-permute-done.3.refs_4_) | copy-start | bytes 1400836
  74.7 19.7 %collective-permute-start.6 = (bf16[8,32,1024]{2,1,0:T(8,128)(2,1)S(1)}, bf16[8,32,1024]{2,1,0:T(8,128)(2,1)S(1)}, u32[]{:S(2)}, u32[]{:S(2)}) collective-permute-start(bf16[8,32,1024]{2,1,0:T(8,128)(2,1)S(1)} %all-to-all-done.refs_0_), channel_id=1, source_target_pairs={{0,22},{2,0},{4,2},{6,4},{8,6},{10,8},{12,10},{14,12},{16,14},{18,... | collective-permute-start | bytes 1572872 | tf_op jit(solution)/shard_map/ppermute | solution.py:242
  80.5 15.0 %collective-permute-start.5 = (bf16[8,32,1024]{2,1,0:T(8,128)(2,1)S(1)}, bf16[8,32,1024]{2,1,0:T(8,128)(2,1)S(1)}, u32[]{:S(2)}, u32[]{:S(2)}) collective-permute-start(bf16[8,32,1024]{2,1,0:T(8,128)(2,1)S(1)} %all-to-all-done.refs_0_), channel_id=1, source_target_pairs={{0,2},{2,4},{4,6},{6,8},{8,10},{10,12},{12,14},{14,16},{16,18},{18... | collective-permute-start | bytes 1572872 | tf_op jit(solution)/shard_map/ppermute | solution.py:242
  82.5 19.4 %collective-permute-start.7 = (bf16[8,32,1024]{2,1,0:T(8,128)(2,1)S(1)}, bf16[8,32,1024]{2,1,0:T(8,128)(2,1)S(1)}, u32[]{:S(2)}, u32[]{:S(2)}) collective-permute-start(bf16[8,32,1024]{2,1,0:T(8,128)(2,1)S(1)} %all-to-all-done.refs_0_), channel_id=1, source_target_pairs={{0,1},{1,0},{2,3},{3,2},{4,5},{5,4},{6,7},{7,6},{8,9},{9,8},{10,11... | collective-permute-start | bytes 1572872 | tf_op jit(solution)/shard_map/ppermute | solution.py:245
  94.4 9.3 %copy-start.7 = (bf16[8,32,1024]{2,1,0:T(8,128)(2,1)}, bf16[8,32,1024]{2,1,0:T(8,128)(2,1)S(1)}, u32[]{:S(2)}) copy-start(bf16[8,32,1024]{2,1,0:T(8,128)(2,1)S(1)} %collective-permute-done.6.refs_2_) | copy-start | bytes 1572868
  95.5 6.3 %copy-start.8 = (bf16[8,32,1024]{2,1,0:T(8,128)(2,1)}, bf16[8,32,1024]{2,1,0:T(8,128)(2,1)S(1)}, u32[]{:S(2)}) copy-start(bf16[8,32,1024]{2,1,0:T(8,128)(2,1)S(1)} %collective-permute-done.5.refs_1_) | copy-start | bytes 1572868
  95.5 6.3 %collective-permute-start.8 = (bf16[8,32,1024]{2,1,0:T(8,128)(2,1)S(1)}, bf16[8,32,1024]{2,1,0:T(8,128)(2,1)S(1)}, u32[]{:S(2)}, u32[]{:S(2)}) collective-permute-start(bf16[8,32,1024]{2,1,0:T(8,128)(2,1)S(1)} %collective-permute-done.5.refs_1_), channel_id=1, source_target_pairs={{0,1},{1,0},{2,3},{3,2},{4,5},{5,4},{6,7},{7,6},{8,9},{9,8},{10,11... | collective-permute-start | bytes 1572872 | tf_op jit(solution)/shard_map/ppermute | solution.py:245
  99.9 3.8 %collective-permute-start.9 = (bf16[8,32,1024]{2,1,0:T(8,128)(2,1)S(1)}, bf16[8,32,1024]{2,1,0:T(8,128)(2,1)S(1)}, u32[]{:S(2)}, u32[]{:S(2)}) collective-permute-start(bf16[8,32,1024]{2,1,0:T(8,128)(2,1)S(1)} %collective-permute-done.6.refs_2_), channel_id=1, source_target_pairs={{0,1},{1,0},{2,3},{3,2},{4,5},{5,4},{6,7},{7,6},{8,9},{9,8},{10,11... | collective-permute-start | bytes 1572872 | tf_op jit(solution)/shard_map/ppermute | solution.py:245
  101.8 0.8 copy-start.9
  102.6 1.1 copy-start.10
  103.7 0.8 copy-start.11
  111.3 19.2 %all-to-all-start.1 = ((bf16[4,528,256]{2,1,0:T(8,128)(2,1)}), bf16[4,528,256]{2,1,0:T(8,128)(2,1)S(1)}, u32[]{:S(2)}, u32[]{:S(2)}) async-start(bf16[4,528,256]{2,1,0:T(8,128)(2,1)} %shard_map.157), calls=%async_computation.1 | async-start | bytes 2162688 | tf_op jit(solution)/shard_map/all_to_all | solution.py:285
Sparse Core Ops, SparseCore 0:
  10.9 49.3 all-gather.4

commit v7 on v6

--- a/solution.py
+++ b/solution.py
@@ -36,17 +36,19 @@
     slots, width = gate_ref.shape[1:]
     tokens, dwidth = dgate_ref.shape
     quarter = tokens // 4
-    out_ref[...] = jnp.zeros_like(out_ref)
+    out_ref[0] = jnp.zeros_like(out_ref[0])
     activated, _ = silu_parts(gate_ref[0].astype(jnp.float32))
     hidden = activated * up_ref[0].astype(jnp.float32)
     pad = jnp.zeros((SLOT_ROWS - slots, width), jnp.float32)
-    out_ref[:SLOT_ROWS, :width] = jnp.concatenate([hidden, pad], axis=0).astype(jnp.bfloat16)
+    out_ref[0, :SLOT_ROWS, :width] = jnp.concatenate([hidden, pad], axis=0).astype(jnp.bfloat16)
     dactivated, _ = silu_parts(dgate_ref[...].astype(jnp.float32))
     dhidden = (dactivated * dup_ref[...].astype(jnp.float32)).astype(jnp.bfloat16)
     for j in range(4):
-        out_ref[SLOT_ROWS : SLOT_ROWS + quarter, j * LANES : j * LANES + dwidth] = dhidden[
+        out_ref[0, SLOT_ROWS : SLOT_ROWS + quarter, j * LANES : j * LANES + dwidth] = dhidden[
             j * quarter : (j + 1) * quarter
         ]
+    for y in range(1, out_ref.shape[0]):
+        out_ref[y] = out_ref[0]
 
 
 def pick_kernel(capacity, expert_ref, part_ref, rows_ref, prob_ref, ids_ref, slots_ref, out_ref):
@@ -216,10 +218,10 @@
 
     hidden = pl.pallas_call(
         hidden_kernel,
-        out_shape=jax.ShapeDtypeStruct((SLOT_ROWS + ne * tokens // 4, 4 * LANES), bf16),
+        out_shape=jax.ShapeDtypeStruct((ny, SLOT_ROWS + ne * tokens // 4, 4 * LANES), bf16),
         compiler_params=params(),
     )(expert_gate_pre, expert_up_pre, dense_gate_pre, dense_up_pre)
-    hiddens = lax.all_gather(hidden, "y", axis=0)
+    hiddens = lax.all_to_all(hidden, "y", split_axis=0, concat_axis=0, tiled=True)
 
     part_arr = part.reshape(1).astype(jnp.int32)
     mine = pl.pallas_call(
@@ -236,6 +238,7 @@
         compiler_params=params(),
     )(rows)
     rows, chunks = lax.optimization_barrier((rows, chunks))
+    chunks, hiddens = lax.optimization_barrier((chunks, hiddens))
     chunks = lax.all_to_all(chunks, "y", split_axis=0, concat_axis=0, tiled=True)
 
     def along(piece):

time: 140 us -> 142 us (1.014)
  starting transfers between devices: 46.6 us -> 67.3 us
  between operations: 14.3 us -> 0.88 us
  waiting for transfers between devices: 15 us -> 9.83 us
    ppermute x4, starting transfers between devices: 17 us -> 31 us  [along(): lax.ppermute(piece, ('e', 'l'), ring(ne * RUN, d))]
    all_to_all x0 -> x1, starting transfers between devices: none -> 7.65 us  [local(): lax.all_to_all(hidden, 'y', split_axis=0, concat_axis=0, tiled=True)]
    all_to_all x1, waiting for transfers between devices: 7.22 us -> 0.01 us  [local(): lax.all_to_all(chunks, 'y', split_axis=0, concat_axis=0, tiled=True)]
    all_to_all x1, starting transfers between devices: 6.83 us -> 4.84 us  [local(): lax.all_to_all(chunks, 'y', split_axis=0, concat_axis=0, tiled=True)]
  transfers between devices with their start and end apart: 13 -> 13, of which waited for: 5 -> 4; matrix products, arithmetic and copies ran while one was open for 0% -> 0% of each run, Pallas kernels for 11% -> 11%
where the time goes in v7:
time: 142 us; the launch traced here: 141 us
  starting transfers between devices  67.3 us (47%)
  blocking collectives  33.6 us (24%)
  Pallas kernels  25 us (18%)
  waiting for transfers between devices  9.83 us (7%)
  local copies, waits for them, and re-layouts  2.4 us (2%)
  other arithmetic  2.04 us (1%)
    ppermute x4, starting transfers between devices, along(): lax.ppermute(piece, ('e', 'l'), ring(ne * RUN, d))  31 us
    all_gather x1, blocking collectives, local(): rows = lax.all_gather(mine, 'e', axis=0, tiled=True)  27.2 us
    ppermute x6, starting transfers between devices, other(): return pieces + [lax.ppermute(p, 'c', ring(CORES, 1)) for p in pieces]  19.7 us
    pallas_call x1, Pallas kernels, local(): pl.pallas_call(product_kernel, grid=(width // depth,), out_shape=(jax.Sha...  8.41 us
    all_to_all x1, starting transfers between devices, local(): lax.all_to_all(hidden, 'y', split_axis=0, concat_axis=0, tiled=True)  7.65 us
    pallas_call x1, Pallas kernels, local(): pl.pallas_call(functools.partial(weight_kernel, block), out_shape=jax.Sha...  6.77 us
    all_gather x1, blocking collectives, local(): all_dots = lax.all_gather(dots, ('l', 'c'), axis=0)  6.38 us
    all_to_all x1, waiting for transfers between devices, local(): lax.all_to_all(partial_sums, 'x', split_axis=0, concat_axis=0, tiled=True)  5.08 us
  transfers between devices with their start and end apart: 13, of which 4 were waited for; matrix products, arithmetic and copies ran while one was open for 0% of the time, Pallas kernels for 11%

profile of v7, /device:TPU:1, one launch (start us, length us, event | category | flops | bytes accessed | tf_op | source)
XLA Modules:
  0.0 141.0 jit_solution(8990683511799289739)
XLA Ops:
  0.6 2.5 %shard_map.155 = bf16[8,208,512]{2,1,0:T(8,128)(2,1)} custom-call(bf16[1,156,416]{2,1,0:T(8,128)(2,1)} %refs_8_.1, bf16[1,156,416]{2,1,0:T(8,128)(2,1)} %refs_9_.1, bf16[192,104]{1,0:T(8,128)(2,1)} %refs_10_.1, bf16[192,104]{1,0:T(8,128)(2,1)} %refs_11_.1), custom_call_target="tpu_custom_call" | custom-call | tf_op jit(solution)/shard_map/pallas_call | solution.py:219
  3.1 7.7 %all-to-all-start = ((bf16[8,208,512]{2,1,0:T(8,128)(2,1)}), bf16[8,208,512]{2,1,0:T(8,128)(2,1)S(1)}, u32[]{:S(2)}, u32[]{:S(2)}) async-start(bf16[8,208,512]{2,1,0:T(8,128)(2,1)} %shard_map.155), calls=%async_computation | async-start | bytes 3407872 | tf_op jit(solution)/shard_map/all_to_all | solution.py:224
  10.7 2.0 %shard_map.153 = bf16[8,7296]{1,0:T(8,128)(2,1)} custom-call(s32[1]{0:T(128)} %bitcast.expert_ref, s32[1]{0:T(128)} %bitcast.1.part_ref, bf16[48,7168]{1,0:T(8,128)(2,1)} %rows_ref.1, bf16[2,48]{1,0:T(2,128)(2,1)} %bitcast.21, s32[2,48]{1,0:T(2,128)} %bitcast.17, s32[2,48]{1,0:T(2,128)} %bitcast.18), custom_call_target="tpu_custom_call" | custom-call | tf_op jit(solution)/shard_map/pallas_call | solution.py:227
  12.7 27.2 %all_gather.9.rows_ref.refs_0_ = bf16[32,7296]{1,0:T(8,128)(2,1)} all-gather(bf16[8,7296]{1,0:T(8,128)(2,1)} %shard_map.153), channel_id=1, replica_groups=mesh['x'=4,'y'=8,'e'=4,'l'=3,'c'=2] {'e'}, dimensions={0}, use_global_device_ids=true | all-gather | bytes 583680 | tf_op jit(solution)/shard_map/all_gather | solution.py:233
  40.0 0.0 copy-start
  40.0 2.2 %shard_map.154 = bf16[8,32,1024]{2,1,0:T(8,128)(2,1)} custom-call(bf16[32,7296]{1,0:T(8,128)(2,1)} %all_gather.9.rows_ref.refs_0_), custom_call_target="tpu_custom_call" | custom-call | tf_op jit(solution)/shard_map/pallas_call | solution.py:235
  42.2 6.1 %collective-permute-start.1 = (bf16[32,7296]{1,0:T(8,128)(2,1)}, bf16[32,7296]{1,0:T(8,128)(2,1)S(1)}, u32[]{:S(2)}, u32[]{:S(2)}) collective-permute-start(bf16[32,7296]{1,0:T(8,128)(2,1)} %all_gather.9.rows_ref.refs_0_), channel_id=1, source_target_pairs={{0,22},{2,0},{4,2},{6,4},{8,6},{10,8},{12,10},{14,12},{16,14},{18,... | collective-permute-start | bytes 1400840 | tf_op jit(solution)/shard_map/ppermute | solution.py:245
  48.4 1.9 %collective-permute-start = (bf16[32,7296]{1,0:T(8,128)(2,1)}, bf16[32,7296]{1,0:T(8,128)(2,1)}, u32[]{:S(2)}, u32[]{:S(2)}) collective-permute-start(bf16[32,7296]{1,0:T(8,128)(2,1)} %all_gather.9.rows_ref.refs_0_), channel_id=1, source_target_pairs={{0,2},{2,4},{4,6},{6,8},{8,10},{10,12},{12,14},{14,16},{16,18},{18... | collective-permute-start | bytes 1400840 | tf_op jit(solution)/shard_map/ppermute | solution.py:245
  50.3 0.0 all-to-all-done.refs_6_
  50.3 0.0 copy-start.1
  50.3 4.8 %all-to-all-start.1 = ((bf16[8,32,1024]{2,1,0:T(8,128)(2,1)}), bf16[8,32,1024]{2,1,0:T(8,128)(2,1)S(1)}, u32[]{:S(2)}, u32[]{:S(2)}) async-start(bf16[8,32,1024]{2,1,0:T(8,128)(2,1)} %shard_map.154), calls=%async_computation.1 | async-start | bytes 1048576 | tf_op jit(solution)/shard_map/all_to_all | solution.py:242
  55.2 0.0 copy-done
  55.2 6.3 %collective-permute-start.2 = (bf16[32,7296]{1,0:T(8,128)(2,1)S(1)}, bf16[32,7296]{1,0:T(8,128)(2,1)S(1)}, u32[]{:S(2)}, u32[]{:S(2)}) collective-permute-start(bf16[32,7296]{1,0:T(8,128)(2,1)S(1)} %copy-done), channel_id=1, source_target_pairs={{0,1},{1,0},{2,3},{3,2},{4,5},{5,4},{6,7},{7,6},{8,9},{9,8},{10,11... | collective-permute-start | bytes 1400840 | tf_op jit(solution)/shard_map/ppermute | solution.py:248
  61.5 0.0 collective-permute-done.1.refs_2_
  61.5 0.0 copy-start.3
  61.5 1.9 %collective-permute-start.4 = (bf16[32,7296]{1,0:T(8,128)(2,1)S(1)}, bf16[32,7296]{1,0:T(8,128)(2,1)S(1)}, u32[]{:S(2)}, u32[]{:S(2)}) collective-permute-start(bf16[32,7296]{1,0:T(8,128)(2,1)S(1)} %collective-permute-done.1.refs_2_), channel_id=1, source_target_pairs={{0,1},{1,0},{2,3},{3,2},{4,5},{5,4},{6,7},{7,6},{8,9},{9,8},{10,11... | collective-permute-start | bytes 1400840 | tf_op jit(solution)/shard_map/ppermute | solution.py:248
  63.5 0.0 collective-permute-done.refs_1_
  63.5 3.3 %collective-permute-start.3 = (bf16[32,7296]{1,0:T(8,128)(2,1)}, bf16[32,7296]{1,0:T(8,128)(2,1)}, u32[]{:S(2)}, u32[]{:S(2)}) collective-permute-start(bf16[32,7296]{1,0:T(8,128)(2,1)} %collective-permute-done.refs_1_), channel_id=1, source_target_pairs={{0,1},{1,0},{2,3},{3,2},{4,5},{5,4},{6,7},{7,6},{8,9},{9,8},{10,11... | collective-permute-start | bytes 1400840 | tf_op jit(solution)/shard_map/ppermute | solution.py:248
  66.8 0.0 collective-permute-done.2.refs_3_
  66.8 0.0 copy-start.4
  66.8 0.0 collective-permute-done.4.refs_5_
  66.8 0.8 copy-done.4
  67.6 0.0 copy-start.5
  67.6 0.8 copy-done.5
  68.4 0.2 collective-permute-done.3.refs_4_
  68.6 0.0 all-to-all-done.1.refs_0_
  68.6 0.0 copy-start.2
  68.6 21.1 %collective-permute-start.6 = (bf16[8,32,1024]{2,1,0:T(8,128)(2,1)S(1)}, bf16[8,32,1024]{2,1,0:T(8,128)(2,1)S(1)}, u32[]{:S(2)}, u32[]{:S(2)}) collective-permute-start(bf16[8,32,1024]{2,1,0:T(8,128)(2,1)S(1)} %all-to-all-done.1.refs_0_), channel_id=1, source_target_pairs={{0,22},{2,0},{4,2},{6,4},{8,6},{10,8},{12,10},{14,12},{16,14},{18,... | collective-permute-start | bytes 1572872 | tf_op jit(solution)/shard_map/ppermute | solution.py:245
  89.7 1.9 %collective-permute-start.5 = (bf16[8,32,1024]{2,1,0:T(8,128)(2,1)S(1)}, bf16[8,32,1024]{2,1,0:T(8,128)(2,1)S(1)}, u32[]{:S(2)}, u32[]{:S(2)}) collective-permute-start(bf16[8,32,1024]{2,1,0:T(8,128)(2,1)S(1)} %all-to-all-done.1.refs_0_), channel_id=1, source_target_pairs={{0,2},{2,4},{4,6},{6,8},{8,10},{10,12},{12,14},{14,16},{16,18},{18... | collective-permute-start | bytes 1572872 | tf_op jit(solution)/shard_map/ppermute | solution.py:245
  91.6 2.7 %collective-permute-start.7 = (bf16[8,32,1024]{2,1,0:T(8,128)(2,1)S(1)}, bf16[8,32,1024]{2,1,0:T(8,128)(2,1)S(1)}, u32[]{:S(2)}, u32[]{:S(2)}) collective-permute-start(bf16[8,32,1024]{2,1,0:T(8,128)(2,1)S(1)} %all-to-all-done.1.refs_0_), channel_id=1, source_target_pairs={{0,1},{1,0},{2,3},{3,2},{4,5},{5,4},{6,7},{7,6},{8,9},{9,8},{10,11... | collective-permute-start | bytes 1572872 | tf_op jit(solution)/shard_map/ppermute | solution.py:248
  94.3 0.0 copy-done.3
  94.3 8.4 %shard_map.156 = (f32[192,416]{1,0:T(8,128)}, f32[192,104]{1,0:T(8,128)}) custom-call(bf16[32,7296]{1,0:T(8,128)(2,1)} %all_gather.9.rows_ref.refs_0_, bf16[32,7296]{1,0:T(8,128)(2,1)} %collective-permute-done.refs_1_, bf16[32,7296]{1,0:T(8,128)(2,1)} %copy-done.3, bf16[32,7296]{1,0:T(8,128)(2,1)} %copy-done.4, ...), custom_call_target="tpu_custom_call" | custom-call | tf_op jit(solution)/shard_map/pallas_call | solution.py:254
  102.7 0.0 copy-done.1
  102.7 0.0 copy-done.2
  102.7 0.0 collective-permute-done.6.refs_2_
  102.7 0.0 copy-start.6
  102.7 2.7 %collective-permute-done.5.refs_1_ = bf16[8,32,1024]{2,1,0:T(8,128)(2,1)S(1)} collective-permute-done((bf16[8,32,1024]{2,1,0:T(8,128)(2,1)S(1)}, bf16[8,32,1024]{2,1,0:T(8,128)(2,1)S(1)}, u32[]{:S(2)}, u32[]{:S(2)}) %collective-permute-start.5) | collective-permute-done | bytes 524320 | tf_op jit(solution)/shard_map/ppermute | solution.py:245
  105.5 0.0 copy-start.7
  105.5 3.5 %collective-permute-start.8 = (bf16[8,32,1024]{2,1,0:T(8,128)(2,1)S(1)}, bf16[8,32,1024]{2,1,0:T(8,128)(2,1)S(1)}, u32[]{:S(2)}, u32[]{:S(2)}) collective-permute-start(bf16[8,32,1024]{2,1,0:T(8,128)(2,1)S(1)} %collective-permute-done.5.refs_1_), channel_id=1, source_target_pairs={{0,1},{1,0},{2,3},{3,2},{4,5},{5,4},{6,7},{7,6},{8,9},{9,8},{10,11... | collective-permute-start | bytes 1572872 | tf_op jit(solution)/shard_map/ppermute | solution.py:248
  109.0 1.9 %collective-permute-start.9 = (bf16[8,32,1024]{2,1,0:T(8,128)(2,1)S(1)}, bf16[8,32,1024]{2,1,0:T(8,128)(2,1)S(1)}, u32[]{:S(2)}, u32[]{:S(2)}) collective-permute-start(bf16[8,32,1024]{2,1,0:T(8,128)(2,1)S(1)} %collective-permute-done.6.refs_2_), channel_id=1, source_target_pairs={{0,1},{1,0},{2,3},{3,2},{4,5},{5,4},{6,7},{7,6},{8,9},{9,8},{10,11... | collective-permute-start | bytes 1572872 | tf_op jit(solution)/shard_map/ppermute | solution.py:248
  110.9 0.0 collective-permute-done.7.refs_3_
  111.0 0.0 copy-start.8
  111.0 0.0 collective-permute-done.8.refs_4_
  111.0 0.0 copy-start.9
  111.0 1.8 %collective-permute-done.9.refs_5_ = bf16[8,32,1024]{2,1,0:T(8,128)(2,1)S(1)} collective-permute-done((bf16[8,32,1024]{2,1,0:T(8,128)(2,1)S(1)}, bf16[8,32,1024]{2,1,0:T(8,128)(2,1)S(1)}, u32[]{:S(2)}, u32[]{:S(2)}) %collective-permute-start.9) | collective-permute-done | bytes 524320 | tf_op jit(solution)/shard_map/ppermute | solution.py:248
  112.8 0.0 copy-done.6
  112.8 0.0 copy-done.7
  112.8 0.0 copy-done.8
  112.8 0.0 copy-done.9
  112.8 0.0 copy-start.10
  112.8 0.8 copy-done.10
  113.6 6.8 %shard_map.157 = bf16[4,528,256]{2,1,0:T(8,128)(2,1)} custom-call(s32[1]{0:T(128)} %bitcast.expert_ref, bf16[8,32,1024]{2,1,0:T(8,128)(2,1)} %copy-done.2, bf16[8,32,1024]{2,1,0:T(8,128)(2,1)} %copy-done.7, bf16[8,32,1024]{2,1,0:T(8,128)(2,1)} %copy-done.6, bf16[8,32,1024]{2,1,0:T(8,128)(2,1)} %copy-done.8, bf16[8,32,1024]{2,1,0:T(8,128)(2,1)} %copy-done.9, ...), custom_call_target="tpu_custom_call" | custom-call | tf_op jit(solution)/shard_map/pallas_call | solution.py:276
  120.4 4.0 %all-to-all-start.2 = ((bf16[4,528,256]{2,1,0:T(8,128)(2,1)}), bf16[4,528,256]{2,1,0:T(8,128)(2,1)S(1)}, u32[]{:S(2)}, u32[]{:S(2)}) async-start(bf16[4,528,256]{2,1,0:T(8,128)(2,1)} %shard_map.157), calls=%async_computation.2 | async-start | bytes 2162688 | tf_op jit(solution)/shard_map/all_to_all | solution.py:288
  124.4 3.1 %shard_map.158 = (bf16[1,156,416]{2,1,0:T(8,128)(2,1)}, bf16[1,156,416]{2,1,0:T(8,128)(2,1)}, f32[1,156]{1,0:T(1,128)}, bf16[192,104]{1,0:T(8,128)(2,1)}, bf16[192,104]{1,0:T(8,128)(2,1)}) custom-call(s32[1]{0:T(128)} %bitcast.expert_ref, bf16[32,7296]{1,0:T(8,128)(2,1)} %all_gather.9.rows_ref.refs_0_, bf16[32,7296]{1,0:T(8,128)(2,1)} %collective-permute-done.refs_1_, ...), custom_call_target="tpu_custom_call" | custom-call | tf_op jit(solution)/shard_map/pallas_call | solution.py:291
  127.5 6.4 %all-gather.1 = f32[6,1,156]{2,1,0:T(1,128)S(1)} all-gather(f32[1,1,156]{2,1,0:T(1,128)} %bitcast.20), channel_id=2, replica_groups=mesh['x'=4,'y'=8,'e'=4,'l'=3,'c'=2] {'l','c'}, dimensions={0}, use_global_device_ids=true | all-gather | bytes 4368 | tf_op jit(solution)/shard_map/all_gather | solution.py:329
  133.9 0.6 reduce.1
  134.5 5.1 %all-to-all-done.2 = bf16[4,528,256]{2,1,0:T(8,128)(2,1)S(1)} async-done(((bf16[4,528,256]{2,1,0:T(8,128)(2,1)}), bf16[4,528,256]{2,1,0:T(8,128)(2,1)S(1)}, u32[]{:S(2)}, u32[]{:S(2)}) %all-to-all-start.2) | async-done | bytes 1081376 | tf_op jit(solution)/shard_map/all_to_all | solution.py:288
  139.6 0.7 fusion.1
  140.2 0.8 fusion
Async XLA Ops:
  3.1 47.2 %all-to-all-start = ((bf16[8,208,512]{2,1,0:T(8,128)(2,1)}), bf16[8,208,512]{2,1,0:T(8,128)(2,1)S(1)}, u32[]{:S(2)}, u32[]{:S(2)}) async-start(bf16[8,208,512]{2,1,0:T(8,128)(2,1)} %shard_map.155), calls=%async_computation | async-start | bytes 3407872 | tf_op jit(solution)/shard_map/all_to_all | solution.py:224
  40.0 15.2 %copy-start = (bf16[32,7296]{1,0:T(8,128)(2,1)S(1)}, bf16[32,7296]{1,0:T(8,128)(2,1)}, u32[]{:S(2)}) copy-start(bf16[32,7296]{1,0:T(8,128)(2,1)} %all_gather.9.rows_ref.refs_0_) | copy-start | bytes 1400836
  42.2 19.3 %collective-permute-start.1 = (bf16[32,7296]{1,0:T(8,128)(2,1)}, bf16[32,7296]{1,0:T(8,128)(2,1)S(1)}, u32[]{:S(2)}, u32[]{:S(2)}) collective-permute-start(bf16[32,7296]{1,0:T(8,128)(2,1)} %all_gather.9.rows_ref.refs_0_), channel_id=1, source_target_pairs={{0,22},{2,0},{4,2},{6,4},{8,6},{10,8},{12,10},{14,12},{16,14},{18,... | collective-permute-start | bytes 1400840 | tf_op jit(solution)/shard_map/ppermute | solution.py:245
  48.4 15.1 %collective-permute-start = (bf16[32,7296]{1,0:T(8,128)(2,1)}, bf16[32,7296]{1,0:T(8,128)(2,1)}, u32[]{:S(2)}, u32[]{:S(2)}) collective-permute-start(bf16[32,7296]{1,0:T(8,128)(2,1)} %all_gather.9.rows_ref.refs_0_), channel_id=1, source_target_pairs={{0,2},{2,4},{4,6},{6,8},{8,10},{10,12},{12,14},{14,16},{16,18},{18... | collective-permute-start | bytes 1400840 | tf_op jit(solution)/shard_map/ppermute | solution.py:245
  50.3 52.4 %copy-start.1 = (bf16[8,208,512]{2,1,0:T(8,128)(2,1)}, bf16[8,208,512]{2,1,0:T(8,128)(2,1)S(1)}, u32[]{:S(2)}) copy-start(bf16[8,208,512]{2,1,0:T(8,128)(2,1)S(1)} %all-to-all-done.refs_6_) | copy-start | bytes 5111812
  50.3 18.3 %all-to-all-start.1 = ((bf16[8,32,1024]{2,1,0:T(8,128)(2,1)}), bf16[8,32,1024]{2,1,0:T(8,128)(2,1)S(1)}, u32[]{:S(2)}, u32[]{:S(2)}) async-start(bf16[8,32,1024]{2,1,0:T(8,128)(2,1)} %shard_map.154), calls=%async_computation.1 | async-start | bytes 1048576 | tf_op jit(solution)/shard_map/all_to_all | solution.py:242
  55.2 11.6 %collective-permute-start.2 = (bf16[32,7296]{1,0:T(8,128)(2,1)S(1)}, bf16[32,7296]{1,0:T(8,128)(2,1)S(1)}, u32[]{:S(2)}, u32[]{:S(2)}) collective-permute-start(bf16[32,7296]{1,0:T(8,128)(2,1)S(1)} %copy-done), channel_id=1, source_target_pairs={{0,1},{1,0},{2,3},{3,2},{4,5},{5,4},{6,7},{7,6},{8,9},{9,8},{10,11... | collective-permute-start | bytes 1400840 | tf_op jit(solution)/shard_map/ppermute | solution.py:248
  61.5 32.8 %copy-start.3 = (bf16[32,7296]{1,0:T(8,128)(2,1)}, bf16[32,7296]{1,0:T(8,128)(2,1)S(1)}, u32[]{:S(2)}) copy-start(bf16[32,7296]{1,0:T(8,128)(2,1)S(1)} %collective-permute-done.1.refs_2_) | copy-start | bytes 1400836
  61.5 5.3 %collective-permute-start.4 = (bf16[32,7296]{1,0:T(8,128)(2,1)S(1)}, bf16[32,7296]{1,0:T(8,128)(2,1)S(1)}, u32[]{:S(2)}, u32[]{:S(2)}) collective-permute-start(bf16[32,7296]{1,0:T(8,128)(2,1)S(1)} %collective-permute-done.1.refs_2_), channel_id=1, source_target_pairs={{0,1},{1,0},{2,3},{3,2},{4,5},{5,4},{6,7},{7,6},{8,9},{9,8},{10,11... | collective-permute-start | bytes 1400840 | tf_op jit(solution)/shard_map/ppermute | solution.py:248
  63.5 5.1 %collective-permute-start.3 = (bf16[32,7296]{1,0:T(8,128)(2,1)}, bf16[32,7296]{1,0:T(8,128)(2,1)}, u32[]{:S(2)}, u32[]{:S(2)}) collective-permute-start(bf16[32,7296]{1,0:T(8,128)(2,1)} %collective-permute-done.refs_1_), channel_id=1, source_target_pairs={{0,1},{1,0},{2,3},{3,2},{4,5},{5,4},{6,7},{7,6},{8,9},{9,8},{10,11... | collective-permute-start | bytes 1400840 | tf_op jit(solution)/shard_map/ppermute | solution.py:248
  66.8 0.8 copy-start.4
  67.6 0.8 copy-start.5
  68.6 34.1 %copy-start.2 = (bf16[8,32,1024]{2,1,0:T(8,128)(2,1)}, bf16[8,32,1024]{2,1,0:T(8,128)(2,1)S(1)}, u32[]{:S(2)}) copy-start(bf16[8,32,1024]{2,1,0:T(8,128)(2,1)S(1)} %all-to-all-done.1.refs_0_) | copy-start | bytes 1572868
  68.6 34.1 %collective-permute-start.6 = (bf16[8,32,1024]{2,1,0:T(8,128)(2,1)S(1)}, bf16[8,32,1024]{2,1,0:T(8,128)(2,1)S(1)}, u32[]{:S(2)}, u32[]{:S(2)}) collective-permute-start(bf16[8,32,1024]{2,1,0:T(8,128)(2,1)S(1)} %all-to-all-done.1.refs_0_), channel_id=1, source_target_pairs={{0,22},{2,0},{4,2},{6,4},{8,6},{10,8},{12,10},{14,12},{16,14},{18,... | collective-permute-start | bytes 1572872 | tf_op jit(solution)/shard_map/ppermute | solution.py:245
  89.7 15.8 %collective-permute-start.5 = (bf16[8,32,1024]{2,1,0:T(8,128)(2,1)S(1)}, bf16[8,32,1024]{2,1,0:T(8,128)(2,1)S(1)}, u32[]{:S(2)}, u32[]{:S(2)}) collective-permute-start(bf16[8,32,1024]{2,1,0:T(8,128)(2,1)S(1)} %all-to-all-done.1.refs_0_), channel_id=1, source_target_pairs={{0,2},{2,4},{4,6},{6,8},{8,10},{10,12},{12,14},{14,16},{16,18},{18... | collective-permute-start | bytes 1572872 | tf_op jit(solution)/shard_map/ppermute | solution.py:245
  91.6 19.4 %collective-permute-start.7 = (bf16[8,32,1024]{2,1,0:T(8,128)(2,1)S(1)}, bf16[8,32,1024]{2,1,0:T(8,128)(2,1)S(1)}, u32[]{:S(2)}, u32[]{:S(2)}) collective-permute-start(bf16[8,32,1024]{2,1,0:T(8,128)(2,1)S(1)} %all-to-all-done.1.refs_0_), channel_id=1, source_target_pairs={{0,1},{1,0},{2,3},{3,2},{4,5},{5,4},{6,7},{7,6},{8,9},{9,8},{10,11... | collective-permute-start | bytes 1572872 | tf_op jit(solution)/shard_map/ppermute | solution.py:248
  102.7 10.1 %copy-start.6 = (bf16[8,32,1024]{2,1,0:T(8,128)(2,1)}, bf16[8,32,1024]{2,1,0:T(8,128)(2,1)S(1)}, u32[]{:S(2)}) copy-start(bf16[8,32,1024]{2,1,0:T(8,128)(2,1)S(1)} %collective-permute-done.6.refs_2_) | copy-start | bytes 1572868
  105.5 7.4 %copy-start.7 = (bf16[8,32,1024]{2,1,0:T(8,128)(2,1)}, bf16[8,32,1024]{2,1,0:T(8,128)(2,1)S(1)}, u32[]{:S(2)}) copy-start(bf16[8,32,1024]{2,1,0:T(8,128)(2,1)S(1)} %collective-permute-done.5.refs_1_) | copy-start | bytes 1572868
  105.5 5.5 %collective-permute-start.8 = (bf16[8,32,1024]{2,1,0:T(8,128)(2,1)S(1)}, bf16[8,32,1024]{2,1,0:T(8,128)(2,1)S(1)}, u32[]{:S(2)}, u32[]{:S(2)}) collective-permute-start(bf16[8,32,1024]{2,1,0:T(8,128)(2,1)S(1)} %collective-permute-done.5.refs_1_), channel_id=1, source_target_pairs={{0,1},{1,0},{2,3},{3,2},{4,5},{5,4},{6,7},{7,6},{8,9},{9,8},{10,11... | collective-permute-start | bytes 1572872 | tf_op jit(solution)/shard_map/ppermute | solution.py:248
  109.0 3.8 %collective-permute-start.9 = (bf16[8,32,1024]{2,1,0:T(8,128)(2,1)S(1)}, bf16[8,32,1024]{2,1,0:T(8,128)(2,1)S(1)}, u32[]{:S(2)}, u32[]{:S(2)}) collective-permute-start(bf16[8,32,1024]{2,1,0:T(8,128)(2,1)S(1)} %collective-permute-done.6.refs_2_), channel_id=1, source_target_pairs={{0,1},{1,0},{2,3},{3,2},{4,5},{5,4},{6,7},{7,6},{8,9},{9,8},{10,11... | collective-permute-start | bytes 1572872 | tf_op jit(solution)/shard_map/ppermute | solution.py:248
  111.0 1.9 %copy-start.8 = (bf16[8,32,1024]{2,1,0:T(8,128)(2,1)}, bf16[8,32,1024]{2,1,0:T(8,128)(2,1)S(1)}, u32[]{:S(2)}) copy-start(bf16[8,32,1024]{2,1,0:T(8,128)(2,1)S(1)} %collective-permute-done.7.refs_3_) | copy-start | bytes 1572868
  111.0 1.9 %copy-start.9 = (bf16[8,32,1024]{2,1,0:T(8,128)(2,1)}, bf16[8,32,1024]{2,1,0:T(8,128)(2,1)S(1)}, u32[]{:S(2)}) copy-start(bf16[8,32,1024]{2,1,0:T(8,128)(2,1)S(1)} %collective-permute-done.8.refs_4_) | copy-start | bytes 1572868
  112.8 0.8 copy-start.10
  120.4 19.1 %all-to-all-start.2 = ((bf16[4,528,256]{2,1,0:T(8,128)(2,1)}), bf16[4,528,256]{2,1,0:T(8,128)(2,1)S(1)}, u32[]{:S(2)}, u32[]{:S(2)}) async-start(bf16[4,528,256]{2,1,0:T(8,128)(2,1)} %shard_map.157), calls=%async_computation.2 | async-start | bytes 2162688 | tf_op jit(solution)/shard_map/all_to_all | solution.py:288

commit v8 on v3

--- a/solution.py
+++ b/solution.py
@@ -36,17 +36,19 @@
     slots, width = gate_ref.shape[1:]
     tokens, dwidth = dgate_ref.shape
     quarter = tokens // 4
-    out_ref[...] = jnp.zeros_like(out_ref)
+    out_ref[0] = jnp.zeros_like(out_ref[0])
     activated, _ = silu_parts(gate_ref[0].astype(jnp.float32))
     hidden = activated * up_ref[0].astype(jnp.float32)
     pad = jnp.zeros((SLOT_ROWS - slots, width), jnp.float32)
-    out_ref[:SLOT_ROWS, :width] = jnp.concatenate([hidden, pad], axis=0).astype(jnp.bfloat16)
+    out_ref[0, :SLOT_ROWS, :width] = jnp.concatenate([hidden, pad], axis=0).astype(jnp.bfloat16)
     dactivated, _ = silu_parts(dgate_ref[...].astype(jnp.float32))
     dhidden = (dactivated * dup_ref[...].astype(jnp.float32)).astype(jnp.bfloat16)
     for j in range(4):
-        out_ref[SLOT_ROWS : SLOT_ROWS + quarter, j * LANES : j * LANES + dwidth] = dhidden[
+        out_ref[0, SLOT_ROWS : SLOT_ROWS + quarter, j * LANES : j * LANES + dwidth] = dhidden[
             j * quarter : (j + 1) * quarter
         ]
+    for y in range(1, out_ref.shape[0]):
+        out_ref[y] = out_ref[0]
 
 
 def pick_kernel(capacity, nx, ny, expert_ref, part_ref, rows_ref, prob_ref, ids_ref, slots_ref, out_ref, cols_ref):
@@ -136,17 +138,6 @@
         out_ref[x, width:, :] = dsummed[: height - width, x * stride : (x + 1) * stride]
 
 
-def sum_kernel(scale, in_ref, dots_ref, expert_ref, dense_ref, dots_out):
-    dots_out[...] = jnp.sum(dots_ref[...], axis=0)
-    summed = in_ref[0].astype(jnp.float32)
-    for x in range(1, in_ref.shape[0]):
-        summed = summed + in_ref[x].astype(jnp.float32)
-    summed = (summed * scale).astype(jnp.bfloat16)
-    width, block = expert_ref.shape
-    expert_ref[...] = summed[:width, :block]
-    dense_ref[...] = summed[width : width + dense_ref.shape[0], :block]
-
-
 def place(onehot, values):
     high = values.astype(jnp.bfloat16)
     rest = values - high.astype(jnp.float32)
@@ -233,10 +224,9 @@
 
     hidden = pl.pallas_call(
         hidden_kernel,
-        out_shape=jax.ShapeDtypeStruct((SLOT_ROWS + ne * tokens // 4, 4 * LANES), bf16),
+        out_shape=jax.ShapeDtypeStruct((ny, SLOT_ROWS + ne * tokens // 4, 4 * LANES), bf16),
         compiler_params=params(),
     )(expert_gate_pre, expert_up_pre, dense_gate_pre, dense_up_pre)
-    hiddens = lax.all_gather(hidden, "y", axis=0)
 
     part_arr = part.reshape(1).astype(jnp.int32)
     span = nx * stride
@@ -250,6 +240,8 @@
         compiler_params=params(),
     )(expert_arr, part_arr, grad_out, gate_prob.T, expert_ids.T, slot_positions.T)
     cols = lax.all_to_all(cols, "y", split_axis=0, concat_axis=0, tiled=True)
+    cols, hidden = lax.optimization_barrier((cols, hidden))
+    hiddens = lax.all_to_all(hidden, "y", split_axis=0, concat_axis=0, tiled=True)
     packed = pl.pallas_call(
         pack_kernel,
         out_shape=jax.ShapeDtypeStruct((eighth, ny * span + width + LANES), bf16),
@@ -329,15 +321,14 @@
     )
 
     all_dots = lax.all_gather(dots, ("l", "c"), axis=0)
-    expert_down_grad, dense_down_grad, slot_prob_grad = pl.pallas_call(
-        functools.partial(sum_kernel, 1.0 / (nx * ny)),
-        out_shape=(
-            jax.ShapeDtypeStruct((hwidth, block), bf16),
-            jax.ShapeDtypeStruct((dwidth, block), bf16),
-            jax.ShapeDtypeStruct((1, slots), jnp.float32),
-        ),
-        compiler_params=params(),
-    )(landed, all_dots)
+
+    def total(top, count):
+        parts = [landed[x, top : top + count, :block].astype(jnp.float32) for x in range(nx)]
+        return (sum(parts[1:], parts[0]) * (1.0 / (nx * ny))).astype(bf16)
+
+    expert_down_grad = total(0, hwidth)
+    dense_down_grad = total(hwidth, dwidth)
+    slot_prob_grad = jnp.sum(all_dots, axis=0)
     return (
         gate_grad,
         up_grad,

time: 141 us -> 128 us (0.908)
  blocking collectives: 54.7 us -> 40.3 us
  between operations: 14.1 us -> 0.74 us
  waiting for transfers between devices: 10.5 us -> 19.4 us
  starting transfers between devices: 33.8 us -> 39.6 us
  other arithmetic: 0 us -> 2.04 us
  Pallas kernels: 24.4 us -> 22.9 us
    all_to_all x1 -> x0, blocking collectives: 15.7 us -> none  [local(): cols = lax.all_to_all(cols, 'y', split_axis=0, concat_axis=0, tiled=True)]
    all_to_all x0 -> x2, starting transfers between devices: none -> 11.9 us  [the longest x1 7.65 us: local(): cols = lax.all_to_all(cols, 'y', split_axis=0, concat_axis=0, tiled=True)]
    all_to_all x0 -> x2, waiting for transfers between devices: none -> 5.51 us  [the longest x1 5.51 us: local(): cols = lax.all_to_all(cols, 'y', split_axis=0, concat_axis=0, tiled=True)]
    ppermute x3, starting transfers between devices: 18.9 us -> 13.9 us  [local(): pieces += [lax.ppermute(p, 'c', ring(CORES, 1)) for p in pieces]]
    ppermute x2, waiting for transfers between devices: 10.1 us -> 13.5 us  [local(): lax.ppermute(packed, ('e', 'l'), ring(ne * RUN, d))]
    all_gather x1, blocking collectives: 32 us -> 33.7 us  [local(): packed = lax.all_gather(packed, 'e', axis=0, tiled=True)]
    pallas_call x2 -> x1, Pallas kernels: 3.86 us -> 2.42 us  [local(): pl.pallas_call(hidden_kernel, out_shape=jax.ShapeDtypeStruct((ny, SLOT_RO...]
  transfers between devices with their start and end apart: 7 -> 8, of which waited for: 3 -> 4; matrix products, arithmetic and copies ran while one was open for 0% -> 0% of each run, Pallas kernels for 10% -> 11%
where the time goes in v8:
time: 128 us
  blocking collectives  40.3 us (31%)
  starting transfers between devices  39.6 us (31%)
  Pallas kernels  22.9 us (18%)
  waiting for transfers between devices  19.4 us (15%)
  local copies, waits for them, and re-layouts  2.65 us (2%)
  other arithmetic  2.04 us (2%)
    all_gather x1, blocking collectives, local(): packed = lax.all_gather(packed, 'e', axis=0, tiled=True)  33.7 us
    ppermute x3, starting transfers between devices, local(): pieces += [lax.ppermute(p, 'c', ring(CORES, 1)) for p in pieces]  13.9 us
    ppermute x2, waiting for transfers between devices, local(): lax.ppermute(packed, ('e', 'l'), ring(ne * RUN, d))  13.5 us
    pallas_call x1, Pallas kernels, local(): pl.pallas_call(back_kernel, grid=(width // depth,), out_shape=(jax.ShapeD...  9.99 us
    ppermute x2, starting transfers between devices, local(): lax.ppermute(packed, ('e', 'l'), ring(ne * RUN, d))  9.78 us
    all_to_all x1, starting transfers between devices, local(): cols = lax.all_to_all(cols, 'y', split_axis=0, concat_axis=0, tiled=True)  7.65 us
    pallas_call x1, Pallas kernels, local(): pl.pallas_call(functools.partial(weight_kernel, block, ny), grid=(1,), ou...  6.75 us
    all_gather x1, blocking collectives, local(): all_dots = lax.all_gather(dots, ('l', 'c'), axis=0)  6.64 us
  transfers between devices with their start and end apart: 8, of which 4 were waited for; matrix products, arithmetic and copies ran while one was open for 0% of the time, Pallas kernels for 11%

profile of v8, /device:TPU:1, one launch (start us, length us, event | category | flops | bytes accessed | tf_op | source)
XLA Modules:
  0.0 127.6 jit_solution(11141474804288232528)
XLA Ops:
  0.6 2.1 %shard_map.153 = (bf16[8,7296]{1,0:T(8,128)(2,1)}, bf16[8,8,1024]{2,1,0:T(8,128)(2,1)}) custom-call(s32[1]{0:T(128)} %bitcast.expert_ref, s32[1]{0:T(128)} %bitcast.1.part_ref, bf16[48,7168]{1,0:T(8,128)(2,1)} %rows_ref.1, bf16[2,48]{1,0:T(2,128)(2,1)} %bitcast.21, s32[2,48]{1,0:T(2,128)} %bitcast.17, s32[2,48]{1,0:T(2,128)} %bitcast.18), custom_call_target="tpu_custom_call" | custom-call | tf_op jit(solution)/shard_map/pallas_call | solution.py:233
  2.7 7.7 %all-to-all-start = ((bf16[8,8,1024]{2,1,0:T(8,128)(2,1)}), bf16[8,8,1024]{2,1,0:T(8,128)(2,1)S(1)}, u32[]{:S(2)}, u32[]{:S(2)}) async-start(bf16[8,8,1024]{2,1,0:T(8,128)(2,1)} %get-tuple-element.18), calls=%async_computation | async-start | bytes 262144 | tf_op jit(solution)/shard_map/all_to_all | solution.py:242
  10.4 2.4 %shard_map.154 = bf16[8,208,512]{2,1,0:T(8,128)(2,1)} custom-call(bf16[1,156,416]{2,1,0:T(8,128)(2,1)} %refs_14_.1, bf16[1,156,416]{2,1,0:T(8,128)(2,1)} %refs_15_.1, bf16[192,104]{1,0:T(8,128)(2,1)} %refs_16_.1, bf16[192,104]{1,0:T(8,128)(2,1)} %refs_17_.1), custom_call_target="tpu_custom_call" | custom-call | tf_op jit(solution)/shard_map/pallas_call | solution.py:225
  12.8 5.5 %all-to-all-done.cols_ref = bf16[8,8,1024]{2,1,0:T(8,128)(2,1)S(1)} async-done(((bf16[8,8,1024]{2,1,0:T(8,128)(2,1)}), bf16[8,8,1024]{2,1,0:T(8,128)(2,1)S(1)}, u32[]{:S(2)}, u32[]{:S(2)}) %all-to-all-start) | async-done | bytes 131104 | tf_op jit(solution)/shard_map/all_to_all | solution.py:242
  18.3 0.0 copy-start.5
  18.3 0.7 copy-done.5
  19.0 4.3 %all-to-all-start.1 = ((bf16[8,208,512]{2,1,0:T(8,128)(2,1)}), bf16[8,208,512]{2,1,0:T(8,128)(2,1)}, u32[]{:S(2)}, u32[]{:S(2)}) async-start(bf16[8,208,512]{2,1,0:T(8,128)(2,1)} %shard_map.154), calls=%async_computation.1 | async-start | bytes 3407872 | tf_op jit(solution)/shard_map/all_to_all | solution.py:244
  23.3 1.7 %shard_map.155 = bf16[8,15488]{1,0:T(8,128)(2,1)} custom-call(bf16[8,8,1024]{2,1,0:T(8,128)(2,1)} %copy-done.5, bf16[8,7296]{1,0:T(8,128)(2,1)} %get-tuple-element.20.rows_ref), custom_call_target="tpu_custom_call" | custom-call | tf_op jit(solution)/shard_map/pallas_call | solution.py:245
  24.9 33.7 %all_gather.9.refs_0_.refs_6_ = bf16[32,15488]{1,0:T(8,128)(2,1)S(1)} all-gather(bf16[8,15488]{1,0:T(8,128)(2,1)} %shard_map.155), channel_id=1, replica_groups=mesh['x'=4,'y'=8,'e'=4,'l'=3,'c'=2] {'e'}, dimensions={0}, use_global_device_ids=true | all-gather | bytes 1239040 | tf_op jit(solution)/shard_map/all_gather | solution.py:250
  58.6 0.0 copy-start
  58.6 7.9 %collective-permute-start.1 = (bf16[32,15488]{1,0:T(8,128)(2,1)S(1)}, bf16[32,15488]{1,0:T(8,128)(2,1)S(1)}, u32[]{:S(2)}, u32[]{:S(2)}) collective-permute-start(bf16[32,15488]{1,0:T(8,128)(2,1)S(1)} %all_gather.9.refs_0_.refs_6_), channel_id=1, source_target_pairs={{0,22},{2,0},{4,2},{6,4},{8,6},{10,8},{12,10},{14,12},{16,14},{18,... | collective-permute-start | bytes 2973704 | tf_op jit(solution)/shard_map/ppermute | solution.py:251
  66.5 1.9 %collective-permute-start = (bf16[32,15488]{1,0:T(8,128)(2,1)S(1)}, bf16[32,15488]{1,0:T(8,128)(2,1)S(1)}, u32[]{:S(2)}, u32[]{:S(2)}) collective-permute-start(bf16[32,15488]{1,0:T(8,128)(2,1)S(1)} %all_gather.9.refs_0_.refs_6_), channel_id=1, source_target_pairs={{0,2},{2,4},{4,6},{6,8},{8,10},{10,12},{12,14},{14,16},{16,18},{18... | collective-permute-start | bytes 2973704 | tf_op jit(solution)/shard_map/ppermute | solution.py:251
  68.4 6.1 %collective-permute-start.2 = (bf16[32,15488]{1,0:T(8,128)(2,1)S(1)}, bf16[32,15488]{1,0:T(8,128)(2,1)S(1)}, u32[]{:S(2)}, u32[]{:S(2)}) collective-permute-start(bf16[32,15488]{1,0:T(8,128)(2,1)S(1)} %all_gather.9.refs_0_.refs_6_), channel_id=1, source_target_pairs={{0,1},{1,0},{2,3},{3,2},{4,5},{5,4},{6,7},{7,6},{8,9},{9,8},{10,11... | collective-permute-start | bytes 2973704 | tf_op jit(solution)/shard_map/ppermute | solution.py:252
  74.5 12.3 %collective-permute-done.1.refs_2_.refs_8_ = bf16[32,15488]{1,0:T(8,128)(2,1)S(1)} collective-permute-done((bf16[32,15488]{1,0:T(8,128)(2,1)S(1)}, bf16[32,15488]{1,0:T(8,128)(2,1)S(1)}, u32[]{:S(2)}, u32[]{:S(2)}) %collective-permute-start.1) | collective-permute-done | bytes 991264 | tf_op jit(solution)/shard_map/ppermute | solution.py:251
  86.8 0.0 copy-start.1
  86.8 3.7 %collective-permute-start.4 = (bf16[32,15488]{1,0:T(8,128)(2,1)S(1)}, bf16[32,15488]{1,0:T(8,128)(2,1)S(1)}, u32[]{:S(2)}, u32[]{:S(2)}) collective-permute-start(bf16[32,15488]{1,0:T(8,128)(2,1)S(1)} %collective-permute-done.1.refs_2_.refs_8_), channel_id=1, source_target_pairs={{0,1},{1,0},{2,3},{3,2},{4,5},{5,4},{6,7},{7,6},{8,9},{9,8},{10,11... | collective-permute-start | bytes 2973704 | tf_op jit(solution)/shard_map/ppermute | solution.py:252
  90.5 1.3 %collective-permute-done.refs_1_.refs_7_ = bf16[32,15488]{1,0:T(8,128)(2,1)S(1)} collective-permute-done((bf16[32,15488]{1,0:T(8,128)(2,1)S(1)}, bf16[32,15488]{1,0:T(8,128)(2,1)S(1)}, u32[]{:S(2)}, u32[]{:S(2)}) %collective-permute-start) | collective-permute-done | bytes 991264 | tf_op jit(solution)/shard_map/ppermute | solution.py:251
  91.8 0.0 copy-start.2
  91.8 4.0 %collective-permute-start.3 = (bf16[32,15488]{1,0:T(8,128)(2,1)S(1)}, bf16[32,15488]{1,0:T(8,128)(2,1)}, u32[]{:S(2)}, u32[]{:S(2)}) collective-permute-start(bf16[32,15488]{1,0:T(8,128)(2,1)S(1)} %collective-permute-done.refs_1_.refs_7_), channel_id=1, source_target_pairs={{0,1},{1,0},{2,3},{3,2},{4,5},{5,4},{6,7},{7,6},{8,9},{9,8},{10,11... | collective-permute-start | bytes 2973704 | tf_op jit(solution)/shard_map/ppermute | solution.py:252
  95.9 0.0 collective-permute-done.2.refs_3_.refs_9_
  95.9 0.0 copy-start.3
  95.9 0.0 collective-permute-done.4.refs_5_.refs_11_
  95.9 0.9 copy-done.3
  96.8 0.0 copy-start.4
  96.8 1.0 copy-done.4
  97.9 0.3 collective-permute-done.3.refs_4_.refs_10_
  98.2 0.0 all-to-all-done.1.refs_6_
  98.2 0.0 copy-done
  98.2 0.0 copy-done.1
  98.2 0.0 copy-done.2
  98.2 6.8 %shard_map.156 = bf16[4,528,256]{2,1,0:T(8,128)(2,1)} custom-call(s32[1]{0:T(128)} %bitcast.expert_ref, bf16[32,15488]{1,0:T(8,128)(2,1)} %copy-done, bf16[32,15488]{1,0:T(8,128)(2,1)} %copy-done.2, bf16[32,15488]{1,0:T(8,128)(2,1)} %copy-done.1, bf16[32,15488]{1,0:T(8,128)(2,1)} %copy-done.3, bf16[32,15488]{1,0:T(8,128)(2,1)} %collective-permute-done.3.refs_4_.refs_10_, ...), custom_call_target="tpu_custom_call" | custom-call | tf_op jit(solution)/shard_map/pallas_call | solution.py:256
  104.9 4.0 %all-to-all-start.2 = ((bf16[4,528,256]{2,1,0:T(8,128)(2,1)}), bf16[4,528,256]{2,1,0:T(8,128)(2,1)S(1)}, u32[]{:S(2)}, u32[]{:S(2)}) async-start(bf16[4,528,256]{2,1,0:T(8,128)(2,1)} %shard_map.156), calls=%async_computation.2 | async-start | bytes 2162688 | tf_op jit(solution)/shard_map/all_to_all | solution.py:272
  108.9 10.0 %shard_map.157 = (bf16[1,156,416]{2,1,0:T(8,128)(2,1)}, bf16[1,156,416]{2,1,0:T(8,128)(2,1)}, f32[1,156]{1,0:T(1,128)}, bf16[192,104]{1,0:T(8,128)(2,1)}, bf16[192,104]{1,0:T(8,128)(2,1)}) custom-call(s32[1]{0:T(128)} %bitcast.expert_ref, bf16[32,15488]{1,0:T(8,128)(2,1)} %copy-done, bf16[32,15488]{1,0:T(8,128)(2,1)} %copy-done.2, ...), custom_call_target="tpu_custom_call" | custom-call | tf_op jit(solution)/shard_map/pallas_call | solution.py:278
  118.9 6.6 %all-gather.1 = f32[6,1,156]{2,1,0:T(1,128)S(1)} all-gather(f32[1,1,156]{2,1,0:T(1,128)} %bitcast.20), channel_id=2, replica_groups=mesh['x'=4,'y'=8,'e'=4,'l'=3,'c'=2] {'l','c'}, dimensions={0}, use_global_device_ids=true | all-gather | bytes 4368 | tf_op jit(solution)/shard_map/all_gather | solution.py:323
  125.6 0.6 reduce.1
  126.2 0.0 all-to-all-done.2
  126.2 0.7 fusion.1
  126.8 0.8 fusion
Async XLA Ops:
  2.7 15.6 %all-to-all-start = ((bf16[8,8,1024]{2,1,0:T(8,128)(2,1)}), bf16[8,8,1024]{2,1,0:T(8,128)(2,1)S(1)}, u32[]{:S(2)}, u32[]{:S(2)}) async-start(bf16[8,8,1024]{2,1,0:T(8,128)(2,1)} %get-tuple-element.18), calls=%async_computation | async-start | bytes 262144 | tf_op jit(solution)/shard_map/all_to_all | solution.py:242
  18.3 0.7 copy-start.5
  19.0 79.2 %all-to-all-start.1 = ((bf16[8,208,512]{2,1,0:T(8,128)(2,1)}), bf16[8,208,512]{2,1,0:T(8,128)(2,1)}, u32[]{:S(2)}, u32[]{:S(2)}) async-start(bf16[8,208,512]{2,1,0:T(8,128)(2,1)} %shard_map.154), calls=%async_computation.1 | async-start | bytes 3407872 | tf_op jit(solution)/shard_map/all_to_all | solution.py:244
  58.6 39.5 %copy-start = (bf16[32,15488]{1,0:T(8,128)(2,1)}, bf16[32,15488]{1,0:T(8,128)(2,1)S(1)}, u32[]{:S(2)}) copy-start(bf16[32,15488]{1,0:T(8,128)(2,1)S(1)} %all_gather.9.refs_0_.refs_6_) | copy-start | bytes 2973700
  58.6 28.1 %collective-permute-start.1 = (bf16[32,15488]{1,0:T(8,128)(2,1)S(1)}, bf16[32,15488]{1,0:T(8,128)(2,1)S(1)}, u32[]{:S(2)}, u32[]{:S(2)}) collective-permute-start(bf16[32,15488]{1,0:T(8,128)(2,1)S(1)} %all_gather.9.refs_0_.refs_6_), channel_id=1, source_target_pairs={{0,22},{2,0},{4,2},{6,4},{8,6},{10,8},{12,10},{14,12},{16,14},{18,... | collective-permute-start | bytes 2973704 | tf_op jit(solution)/shard_map/ppermute | solution.py:251
  66.5 25.3 %collective-permute-start = (bf16[32,15488]{1,0:T(8,128)(2,1)S(1)}, bf16[32,15488]{1,0:T(8,128)(2,1)S(1)}, u32[]{:S(2)}, u32[]{:S(2)}) collective-permute-start(bf16[32,15488]{1,0:T(8,128)(2,1)S(1)} %all_gather.9.refs_0_.refs_6_), channel_id=1, source_target_pairs={{0,2},{2,4},{4,6},{6,8},{8,10},{10,12},{12,14},{14,16},{16,18},{18... | collective-permute-start | bytes 2973704 | tf_op jit(solution)/shard_map/ppermute | solution.py:251
  68.4 27.4 %collective-permute-start.2 = (bf16[32,15488]{1,0:T(8,128)(2,1)S(1)}, bf16[32,15488]{1,0:T(8,128)(2,1)S(1)}, u32[]{:S(2)}, u32[]{:S(2)}) collective-permute-start(bf16[32,15488]{1,0:T(8,128)(2,1)S(1)} %all_gather.9.refs_0_.refs_6_), channel_id=1, source_target_pairs={{0,1},{1,0},{2,3},{3,2},{4,5},{5,4},{6,7},{7,6},{8,9},{9,8},{10,11... | collective-permute-start | bytes 2973704 | tf_op jit(solution)/shard_map/ppermute | solution.py:252
  86.8 11.4 %copy-start.1 = (bf16[32,15488]{1,0:T(8,128)(2,1)}, bf16[32,15488]{1,0:T(8,128)(2,1)S(1)}, u32[]{:S(2)}) copy-start(bf16[32,15488]{1,0:T(8,128)(2,1)S(1)} %collective-permute-done.1.refs_2_.refs_8_) | copy-start | bytes 2973700
  86.8 9.1 %collective-permute-start.4 = (bf16[32,15488]{1,0:T(8,128)(2,1)S(1)}, bf16[32,15488]{1,0:T(8,128)(2,1)S(1)}, u32[]{:S(2)}, u32[]{:S(2)}) collective-permute-start(bf16[32,15488]{1,0:T(8,128)(2,1)S(1)} %collective-permute-done.1.refs_2_.refs_8_), channel_id=1, source_target_pairs={{0,1},{1,0},{2,3},{3,2},{4,5},{5,4},{6,7},{7,6},{8,9},{9,8},{10,11... | collective-permute-start | bytes 2973704 | tf_op jit(solution)/shard_map/ppermute | solution.py:252
  91.8 6.4 %copy-start.2 = (bf16[32,15488]{1,0:T(8,128)(2,1)}, bf16[32,15488]{1,0:T(8,128)(2,1)S(1)}, u32[]{:S(2)}) copy-start(bf16[32,15488]{1,0:T(8,128)(2,1)S(1)} %collective-permute-done.refs_1_.refs_7_) | copy-start | bytes 2973700
  91.8 6.4 %collective-permute-start.3 = (bf16[32,15488]{1,0:T(8,128)(2,1)S(1)}, bf16[32,15488]{1,0:T(8,128)(2,1)}, u32[]{:S(2)}, u32[]{:S(2)}) collective-permute-start(bf16[32,15488]{1,0:T(8,128)(2,1)S(1)} %collective-permute-done.refs_1_.refs_7_), channel_id=1, source_target_pairs={{0,1},{1,0},{2,3},{3,2},{4,5},{5,4},{6,7},{7,6},{8,9},{9,8},{10,11... | collective-permute-start | bytes 2973704 | tf_op jit(solution)/shard_map/ppermute | solution.py:252
  95.9 1.0 copy-start.3
  96.8 1.1 copy-start.4
  104.9 21.2 %all-to-all-start.2 = ((bf16[4,528,256]{2,1,0:T(8,128)(2,1)}), bf16[4,528,256]{2,1,0:T(8,128)(2,1)S(1)}, u32[]{:S(2)}, u32[]{:S(2)}) async-start(bf16[4,528,256]{2,1,0:T(8,128)(2,1)} %shard_map.156), calls=%async_computation.2 | async-start | bytes 2162688 | tf_op jit(solution)/shard_map/all_to_all | solution.py:272

commit v9 on v8

--- a/solution.py
+++ b/solution.py
@@ -1,5 +1,4 @@
 import functools
-import math
 
 import jax
 import jax.numpy as jnp
@@ -14,6 +13,7 @@
 CORES = 2
 LANES = 128
 SLOT_ROWS = 160
+META = 8
 VMEM_BYTES = 56 * 1024 * 1024
 
 
@@ -68,25 +68,34 @@
         ],
         axis=0,
     ).astype(jnp.bfloat16)
-    meta = jnp.concatenate([meta, jnp.zeros((LANES - 8, tokens), jnp.bfloat16)], axis=0)
+    meta = jnp.concatenate([meta, jnp.zeros((LANES - META, tokens), jnp.bfloat16)], axis=0)
     meta = dot(chosen, meta, ((1,), (1,))).astype(jnp.bfloat16)
     picked = dot(chosen, rows_ref[...], ((1,), (0,))).astype(jnp.bfloat16)
     out_ref[:, :width] = picked
     out_ref[:, width:] = meta
     block = width // (nx * ny)
-    stride = cols_ref.shape[2] // nx
     for y in range(ny):
         for x in range(nx):
             at = (x * ny + y) * block
-            cols_ref[y, :, x * stride : x * stride + block] = picked[:, at : at + block]
-            cols_ref[y, :, x * stride + block : (x + 1) * stride] = meta[:, : stride - block]
+            cols_ref[y, :, x * block : (x + 1) * block] = picked[:, at : at + block]
+        cols_ref[y, :, nx * block :] = meta
 
 
 def pack_kernel(cols_ref, rows_ref, out_ref):
-    ny, _, span = cols_ref.shape
-    for y in range(ny):
-        out_ref[:, y * span : (y + 1) * span] = cols_ref[y]
-    out_ref[:, ny * span :] = rows_ref[...]
+    ny, _, total = cols_ref.shape
+    span = total - LANES
+    width = rows_ref.shape[1] - LANES
+    out_ref[:, :width] = rows_ref[:, :width]
+    source = lax.broadcasted_iota(jnp.int32, (LANES, LANES), 0)
+    target = lax.broadcasted_iota(jnp.int32, (LANES, LANES), 1)
+    packed = jnp.zeros((out_ref.shape[0], LANES), jnp.float32)
+    for y in range(ny + 1):
+        if y < ny:
+            out_ref[:, width + y * span : width + (y + 1) * span] = cols_ref[y, :, :span]
+        meta = cols_ref[y, :, span:] if y < ny else rows_ref[:, width:]
+        moved = (target == source + y * META) & (source < META)
+        packed = packed + dot(meta, jnp.where(moved, 1.0, 0.0).astype(jnp.bfloat16), ((1,), (0,)))
+    out_ref[:, 2 * width :] = packed.astype(jnp.bfloat16)
 
 
 def routing(meta, expert):
@@ -108,20 +117,19 @@
 
 
 def weight_kernel(block, ny, expert_ref, *refs):
-    pieces, hid_ref, out_ref, a_ref, be_ref, bd_ref = refs[:6], *refs[6:11]
+    pieces, metas, hid_ref, out_ref, a_ref, be_ref, bd_ref = refs[:6], refs[6:12], *refs[12:17]
     rows, total = pieces[0].shape
     span = total // ny
     group = 6 * rows
     expert = expert_ref[0].astype(jnp.float32)
     width = be_ref.shape[1]
     quarter = hid_ref.shape[1] - SLOT_ROWS
+    meta = jnp.concatenate([m[...] for m in metas], axis=0).astype(jnp.float32)
     for y in range(ny):
         top = y * group
         for i, piece in enumerate(pieces):
             a_ref[top + i * rows : top + (i + 1) * rows, :] = piece[:, y * span : (y + 1) * span]
-        at = y * span + block
-        meta = jnp.concatenate([piece[:, at : at + 8] for piece in pieces], axis=0)
-        slot, prob, token = routing(meta.astype(jnp.float32), expert)
+        slot, prob, token = routing(meta[:, y * META : (y + 1) * META], expert)
         weighted = dot(one_hot(slot, SLOT_ROWS, prob), hid_ref[y, :SLOT_ROWS, :width], ((1,), (0,)))
         be_ref[top : top + group, :] = weighted.astype(jnp.bfloat16)
         dense = jnp.concatenate(
@@ -130,12 +138,12 @@
         moved = dot(one_hot(token, 4 * quarter), dense, ((1,), (0,)))
         bd_ref[top : top + group, :] = moved.astype(jnp.bfloat16)
     rows_in = a_ref[...]
-    nx, height, stride = out_ref.shape
+    nx, height, _ = out_ref.shape
     summed = dot(be_ref[...], rows_in, ((0,), (0,))).astype(jnp.bfloat16)
     dsummed = dot(bd_ref[...], rows_in, ((0,), (0,))).astype(jnp.bfloat16)
     for x in range(nx):
-        out_ref[x, :width, :] = summed[:, x * stride : (x + 1) * stride]
-        out_ref[x, width:, :] = dsummed[: height - width, x * stride : (x + 1) * stride]
+        out_ref[x, :width, :block] = summed[:, x * block : (x + 1) * block]
+        out_ref[x, width:, :block] = dsummed[: height - width, x * block : (x + 1) * block]
 
 
 def place(onehot, values):
@@ -147,7 +155,7 @@
     return dot(onehot, high, dims) + dot(onehot, middle, dims) + dot(onehot, low, dims)
 
 
-def back_kernel(expert_ref, *refs):
+def back_kernel(at, expert_ref, *refs):
     datas, metas = refs[:6], refs[6:12]
     we_ref, wd_ref, gate_ref, up_ref, dgate_ref, dup_ref = refs[12:18]
     gate_out, up_out, dots_out, dgate_out, dup_out = refs[18:23]
@@ -166,7 +174,7 @@
     @pl.when(step == pl.num_programs(0) - 1)
     def _():
         meta = jnp.concatenate([m[...] for m in metas], axis=0).astype(jnp.float32)
-        slot, prob, token = routing(meta, expert_ref[0].astype(jnp.float32))
+        slot, prob, token = routing(meta[:, at : at + META], expert_ref[0].astype(jnp.float32))
         slots = gate_ref.shape[1]
         hot = one_hot(slot, slots)
         back = place(hot, acc_e[...])
@@ -217,7 +225,7 @@
     eighth = tokens // (RUN * CORES)
     block = width // (nx * ny)
     bf16 = jnp.bfloat16
-    stride = -(-(block + 8) // LANES) * LANES
+    stride = -(-block // LANES) * LANES
     expert_arr = expert.reshape(1).astype(jnp.int32)
     smem = pl.BlockSpec(memory_space=pltpu.SMEM)
     vmem = pl.BlockSpec(memory_space=pltpu.VMEM)
@@ -229,12 +237,12 @@
     )(expert_gate_pre, expert_up_pre, dense_gate_pre, dense_up_pre)
 
     part_arr = part.reshape(1).astype(jnp.int32)
-    span = nx * stride
+    span = nx * block
     mine, cols = pl.pallas_call(
         functools.partial(pick_kernel, capacity, nx, ny),
         out_shape=(
             jax.ShapeDtypeStruct((eighth, width + LANES), bf16),
-            jax.ShapeDtypeStruct((ny, eighth, span), bf16),
+            jax.ShapeDtypeStruct((ny, eighth, span + LANES), bf16),
         ),
         in_specs=[smem] * 2 + [vmem] * 4,
         compiler_params=params(),
@@ -244,13 +252,14 @@
     hiddens = lax.all_to_all(hidden, "y", split_axis=0, concat_axis=0, tiled=True)
     packed = pl.pallas_call(
         pack_kernel,
-        out_shape=jax.ShapeDtypeStruct((eighth, ny * span + width + LANES), bf16),
+        out_shape=jax.ShapeDtypeStruct((eighth, 2 * width + LANES), bf16),
         compiler_params=params(),
     )(cols, mine)
     packed = lax.all_gather(packed, "e", axis=0, tiled=True)
     pieces = [packed] + [lax.ppermute(packed, ("e", "l"), ring(ne * RUN, d)) for d in (1, -1)]
     pieces += [lax.ppermute(p, "c", ring(CORES, 1)) for p in pieces]
 
+    meta_spec = pl.BlockSpec((ne * eighth, LANES), lambda k: (0, 2 * width // LANES))
     height = hwidth + -(-dwidth // 16) * 16
     ktotal = ny * ne * tokens
     partial_sums = pl.pallas_call(
@@ -258,7 +267,8 @@
         grid=(1,),
         out_shape=jax.ShapeDtypeStruct((nx, height, stride), bf16),
         in_specs=[smem]
-        + [pl.BlockSpec((ne * eighth, ny * span), lambda k: (0, 0))] * 6
+        + [pl.BlockSpec((ne * eighth, width), lambda k: (0, 1))] * 6
+        + [meta_spec] * 6
         + [whole(*hiddens.shape)],
         out_specs=whole(nx, height, stride),
         scratch_shapes=[
@@ -267,16 +277,14 @@
             pltpu.VMEM((ktotal, LANES), bf16),
         ],
         compiler_params=params(),
-    )(expert_arr, *pieces, hiddens)
+    )(expert_arr, *pieces, *pieces, hiddens)
     partial_sums, expert_arr = lax.optimization_barrier((partial_sums, expert_arr))
     landed = lax.all_to_all(partial_sums, "x", split_axis=0, concat_axis=0, tiled=True)
 
-    depth = math.gcd(ny * span, width)
-    base = ny * span // depth
-    data_spec = pl.BlockSpec((ne * eighth, depth), lambda k: (0, base + k))
-    meta_spec = pl.BlockSpec((ne * eighth, LANES), lambda k: (0, (ny * span + width) // LANES))
+    depth = width // 2
+    data_spec = pl.BlockSpec((ne * eighth, depth), lambda k: (0, k))
     gate_grad, up_grad, dots, dense_gate_grad, dense_up_grad = pl.pallas_call(
-        back_kernel,
+        functools.partial(back_kernel, ny * META),
         grid=(width // depth,),
         out_shape=(
             jax.ShapeDtypeStruct((1, slots, hwidth), bf16),

time: 128 us -> 124 us (0.969)
  Pallas kernels: 22.9 us -> 20.2 us
  starting transfers between devices: 39.6 us -> 37.4 us
    ppermute x3, starting transfers between devices: 13.9 us -> 11.4 us  [local(): pieces += [lax.ppermute(p, 'c', ring(CORES, 1)) for p in pieces]]
    pallas_call x2, Pallas kernels: 11.7 us -> 9.47 us  [the longest x1 7.65 us: local(): pl.pallas_call(functools.partial(back_kernel, ny * META), grid=(width //...]
  transfers between devices with their start and end apart: 8 -> 8, of which waited for: 4 -> 4; matrix products, arithmetic and copies ran while one was open for 0% -> 0% of each run, Pallas kernels for 11% -> 10%
where the time goes in v9:
time: 124 us; the launch traced here: 123 us
  blocking collectives  40 us (32%)
  starting transfers between devices  37.4 us (30%)
  waiting for transfers between devices  20.3 us (16%)
  Pallas kernels  20.2 us (16%)
  local copies, waits for them, and re-layouts  2.62 us (2%)
  other arithmetic  2.04 us (2%)
    all_gather x1, blocking collectives, local(): packed = lax.all_gather(packed, 'e', axis=0, tiled=True)  33.4 us
    ppermute x2, waiting for transfers between devices, local(): lax.ppermute(packed, ('e', 'l'), ring(ne * RUN, d))  14.6 us
    ppermute x3, starting transfers between devices, local(): pieces += [lax.ppermute(p, 'c', ring(CORES, 1)) for p in pieces]  11.4 us
    ppermute x2, starting transfers between devices, local(): lax.ppermute(packed, ('e', 'l'), ring(ne * RUN, d))  9.92 us
    pallas_call x1, Pallas kernels, local(): pl.pallas_call(functools.partial(back_kernel, ny * META), grid=(width //...  7.65 us
    all_to_all x1, starting transfers between devices, local(): cols = lax.all_to_all(cols, 'y', split_axis=0, concat_axis=0, tiled=True)  7.65 us
    all_gather x1, blocking collectives, local(): all_dots = lax.all_gather(dots, ('l', 'c'), axis=0)  6.62 us
    pallas_call x1, Pallas kernels, local(): pl.pallas_call(functools.partial(weight_kernel, block, ny), grid=(1,), ou...  6.23 us
  transfers between devices with their start and end apart: 8, of which 4 were waited for; matrix products, arithmetic and copies ran while one was open for 0% of the time, Pallas kernels for 10%

profile of v9, /device:TPU:1, one launch (start us, length us, event | category | flops | bytes accessed | tf_op | source)
XLA Modules:
  0.0 123.3 jit_solution(12986658803091680349)
XLA Ops:
  0.6 2.1 %shard_map.153 = (bf16[8,7296]{1,0:T(8,128)(2,1)}, bf16[8,8,1024]{2,1,0:T(8,128)(2,1)}) custom-call(s32[1]{0:T(128)} %bitcast.expert_ref, s32[1]{0:T(128)} %bitcast.1.part_ref, bf16[48,7168]{1,0:T(8,128)(2,1)} %rows_ref.1, bf16[2,48]{1,0:T(2,128)(2,1)} %bitcast.21, s32[2,48]{1,0:T(2,128)} %bitcast.17, s32[2,48]{1,0:T(2,128)} %bitcast.18), custom_call_target="tpu_custom_call" | custom-call | tf_op jit(solution)/shard_map/pallas_call | solution.py:241
  2.7 7.7 %all-to-all-start = ((bf16[8,8,1024]{2,1,0:T(8,128)(2,1)}), bf16[8,8,1024]{2,1,0:T(8,128)(2,1)S(1)}, u32[]{:S(2)}, u32[]{:S(2)}) async-start(bf16[8,8,1024]{2,1,0:T(8,128)(2,1)} %get-tuple-element.18), calls=%async_computation | async-start | bytes 262144 | tf_op jit(solution)/shard_map/all_to_all | solution.py:250
  10.4 2.4 %shard_map.154 = bf16[8,208,512]{2,1,0:T(8,128)(2,1)} custom-call(bf16[1,156,416]{2,1,0:T(8,128)(2,1)} %refs_14_.1, bf16[1,156,416]{2,1,0:T(8,128)(2,1)} %refs_15_.1, bf16[192,104]{1,0:T(8,128)(2,1)} %refs_16_.1, bf16[192,104]{1,0:T(8,128)(2,1)} %refs_17_.1), custom_call_target="tpu_custom_call" | custom-call | tf_op jit(solution)/shard_map/pallas_call | solution.py:233
  12.8 5.5 %all-to-all-done.cols_ref = bf16[8,8,1024]{2,1,0:T(8,128)(2,1)S(1)} async-done(((bf16[8,8,1024]{2,1,0:T(8,128)(2,1)}), bf16[8,8,1024]{2,1,0:T(8,128)(2,1)S(1)}, u32[]{:S(2)}, u32[]{:S(2)}) %all-to-all-start) | async-done | bytes 131104 | tf_op jit(solution)/shard_map/all_to_all | solution.py:250
  18.3 0.0 copy-start.5
  18.3 0.7 copy-done.5
  19.0 4.3 %all-to-all-start.1 = ((bf16[8,208,512]{2,1,0:T(8,128)(2,1)}), bf16[8,208,512]{2,1,0:T(8,128)(2,1)}, u32[]{:S(2)}, u32[]{:S(2)}) async-start(bf16[8,208,512]{2,1,0:T(8,128)(2,1)} %shard_map.154), calls=%async_computation.1 | async-start | bytes 3407872 | tf_op jit(solution)/shard_map/all_to_all | solution.py:252
  23.3 1.8 %shard_map.155 = bf16[8,14464]{1,0:T(8,128)(2,1)} custom-call(bf16[8,8,1024]{2,1,0:T(8,128)(2,1)} %copy-done.5, bf16[8,7296]{1,0:T(8,128)(2,1)} %get-tuple-element.20.rows_ref), custom_call_target="tpu_custom_call" | custom-call | tf_op jit(solution)/shard_map/pallas_call | solution.py:253
  25.1 33.4 %all_gather.9.refs_0_.refs_6_ = bf16[32,14464]{1,0:T(8,128)(2,1)S(1)} all-gather(bf16[8,14464]{1,0:T(8,128)(2,1)} %shard_map.155), channel_id=1, replica_groups=mesh['x'=4,'y'=8,'e'=4,'l'=3,'c'=2] {'e'}, dimensions={0}, use_global_device_ids=true | all-gather | bytes 1157120 | tf_op jit(solution)/shard_map/all_gather | solution.py:258
  58.4 0.0 copy-start
  58.4 8.0 %collective-permute-start.1 = (bf16[32,14464]{1,0:T(8,128)(2,1)S(1)}, bf16[32,14464]{1,0:T(8,128)(2,1)S(1)}, u32[]{:S(2)}, u32[]{:S(2)}) collective-permute-start(bf16[32,14464]{1,0:T(8,128)(2,1)S(1)} %all_gather.9.refs_0_.refs_6_), channel_id=1, source_target_pairs={{0,22},{2,0},{4,2},{6,4},{8,6},{10,8},{12,10},{14,12},{16,14},{18,... | collective-permute-start | bytes 2777096 | tf_op jit(solution)/shard_map/ppermute | solution.py:259
  66.4 1.9 %collective-permute-start = (bf16[32,14464]{1,0:T(8,128)(2,1)S(1)}, bf16[32,14464]{1,0:T(8,128)(2,1)S(1)}, u32[]{:S(2)}, u32[]{:S(2)}) collective-permute-start(bf16[32,14464]{1,0:T(8,128)(2,1)S(1)} %all_gather.9.refs_0_.refs_6_), channel_id=1, source_target_pairs={{0,2},{2,4},{4,6},{6,8},{8,10},{10,12},{12,14},{14,16},{16,18},{18... | collective-permute-start | bytes 2777096 | tf_op jit(solution)/shard_map/ppermute | solution.py:259
  68.4 4.6 %collective-permute-start.2 = (bf16[32,14464]{1,0:T(8,128)(2,1)S(1)}, bf16[32,14464]{1,0:T(8,128)(2,1)S(1)}, u32[]{:S(2)}, u32[]{:S(2)}) collective-permute-start(bf16[32,14464]{1,0:T(8,128)(2,1)S(1)} %all_gather.9.refs_0_.refs_6_), channel_id=1, source_target_pairs={{0,1},{1,0},{2,3},{3,2},{4,5},{5,4},{6,7},{7,6},{8,9},{9,8},{10,11... | collective-permute-start | bytes 2777096 | tf_op jit(solution)/shard_map/ppermute | solution.py:260
  73.0 12.8 %collective-permute-done.1.refs_2_.refs_8_ = bf16[32,14464]{1,0:T(8,128)(2,1)S(1)} collective-permute-done((bf16[32,14464]{1,0:T(8,128)(2,1)S(1)}, bf16[32,14464]{1,0:T(8,128)(2,1)S(1)}, u32[]{:S(2)}, u32[]{:S(2)}) %collective-permute-start.1) | collective-permute-done | bytes 925728 | tf_op jit(solution)/shard_map/ppermute | solution.py:259
  85.8 0.0 copy-start.1
  85.8 3.2 %collective-permute-start.4 = (bf16[32,14464]{1,0:T(8,128)(2,1)S(1)}, bf16[32,14464]{1,0:T(8,128)(2,1)S(1)}, u32[]{:S(2)}, u32[]{:S(2)}) collective-permute-start(bf16[32,14464]{1,0:T(8,128)(2,1)S(1)} %collective-permute-done.1.refs_2_.refs_8_), channel_id=1, source_target_pairs={{0,1},{1,0},{2,3},{3,2},{4,5},{5,4},{6,7},{7,6},{8,9},{9,8},{10,11... | collective-permute-start | bytes 2777096 | tf_op jit(solution)/shard_map/ppermute | solution.py:260
  89.1 1.7 %collective-permute-done.refs_1_.refs_7_ = bf16[32,14464]{1,0:T(8,128)(2,1)S(1)} collective-permute-done((bf16[32,14464]{1,0:T(8,128)(2,1)S(1)}, bf16[32,14464]{1,0:T(8,128)(2,1)S(1)}, u32[]{:S(2)}, u32[]{:S(2)}) %collective-permute-start) | collective-permute-done | bytes 925728 | tf_op jit(solution)/shard_map/ppermute | solution.py:259
  90.8 0.0 copy-start.2
  90.8 3.6 %collective-permute-start.3 = (bf16[32,14464]{1,0:T(8,128)(2,1)S(1)}, bf16[32,14464]{1,0:T(8,128)(2,1)}, u32[]{:S(2)}, u32[]{:S(2)}) collective-permute-start(bf16[32,14464]{1,0:T(8,128)(2,1)S(1)} %collective-permute-done.refs_1_.refs_7_), channel_id=1, source_target_pairs={{0,1},{1,0},{2,3},{3,2},{4,5},{5,4},{6,7},{7,6},{8,9},{9,8},{10,11... | collective-permute-start | bytes 2777096 | tf_op jit(solution)/shard_map/ppermute | solution.py:260
  94.4 0.0 collective-permute-done.2.refs_3_.refs_9_
  94.4 0.0 copy-start.3
  94.4 0.0 collective-permute-done.4.refs_5_.refs_11_
  94.4 0.9 copy-done.3
  95.4 0.0 copy-start.4
  95.4 1.0 copy-done.4
  96.4 0.2 collective-permute-done.3.refs_4_.refs_10_
  96.6 0.0 all-to-all-done.1.refs_12_
  96.6 0.0 copy-done
  96.6 0.0 copy-done.1
  96.6 0.0 copy-done.2
  96.6 6.2 %shard_map.156 = bf16[4,528,256]{2,1,0:T(8,128)(2,1)} custom-call(s32[1]{0:T(128)} %bitcast.expert_ref, bf16[32,14464]{1,0:T(8,128)(2,1)} %copy-done, bf16[32,14464]{1,0:T(8,128)(2,1)} %copy-done.2, bf16[32,14464]{1,0:T(8,128)(2,1)} %copy-done.1, bf16[32,14464]{1,0:T(8,128)(2,1)} %copy-done.3, bf16[32,14464]{1,0:T(8,128)(2,1)} %collective-permute-done.3.refs_4_.refs_10_, ...), custom_call_target="tpu_custom_call" | custom-call | tf_op jit(solution)/shard_map/pallas_call | solution.py:265
  102.9 4.1 %all-to-all-start.2 = ((bf16[4,528,256]{2,1,0:T(8,128)(2,1)}), bf16[4,528,256]{2,1,0:T(8,128)(2,1)S(1)}, u32[]{:S(2)}, u32[]{:S(2)}) async-start(bf16[4,528,256]{2,1,0:T(8,128)(2,1)} %shard_map.156), calls=%async_computation.2 | async-start | bytes 2162688 | tf_op jit(solution)/shard_map/all_to_all | solution.py:282
  106.9 7.7 %shard_map.157 = (bf16[1,156,416]{2,1,0:T(8,128)(2,1)}, bf16[1,156,416]{2,1,0:T(8,128)(2,1)}, f32[1,156]{1,0:T(1,128)}, bf16[192,104]{1,0:T(8,128)(2,1)}, bf16[192,104]{1,0:T(8,128)(2,1)}) custom-call(s32[1]{0:T(128)} %bitcast.expert_ref, bf16[32,14464]{1,0:T(8,128)(2,1)} %copy-done, bf16[32,14464]{1,0:T(8,128)(2,1)} %copy-done.2, ...), custom_call_target="tpu_custom_call" | custom-call | tf_op jit(solution)/shard_map/pallas_call | solution.py:286
  114.6 6.6 %all-gather.1 = f32[6,1,156]{2,1,0:T(1,128)S(1)} all-gather(f32[1,1,156]{2,1,0:T(1,128)} %bitcast.20), channel_id=2, replica_groups=mesh['x'=4,'y'=8,'e'=4,'l'=3,'c'=2] {'l','c'}, dimensions={0}, use_global_device_ids=true | all-gather | bytes 4368 | tf_op jit(solution)/shard_map/all_gather | solution.py:331
  121.2 0.6 reduce.1
  121.8 0.0 all-to-all-done.2
  121.8 0.7 fusion.1
  122.5 0.8 fusion
Async XLA Ops:
  2.7 15.6 %all-to-all-start = ((bf16[8,8,1024]{2,1,0:T(8,128)(2,1)}), bf16[8,8,1024]{2,1,0:T(8,128)(2,1)S(1)}, u32[]{:S(2)}, u32[]{:S(2)}) async-start(bf16[8,8,1024]{2,1,0:T(8,128)(2,1)} %get-tuple-element.18), calls=%async_computation | async-start | bytes 262144 | tf_op jit(solution)/shard_map/all_to_all | solution.py:250
  18.3 0.7 copy-start.5
  19.0 77.7 %all-to-all-start.1 = ((bf16[8,208,512]{2,1,0:T(8,128)(2,1)}), bf16[8,208,512]{2,1,0:T(8,128)(2,1)}, u32[]{:S(2)}, u32[]{:S(2)}) async-start(bf16[8,208,512]{2,1,0:T(8,128)(2,1)} %shard_map.154), calls=%async_computation.1 | async-start | bytes 3407872 | tf_op jit(solution)/shard_map/all_to_all | solution.py:252
  58.4 38.2 %copy-start = (bf16[32,14464]{1,0:T(8,128)(2,1)}, bf16[32,14464]{1,0:T(8,128)(2,1)S(1)}, u32[]{:S(2)}) copy-start(bf16[32,14464]{1,0:T(8,128)(2,1)S(1)} %all_gather.9.refs_0_.refs_6_) | copy-start | bytes 2777092
  58.4 27.4 %collective-permute-start.1 = (bf16[32,14464]{1,0:T(8,128)(2,1)S(1)}, bf16[32,14464]{1,0:T(8,128)(2,1)S(1)}, u32[]{:S(2)}, u32[]{:S(2)}) collective-permute-start(bf16[32,14464]{1,0:T(8,128)(2,1)S(1)} %all_gather.9.refs_0_.refs_6_), channel_id=1, source_target_pairs={{0,22},{2,0},{4,2},{6,4},{8,6},{10,8},{12,10},{14,12},{16,14},{18,... | collective-permute-start | bytes 2777096 | tf_op jit(solution)/shard_map/ppermute | solution.py:259
  66.4 24.4 %collective-permute-start = (bf16[32,14464]{1,0:T(8,128)(2,1)S(1)}, bf16[32,14464]{1,0:T(8,128)(2,1)S(1)}, u32[]{:S(2)}, u32[]{:S(2)}) collective-permute-start(bf16[32,14464]{1,0:T(8,128)(2,1)S(1)} %all_gather.9.refs_0_.refs_6_), channel_id=1, source_target_pairs={{0,2},{2,4},{4,6},{6,8},{8,10},{10,12},{12,14},{14,16},{16,18},{18... | collective-permute-start | bytes 2777096 | tf_op jit(solution)/shard_map/ppermute | solution.py:259
  68.4 26.0 %collective-permute-start.2 = (bf16[32,14464]{1,0:T(8,128)(2,1)S(1)}, bf16[32,14464]{1,0:T(8,128)(2,1)S(1)}, u32[]{:S(2)}, u32[]{:S(2)}) collective-permute-start(bf16[32,14464]{1,0:T(8,128)(2,1)S(1)} %all_gather.9.refs_0_.refs_6_), channel_id=1, source_target_pairs={{0,1},{1,0},{2,3},{3,2},{4,5},{5,4},{6,7},{7,6},{8,9},{9,8},{10,11... | collective-permute-start | bytes 2777096 | tf_op jit(solution)/shard_map/ppermute | solution.py:260
  85.8 10.8 %copy-start.1 = (bf16[32,14464]{1,0:T(8,128)(2,1)}, bf16[32,14464]{1,0:T(8,128)(2,1)S(1)}, u32[]{:S(2)}) copy-start(bf16[32,14464]{1,0:T(8,128)(2,1)S(1)} %collective-permute-done.1.refs_2_.refs_8_) | copy-start | bytes 2777092
  85.8 8.6 %collective-permute-start.4 = (bf16[32,14464]{1,0:T(8,128)(2,1)S(1)}, bf16[32,14464]{1,0:T(8,128)(2,1)S(1)}, u32[]{:S(2)}, u32[]{:S(2)}) collective-permute-start(bf16[32,14464]{1,0:T(8,128)(2,1)S(1)} %collective-permute-done.1.refs_2_.refs_8_), channel_id=1, source_target_pairs={{0,1},{1,0},{2,3},{3,2},{4,5},{5,4},{6,7},{7,6},{8,9},{9,8},{10,11... | collective-permute-start | bytes 2777096 | tf_op jit(solution)/shard_map/ppermute | solution.py:260
  90.8 5.8 %copy-start.2 = (bf16[32,14464]{1,0:T(8,128)(2,1)}, bf16[32,14464]{1,0:T(8,128)(2,1)S(1)}, u32[]{:S(2)}) copy-start(bf16[32,14464]{1,0:T(8,128)(2,1)S(1)} %collective-permute-done.refs_1_.refs_7_) | copy-start | bytes 2777092
  90.8 5.8 %collective-permute-start.3 = (bf16[32,14464]{1,0:T(8,128)(2,1)S(1)}, bf16[32,14464]{1,0:T(8,128)(2,1)}, u32[]{:S(2)}, u32[]{:S(2)}) collective-permute-start(bf16[32,14464]{1,0:T(8,128)(2,1)S(1)} %collective-permute-done.refs_1_.refs_7_), channel_id=1, source_target_pairs={{0,1},{1,0},{2,3},{3,2},{4,5},{5,4},{6,7},{7,6},{8,9},{9,8},{10,11... | collective-permute-start | bytes 2777096 | tf_op jit(solution)/shard_map/ppermute | solution.py:260
  94.4 1.0 copy-start.3
  95.4 1.0 copy-start.4
  102.9 18.9 %all-to-all-start.2 = ((bf16[4,528,256]{2,1,0:T(8,128)(2,1)}), bf16[4,528,256]{2,1,0:T(8,128)(2,1)S(1)}, u32[]{:S(2)}, u32[]{:S(2)}) async-start(bf16[4,528,256]{2,1,0:T(8,128)(2,1)} %shard_map.156), calls=%async_computation.2 | async-start | bytes 2162688 | tf_op jit(solution)/shard_map/all_to_all | solution.py:282

commit v10 on v9

--- a/solution.py
+++ b/solution.py
@@ -257,7 +257,9 @@
     )(cols, mine)
     packed = lax.all_gather(packed, "e", axis=0, tiled=True)
     pieces = [packed] + [lax.ppermute(packed, ("e", "l"), ring(ne * RUN, d)) for d in (1, -1)]
-    pieces += [lax.ppermute(p, "c", ring(CORES, 1)) for p in pieces]
+    other = lax.ppermute(packed, "c", ring(CORES, 1))
+    pieces[2], other = lax.optimization_barrier((pieces[2], other))
+    pieces += [other] + [lax.ppermute(p, "c", ring(CORES, 1)) for p in pieces[1:]]
 
     meta_spec = pl.BlockSpec((ne * eighth, LANES), lambda k: (0, 2 * width // LANES))
     height = hwidth + -(-dwidth // 16) * 16

time: 124 us -> 127 us (1.024)
  waiting for transfers between devices: 20.3 us -> 25.6 us
  starting transfers between devices: 37.4 us -> 35.4 us
    ppermute x2, waiting for transfers between devices: 14.6 us -> 18.9 us  [local(): lax.ppermute(packed, ('e', 'l'), ring(ne * RUN, d))]
    ppermute x2, starting transfers between devices: 9.92 us -> 5.8 us  [local(): lax.ppermute(packed, ('e', 'l'), ring(ne * RUN, d))]
    ppermute x3, starting transfers between devices: 11.4 us -> 13.6 us  [the longest x1 8.44 us: local(): other = lax.ppermute(packed, 'c', ring(CORES, 1))]
  transfers between devices with their start and end apart: 8 -> 8, of which waited for: 4 -> 3; matrix products, arithmetic and copies ran while one was open for 0% -> 0% of each run, Pallas kernels for 10% -> 9%
where the time goes in v10:
time: 127 us; the launch traced here: 126 us
  blocking collectives  40 us (31%)
  starting transfers between devices  35.4 us (28%)
  waiting for transfers between devices  25.6 us (20%)
  Pallas kernels  20.2 us (16%)
  other arithmetic  2.04 us (2%)
  local copies, waits for them, and re-layouts  1.68 us (1%)
    all_gather x1, blocking collectives, local(): packed = lax.all_gather(packed, 'e', axis=0, tiled=True)  33.4 us
    ppermute x2, waiting for transfers between devices, local(): lax.ppermute(packed, ('e', 'l'), ring(ne * RUN, d))  18.9 us
    ppermute x1, starting transfers between devices, local(): other = lax.ppermute(packed, 'c', ring(CORES, 1))  8.44 us
    pallas_call x1, Pallas kernels, local(): pl.pallas_call(functools.partial(back_kernel, ny * META), grid=(width //...  7.65 us
    all_to_all x1, starting transfers between devices, local(): cols = lax.all_to_all(cols, 'y', split_axis=0, concat_axis=0, tiled=True)  7.65 us
    all_gather x1, blocking collectives, local(): all_dots = lax.all_gather(dots, ('l', 'c'), axis=0)  6.62 us
    pallas_call x1, Pallas kernels, local(): pl.pallas_call(functools.partial(weight_kernel, block, ny), grid=(1,), ou...  6.23 us
    ppermute x2, starting transfers between devices, local(): lax.ppermute(packed, ('e', 'l'), ring(ne * RUN, d))  5.8 us
  transfers between devices with their start and end apart: 8, of which 3 were waited for; matrix products, arithmetic and copies ran while one was open for 0% of the time, Pallas kernels for 9%

profile of v10, /device:TPU:1, one launch (start us, length us, event | category | flops | bytes accessed | tf_op | source)
XLA Modules:
  0.0 125.7 jit_solution(2608380211738577365)
XLA Ops:
  0.6 2.1 %shard_map.153 = (bf16[8,7296]{1,0:T(8,128)(2,1)}, bf16[8,8,1024]{2,1,0:T(8,128)(2,1)}) custom-call(s32[1]{0:T(128)} %bitcast.expert_ref, s32[1]{0:T(128)} %bitcast.1.part_ref, bf16[48,7168]{1,0:T(8,128)(2,1)} %rows_ref.1, bf16[2,48]{1,0:T(2,128)(2,1)} %bitcast.21, s32[2,48]{1,0:T(2,128)} %bitcast.17, s32[2,48]{1,0:T(2,128)} %bitcast.18), custom_call_target="tpu_custom_call" | custom-call | tf_op jit(solution)/shard_map/pallas_call | solution.py:241
  2.7 7.7 %all-to-all-start = ((bf16[8,8,1024]{2,1,0:T(8,128)(2,1)}), bf16[8,8,1024]{2,1,0:T(8,128)(2,1)S(1)}, u32[]{:S(2)}, u32[]{:S(2)}) async-start(bf16[8,8,1024]{2,1,0:T(8,128)(2,1)} %get-tuple-element.20), calls=%async_computation | async-start | bytes 262144 | tf_op jit(solution)/shard_map/all_to_all | solution.py:250
  10.4 2.4 %shard_map.154 = bf16[8,208,512]{2,1,0:T(8,128)(2,1)} custom-call(bf16[1,156,416]{2,1,0:T(8,128)(2,1)} %refs_14_.1, bf16[1,156,416]{2,1,0:T(8,128)(2,1)} %refs_15_.1, bf16[192,104]{1,0:T(8,128)(2,1)} %refs_16_.1, bf16[192,104]{1,0:T(8,128)(2,1)} %refs_17_.1), custom_call_target="tpu_custom_call" | custom-call | tf_op jit(solution)/shard_map/pallas_call | solution.py:233
  12.8 5.5 %all-to-all-done.cols_ref = bf16[8,8,1024]{2,1,0:T(8,128)(2,1)S(1)} async-done(((bf16[8,8,1024]{2,1,0:T(8,128)(2,1)}), bf16[8,8,1024]{2,1,0:T(8,128)(2,1)S(1)}, u32[]{:S(2)}, u32[]{:S(2)}) %all-to-all-start) | async-done | bytes 131104 | tf_op jit(solution)/shard_map/all_to_all | solution.py:250
  18.3 0.0 copy-start.5
  18.3 0.7 copy-done.5
  19.0 4.3 %all-to-all-start.1 = ((bf16[8,208,512]{2,1,0:T(8,128)(2,1)}), bf16[8,208,512]{2,1,0:T(8,128)(2,1)}, u32[]{:S(2)}, u32[]{:S(2)}) async-start(bf16[8,208,512]{2,1,0:T(8,128)(2,1)} %shard_map.154), calls=%async_computation.1 | async-start | bytes 3407872 | tf_op jit(solution)/shard_map/all_to_all | solution.py:252
  23.3 1.8 %shard_map.155 = bf16[8,14464]{1,0:T(8,128)(2,1)} custom-call(bf16[8,8,1024]{2,1,0:T(8,128)(2,1)} %copy-done.5, bf16[8,7296]{1,0:T(8,128)(2,1)} %get-tuple-element.22.rows_ref), custom_call_target="tpu_custom_call" | custom-call | tf_op jit(solution)/shard_map/pallas_call | solution.py:253
  25.1 33.4 %all_gather.9.refs_0_.refs_6_ = bf16[32,14464]{1,0:T(8,128)(2,1)S(1)} all-gather(bf16[8,14464]{1,0:T(8,128)(2,1)} %shard_map.155), channel_id=1, replica_groups=mesh['x'=4,'y'=8,'e'=4,'l'=3,'c'=2] {'e'}, dimensions={0}, use_global_device_ids=true | all-gather | bytes 1157120 | tf_op jit(solution)/shard_map/all_gather | solution.py:258
  58.4 0.0 copy-start
  58.4 8.4 %collective-permute-start.2 = (bf16[32,14464]{1,0:T(8,128)(2,1)S(1)}, bf16[32,14464]{1,0:T(8,128)(2,1)S(1)}, u32[]{:S(2)}, u32[]{:S(2)}) collective-permute-start(bf16[32,14464]{1,0:T(8,128)(2,1)S(1)} %all_gather.9.refs_0_.refs_6_), channel_id=1, source_target_pairs={{0,1},{1,0},{2,3},{3,2},{4,5},{5,4},{6,7},{7,6},{8,9},{9,8},{10,11... | collective-permute-start | bytes 2777096 | tf_op jit(solution)/shard_map/ppermute | solution.py:260
  66.9 2.0 %collective-permute-start.1 = (bf16[32,14464]{1,0:T(8,128)(2,1)S(1)}, bf16[32,14464]{1,0:T(8,128)(2,1)S(1)}, u32[]{:S(2)}, u32[]{:S(2)}) collective-permute-start(bf16[32,14464]{1,0:T(8,128)(2,1)S(1)} %all_gather.9.refs_0_.refs_6_), channel_id=1, source_target_pairs={{0,22},{2,0},{4,2},{6,4},{8,6},{10,8},{12,10},{14,12},{16,14},{18,... | collective-permute-start | bytes 2777096 | tf_op jit(solution)/shard_map/ppermute | solution.py:259
  68.9 3.8 %collective-permute-start = (bf16[32,14464]{1,0:T(8,128)(2,1)S(1)}, bf16[32,14464]{1,0:T(8,128)(2,1)S(1)}, u32[]{:S(2)}, u32[]{:S(2)}) collective-permute-start(bf16[32,14464]{1,0:T(8,128)(2,1)S(1)} %all_gather.9.refs_0_.refs_6_), channel_id=1, source_target_pairs={{0,2},{2,4},{4,6},{6,8},{8,10},{10,12},{12,14},{14,16},{16,18},{18... | collective-permute-start | bytes 2777096 | tf_op jit(solution)/shard_map/ppermute | solution.py:259
  72.7 0.0 collective-permute-done.2.refs_3_.refs_9_
  72.7 0.0 copy-start.1
  72.7 18.9 %collective-permute-done.1.refs_2_.refs_8_ = bf16[32,14464]{1,0:T(8,128)(2,1)S(1)} collective-permute-done((bf16[32,14464]{1,0:T(8,128)(2,1)S(1)}, bf16[32,14464]{1,0:T(8,128)(2,1)S(1)}, u32[]{:S(2)}, u32[]{:S(2)}) %collective-permute-start.1) | collective-permute-done | bytes 925728 | tf_op jit(solution)/shard_map/ppermute | solution.py:259
  91.6 0.0 copy-start.2
  91.7 2.5 %collective-permute-start.4 = (bf16[32,14464]{1,0:T(8,128)(2,1)S(1)}, bf16[32,14464]{1,0:T(8,128)(2,1)S(1)}, u32[]{:S(2)}, u32[]{:S(2)}) collective-permute-start(bf16[32,14464]{1,0:T(8,128)(2,1)S(1)} %collective-permute-done.1.refs_2_.refs_8_), channel_id=1, source_target_pairs={{0,1},{1,0},{2,3},{3,2},{4,5},{5,4},{6,7},{7,6},{8,9},{9,8},{10,11... | collective-permute-start | bytes 2777096 | tf_op jit(solution)/shard_map/ppermute | solution.py:262
  94.1 0.0 collective-permute-done.refs_1_.refs_7_
  94.2 0.0 copy-start.3
  94.2 2.6 %collective-permute-start.3 = (bf16[32,14464]{1,0:T(8,128)(2,1)S(1)}, bf16[32,14464]{1,0:T(8,128)(2,1)}, u32[]{:S(2)}, u32[]{:S(2)}) collective-permute-start(bf16[32,14464]{1,0:T(8,128)(2,1)S(1)} %collective-permute-done.refs_1_.refs_7_), channel_id=1, source_target_pairs={{0,1},{1,0},{2,3},{3,2},{4,5},{5,4},{6,7},{7,6},{8,9},{9,8},{10,11... | collective-permute-start | bytes 2777096 | tf_op jit(solution)/shard_map/ppermute | solution.py:262
  96.8 0.0 collective-permute-done.4.refs_5_.refs_11_
  96.8 0.0 copy-done.3
  96.8 0.0 copy-start.4
  96.8 1.0 copy-done.4
  97.8 1.2 collective-permute-done.3.refs_4_.refs_10_
  99.0 0.0 all-to-all-done.1.refs_12_
  99.0 0.0 copy-done
  99.0 0.0 copy-done.1
  99.0 0.0 copy-done.2
  99.0 6.2 %shard_map.156 = bf16[4,528,256]{2,1,0:T(8,128)(2,1)} custom-call(s32[1]{0:T(128)} %bitcast.expert_ref, bf16[32,14464]{1,0:T(8,128)(2,1)} %copy-done, bf16[32,14464]{1,0:T(8,128)(2,1)} %copy-done.3, bf16[32,14464]{1,0:T(8,128)(2,1)} %copy-done.2, bf16[32,14464]{1,0:T(8,128)(2,1)} %copy-done.1, bf16[32,14464]{1,0:T(8,128)(2,1)} %collective-permute-done.3.refs_4_.refs_10_, ...), custom_call_target="tpu_custom_call" | custom-call | tf_op jit(solution)/shard_map/pallas_call | solution.py:267
  105.3 4.1 %all-to-all-start.2 = ((bf16[4,528,256]{2,1,0:T(8,128)(2,1)}), bf16[4,528,256]{2,1,0:T(8,128)(2,1)S(1)}, u32[]{:S(2)}, u32[]{:S(2)}) async-start(bf16[4,528,256]{2,1,0:T(8,128)(2,1)} %shard_map.156), calls=%async_computation.2 | async-start | bytes 2162688 | tf_op jit(solution)/shard_map/all_to_all | solution.py:284
  109.4 7.7 %shard_map.157 = (bf16[1,156,416]{2,1,0:T(8,128)(2,1)}, bf16[1,156,416]{2,1,0:T(8,128)(2,1)}, f32[1,156]{1,0:T(1,128)}, bf16[192,104]{1,0:T(8,128)(2,1)}, bf16[192,104]{1,0:T(8,128)(2,1)}) custom-call(s32[1]{0:T(128)} %bitcast.expert_ref, bf16[32,14464]{1,0:T(8,128)(2,1)} %copy-done, bf16[32,14464]{1,0:T(8,128)(2,1)} %copy-done.3, ...), custom_call_target="tpu_custom_call" | custom-call | tf_op jit(solution)/shard_map/pallas_call | solution.py:288
  117.1 6.6 %all-gather.1 = f32[6,1,156]{2,1,0:T(1,128)S(1)} all-gather(f32[1,1,156]{2,1,0:T(1,128)} %bitcast.20), channel_id=2, replica_groups=mesh['x'=4,'y'=8,'e'=4,'l'=3,'c'=2] {'l','c'}, dimensions={0}, use_global_device_ids=true | all-gather | bytes 4368 | tf_op jit(solution)/shard_map/all_gather | solution.py:333
  123.7 0.6 reduce.1
  124.3 0.0 all-to-all-done.2
  124.3 0.7 fusion.1
  124.9 0.8 fusion
Async XLA Ops:
  2.7 15.6 %all-to-all-start = ((bf16[8,8,1024]{2,1,0:T(8,128)(2,1)}), bf16[8,8,1024]{2,1,0:T(8,128)(2,1)S(1)}, u32[]{:S(2)}, u32[]{:S(2)}) async-start(bf16[8,8,1024]{2,1,0:T(8,128)(2,1)} %get-tuple-element.20), calls=%async_computation | async-start | bytes 262144 | tf_op jit(solution)/shard_map/all_to_all | solution.py:250
  18.3 0.7 copy-start.5
  19.0 80.1 %all-to-all-start.1 = ((bf16[8,208,512]{2,1,0:T(8,128)(2,1)}), bf16[8,208,512]{2,1,0:T(8,128)(2,1)}, u32[]{:S(2)}, u32[]{:S(2)}) async-start(bf16[8,208,512]{2,1,0:T(8,128)(2,1)} %shard_map.154), calls=%async_computation.1 | async-start | bytes 3407872 | tf_op jit(solution)/shard_map/all_to_all | solution.py:252
  58.4 40.6 %copy-start = (bf16[32,14464]{1,0:T(8,128)(2,1)}, bf16[32,14464]{1,0:T(8,128)(2,1)S(1)}, u32[]{:S(2)}) copy-start(bf16[32,14464]{1,0:T(8,128)(2,1)S(1)} %all_gather.9.refs_0_.refs_6_) | copy-start | bytes 2777092
  58.4 14.3 %collective-permute-start.2 = (bf16[32,14464]{1,0:T(8,128)(2,1)S(1)}, bf16[32,14464]{1,0:T(8,128)(2,1)S(1)}, u32[]{:S(2)}, u32[]{:S(2)}) collective-permute-start(bf16[32,14464]{1,0:T(8,128)(2,1)S(1)} %all_gather.9.refs_0_.refs_6_), channel_id=1, source_target_pairs={{0,1},{1,0},{2,3},{3,2},{4,5},{5,4},{6,7},{7,6},{8,9},{9,8},{10,11... | collective-permute-start | bytes 2777096 | tf_op jit(solution)/shard_map/ppermute | solution.py:260
  66.9 24.8 %collective-permute-start.1 = (bf16[32,14464]{1,0:T(8,128)(2,1)S(1)}, bf16[32,14464]{1,0:T(8,128)(2,1)S(1)}, u32[]{:S(2)}, u32[]{:S(2)}) collective-permute-start(bf16[32,14464]{1,0:T(8,128)(2,1)S(1)} %all_gather.9.refs_0_.refs_6_), channel_id=1, source_target_pairs={{0,22},{2,0},{4,2},{6,4},{8,6},{10,8},{12,10},{14,12},{16,14},{18,... | collective-permute-start | bytes 2777096 | tf_op jit(solution)/shard_map/ppermute | solution.py:259
  68.9 25.3 %collective-permute-start = (bf16[32,14464]{1,0:T(8,128)(2,1)S(1)}, bf16[32,14464]{1,0:T(8,128)(2,1)S(1)}, u32[]{:S(2)}, u32[]{:S(2)}) collective-permute-start(bf16[32,14464]{1,0:T(8,128)(2,1)S(1)} %all_gather.9.refs_0_.refs_6_), channel_id=1, source_target_pairs={{0,2},{2,4},{4,6},{6,8},{8,10},{10,12},{12,14},{14,16},{16,18},{18... | collective-permute-start | bytes 2777096 | tf_op jit(solution)/shard_map/ppermute | solution.py:259
  72.7 26.3 %copy-start.1 = (bf16[32,14464]{1,0:T(8,128)(2,1)}, bf16[32,14464]{1,0:T(8,128)(2,1)S(1)}, u32[]{:S(2)}) copy-start(bf16[32,14464]{1,0:T(8,128)(2,1)S(1)} %collective-permute-done.2.refs_3_.refs_9_) | copy-start | bytes 2777092
  91.6 7.4 %copy-start.2 = (bf16[32,14464]{1,0:T(8,128)(2,1)}, bf16[32,14464]{1,0:T(8,128)(2,1)S(1)}, u32[]{:S(2)}) copy-start(bf16[32,14464]{1,0:T(8,128)(2,1)S(1)} %collective-permute-done.1.refs_2_.refs_8_) | copy-start | bytes 2777092
  91.7 5.2 %collective-permute-start.4 = (bf16[32,14464]{1,0:T(8,128)(2,1)S(1)}, bf16[32,14464]{1,0:T(8,128)(2,1)S(1)}, u32[]{:S(2)}, u32[]{:S(2)}) collective-permute-start(bf16[32,14464]{1,0:T(8,128)(2,1)S(1)} %collective-permute-done.1.refs_2_.refs_8_), channel_id=1, source_target_pairs={{0,1},{1,0},{2,3},{3,2},{4,5},{5,4},{6,7},{7,6},{8,9},{9,8},{10,11... | collective-permute-start | bytes 2777096 | tf_op jit(solution)/shard_map/ppermute | solution.py:262
  94.2 2.7 %copy-start.3 = (bf16[32,14464]{1,0:T(8,128)(2,1)}, bf16[32,14464]{1,0:T(8,128)(2,1)S(1)}, u32[]{:S(2)}) copy-start(bf16[32,14464]{1,0:T(8,128)(2,1)S(1)} %collective-permute-done.refs_1_.refs_7_) | copy-start | bytes 2777092
  94.2 4.9 %collective-permute-start.3 = (bf16[32,14464]{1,0:T(8,128)(2,1)S(1)}, bf16[32,14464]{1,0:T(8,128)(2,1)}, u32[]{:S(2)}, u32[]{:S(2)}) collective-permute-start(bf16[32,14464]{1,0:T(8,128)(2,1)S(1)} %collective-permute-done.refs_1_.refs_7_), channel_id=1, source_target_pairs={{0,1},{1,0},{2,3},{3,2},{4,5},{5,4},{6,7},{7,6},{8,9},{9,8},{10,11... | collective-permute-start | bytes 2777096 | tf_op jit(solution)/shard_map/ppermute | solution.py:262
  96.8 1.0 copy-start.4
  105.3 19.0 %all-to-all-start.2 = ((bf16[4,528,256]{2,1,0:T(8,128)(2,1)}), bf16[4,528,256]{2,1,0:T(8,128)(2,1)S(1)}, u32[]{:S(2)}, u32[]{:S(2)}) async-start(bf16[4,528,256]{2,1,0:T(8,128)(2,1)} %shard_map.156), calls=%async_computation.2 | async-start | bytes 2162688 | tf_op jit(solution)/shard_map/all_to_all | solution.py:284
